TPU v7x, 32 devices: a whole 2x2x4 slice. The times are simulated.
32 devices in a mesh: groups: 2 (over x), store: 16 (over z, y, core).
Axes of the slice: x: 2, y: 2, z: 4, core: 2. Of those that a mesh axis runs over, the one named last changes fastest.
Arguments:
- activations: bfloat16 [8192, 4096], P(('groups', 'store')), parts along dimension 0, may hold values from -6 to 6
- out_grads: bfloat16 [8192, 14336], P(('groups', 'store')), parts along dimension 0, may hold values from -6 to 6
- basis_in: bfloat16 [32, 4096], replicated, may hold values from -0.09375 to 0.09375
- basis_out: bfloat16 [32, 14336], replicated, may hold values from -0.046875 to 0.046875
- lengths: int32 [32, 8], P(('groups', 'store')), parts along dimension 0, may hold values from 1 to 64, 256 in all within a row
- codes: int32 [131072, 1024], P(('groups', 'store')), parts along dimension 0, may hold values from -127 to 127
- scale_index: int32 [131072], P(('groups', 'store')), parts along dimension 0, may hold values from 68 to 131
- queries: bfloat16 [128, 1024], P(('groups', 'store')), parts along dimension 0, may hold values from -1.25 to 1.25
Outputs:
- new_rows: float32 [256, 1024], P(('groups', 'store')), parts along dimension 0
- store_scores: float32 [128, 65536], P('groups', 'store'), parts along dimension 0
- new_scores: float32 [128, 128], P('groups', 'store'), parts along dimension 0
There are 2 independent parts, one for each index of `groups`. A program takes and returns all parts, laid end to end along the dimension named above; an argument that names none is the same for every part. Nothing has to cross between parts.
Inputs may be any that keep to these rules, and one draw needn't show every extreme that they name: Each row of lengths sums to 256.
All inputs are finite; a program needn't handle non-finite values.
Results may differ from a plain program's by a relative error of at most 0.0068.
Values may be sent and summed in bfloat16 or wider, within the bound.
No kernel may reach another device: no remote copies, remote signals or barrier semaphores. Data moves between devices by JAX's collectives and lax.ppermute only.
A program may use at most 128 MiB of HBM per device.

v0:
```python
import jax
import jax.numpy as jnp
from jax import lax
from jax.sharding import PartitionSpec as P


def contract_rows(left_side, right_rows):
    return lax.dot_general(
        left_side, right_rows, (((1,), (1,)), ((), ())), preferred_element_type=jnp.float32
    )


def precise_rows(left_side, right_rows):
    return lax.dot_general(
        left_side,
        right_rows,
        (((1,), (1,)), ((), ())),
        precision=lax.Precision.HIGHEST,
        preferred_element_type=jnp.float32,
    )


def contract_cols(left_side, right_side):
    return lax.dot_general(
        left_side, right_side, (((0,), (0,)), ((), ())), preferred_element_type=jnp.float32
    )


def precise_cols(left_side, right_side):
    return lax.dot_general(
        left_side,
        right_side,
        (((0,), (0,)), ((), ())),
        precision=lax.Precision.HIGHEST,
        preferred_element_type=jnp.float32,
    )


def shards(activations, out_grads, basis_in, basis_out, lengths, codes, scale_index, queries):
    store_count = lax.axis_size("store")
    row_count = codes.shape[0]
    example_count = lengths.shape[1]
    token_count = activations.shape[0]
    full_width = codes.shape[1]
    proj_in = contract_rows(activations, basis_in)
    proj_out = contract_rows(out_grads, basis_out)
    finishes = jnp.cumsum(lengths[0])
    starts = finishes - lengths[0]
    position = jnp.arange(token_count, dtype=jnp.int32)[None, :]
    member = ((position >= starts[:, None]) & (position < finishes[:, None])).astype(jnp.float32)
    summed = jnp.einsum("et,ti,tj->eij", member, proj_in, proj_out, precision=lax.Precision.HIGHEST)
    new_rows = summed.reshape(example_count, full_width)
    scales = jnp.exp2(scale_index.astype(jnp.float32) / 16.0) / 128.0
    stored = (codes.astype(jnp.float32) * scales[:, None]).astype(jnp.bfloat16)
    weight_store = 0.75 / (store_count * row_count)
    weight_new = 0.25 / (store_count * example_count)
    partial_value = weight_store * contract_cols(stored, stored) + weight_new * precise_cols(
        new_rows, new_rows
    )
    fisher = lax.psum(partial_value, "store")
    stored_wide = stored.astype(jnp.float32)
    local_trace = weight_store * jnp.sum(stored_wide * stored_wide) + weight_new * jnp.sum(
        new_rows * new_rows
    )
    trace_total = lax.psum(local_trace, "store")
    damping = 0.1 * trace_total / full_width
    system = fisher + damping * jnp.eye(full_width, dtype=jnp.float32)
    factor = jnp.linalg.cholesky(system)
    right_side = queries.astype(jnp.float32).T
    middle = lax.linalg.triangular_solve(factor, right_side, left_side=True, lower=True)
    solved = lax.linalg.triangular_solve(
        factor, middle, left_side=True, lower=True, transpose_a=True
    )
    shard_rows = lax.all_gather(solved.T, "store", axis=0, tiled=True)
    combined = jnp.concatenate(
        [precise_rows(shard_rows, stored.astype(jnp.float32)), precise_rows(shard_rows, new_rows)],
        axis=1,
    )
    return (new_rows, combined[:, :row_count], combined[:, row_count:])


def solution(mesh):
    return jax.shard_map(
        shards,
        mesh=mesh,
        in_specs=(
            P(("groups", "store"), None),
            P(("groups", "store"), None),
            P(),
            P(),
            P(("groups", "store"), None),
            P(("groups", "store"), None),
            P(("groups", "store")),
            P(("groups", "store"), None),
        ),
        out_specs=(P(("groups", "store"), None), P("groups", "store"), P("groups", "store")),
        check_vma=False,
    )
```

profile of v0, /device:TPU:0, one launch (start us, length us, event | category | flops | bytes accessed | tf_op | source)
XLA Modules:
  0.0 548.5 jit_solution(3343833848088271733)
XLA Ops:
  8.9 5.6 %convolution_bitcast_fusion.1 = f32[256,32,1]{0,1,2:T(8,128)S(1)} fusion(bf16[256,14336]{1,0:T(8,128)(2,1)} %param.9, bf16[32,14336]{1,0:T(8,128)(2,1)} %param.11), kind=kOutput, calls=%fused_computation.25 | convolution fusion | flops 234881024 | bytes 8290304 | tf_op jit(solution)/shard_map/dot_general | solution.py:8
  16.4 3.5 fusion.100
  19.9 9.5 %multiply_reduce_fusion = (f32[]{:T(128)}, bf16[4096,1024]{1,0:T(8,128)(2,1)S(1)}) fusion(f32[4096]{0:T(1024)S(1)} %exponential_multiply_fusion, s32[4096,1024]{1,0:T(8,128)} %param.13), kind=kLoop, calls=%fused_computation.2 | loop fusion | flops 25165824 | bytes 25182212 | tf_op jit(solution)/shard_map/reduce_sum | solution.py:62
  29.4 3.2 copy-done.3
  32.7 10.5 %multiply_add_fusion = f32[1024,1024]{0,1:T(8,128)} fusion(f32[1024,1024]{0,1:T(8,128)S(1)} %fusion.100, bf16[4096,1024]{1,0:T(8,128)(2,1)S(1)} %get-tuple-element.32), kind=kOutput, calls=%fused_computation.9 | convolution fusion | flops 8593080320 | bytes 16777216 | tf_op jit(solution)/shard_map/dot_general | solution.py:24
  44.4 36.3 %psum.15 = f32[]{:T(128)} all-reduce(f32[]{:T(128)S(6)} %add.92), channel_id=1, replica_groups=mesh['groups'=2,'store'=16] {'store'}, use_global_device_ids=true, to_apply=%region_4.5 | all-reduce | flops 1 | bytes 8 | tf_op jit(solution)/shard_map/psum | solution.py:65
  81.5 76.2 %all-reduce.3.cloned.1.call-done = f32[1024,1024]{0,1:T(8,128)} async-done(((f32[1024,1024]{0,1:T(8,128)}), f32[1024,1024]{0,1:T(8,128)}) %all-reduce.3.cloned.1.call-update) | async-done | bytes 4194320 | tf_op jit(solution)/shard_map/psum | solution.py:60
  157.6 4.8 select_add_fusion
  162.4 5.7 %copy.53 = f32[1024,1024]{1,0:T(8,128)} copy(f32[1024,1024]{0,1:T(8,128)} %select_add_fusion) | data formatting | bytes 8388608 | tf_op jit(solution)/shard_map/add | solution.py:67
  168.1 4.5 fusion
  172.6 2.0 copy-done.4
  174.6 11.7 %cholesky.222 = f32[128,128]{1,0:T(8,128)S(1)} custom-call(f32[128,128]{1,0:T(8,128)S(1)} %cholesky.577), custom_call_target="Cholesky" | custom-call | tf_op jit(solution)/shard_map/jit(cholesky)/cholesky | solution.py:68
  186.4 9.8 %custom-call.64 = f32[1,128,128]{1,2,0:T(8,128)S(1)} custom-call(f32[1,128,128]{2,1,0:T(8,128)S(1)} %get-tuple-element.48), custom_call_target="InvertDiagBlocksLowerTriangular" | custom-call | tf_op jit(solution)/shard_map/jit(cholesky)/cholesky | solution.py:68
  196.2 1.5 fusion.9
  198.0 1.6 convolution_subtract_fusion
  199.6 11.7 %cholesky.243 = f32[128,128]{1,0:T(8,128)S(1)} custom-call(f32[128,128]{1,0:T(8,128)S(1)} %cholesky.581), custom_call_target="Cholesky" | custom-call | tf_op jit(solution)/shard_map/jit(cholesky)/cholesky | solution.py:68
  211.6 9.8 %custom-call.65 = f32[1,128,128]{1,2,0:T(8,128)S(1)} custom-call(f32[1,128,128]{2,1,0:T(8,128)S(1)} %get-tuple-element.46), custom_call_target="InvertDiagBlocksLowerTriangular" | custom-call | tf_op jit(solution)/shard_map/jit(cholesky)/cholesky | solution.py:68
  222.5 1.9 copy-done.2
  224.5 2.4 convolution_subtract_fusion.1
  226.9 11.7 %cholesky.466 = f32[128,128]{1,0:T(8,128)S(1)} custom-call(f32[128,128]{1,0:T(8,128)S(1)} %cholesky.586), custom_call_target="Cholesky" | custom-call | tf_op jit(solution)/shard_map/jit(cholesky)/cholesky | solution.py:68
  239.4 9.8 %custom-call.66 = f32[1,128,128]{1,2,0:T(8,128)S(1)} custom-call(f32[1,128,128]{2,1,0:T(8,128)S(1)} %get-tuple-element.44), custom_call_target="InvertDiagBlocksLowerTriangular" | custom-call | tf_op jit(solution)/shard_map/jit(cholesky)/cholesky | solution.py:68
  249.2 1.2 convolution_dynamic-update-slice_fusion.1
  250.4 3.3 convolution_subtract_fusion.2
  253.8 11.7 %cholesky.485 = f32[128,128]{1,0:T(8,128)S(1)} custom-call(f32[128,128]{1,0:T(8,128)S(1)} %cholesky.591), custom_call_target="Cholesky" | custom-call | tf_op jit(solution)/shard_map/jit(cholesky)/cholesky | solution.py:68
  266.3 9.8 %custom-call.67 = f32[1,128,128]{1,2,0:T(8,128)S(1)} custom-call(f32[1,128,128]{2,1,0:T(8,128)S(1)} %get-tuple-element.42), custom_call_target="InvertDiagBlocksLowerTriangular" | custom-call | tf_op jit(solution)/shard_map/jit(cholesky)/cholesky | solution.py:68
  276.1 1.1 convolution_dynamic-update-slice_fusion.2
  277.2 3.2 convolution_subtract_fusion.3
  280.4 12.1 %cholesky.504 = f32[128,128]{1,0:T(8,128)S(1)} custom-call(f32[128,128]{1,0:T(8,128)S(1)} %cholesky.596), custom_call_target="Cholesky" | custom-call | tf_op jit(solution)/shard_map/jit(cholesky)/cholesky | solution.py:68
  293.3 9.8 %custom-call.68 = f32[1,128,128]{1,2,0:T(8,128)S(1)} custom-call(f32[1,128,128]{2,1,0:T(8,128)S(1)} %get-tuple-element.40), custom_call_target="InvertDiagBlocksLowerTriangular" | custom-call | tf_op jit(solution)/shard_map/jit(cholesky)/cholesky | solution.py:68
  303.1 1.1 convolution_dynamic-update-slice_fusion.3
  304.2 3.1 convolution_subtract_fusion.4
  307.3 11.7 %cholesky.524 = f32[128,128]{1,0:T(8,128)S(1)} custom-call(f32[128,128]{1,0:T(8,128)S(1)} %cholesky.601), custom_call_target="Cholesky" | custom-call | tf_op jit(solution)/shard_map/jit(cholesky)/cholesky | solution.py:68
  319.8 9.8 %custom-call.69 = f32[1,128,128]{1,2,0:T(8,128)S(1)} custom-call(f32[1,128,128]{2,1,0:T(8,128)S(1)} %get-tuple-element.38), custom_call_target="InvertDiagBlocksLowerTriangular" | custom-call | tf_op jit(solution)/shard_map/jit(cholesky)/cholesky | solution.py:68
  330.6 2.8 convolution_subtract_fusion.5
  333.4 11.7 %cholesky.544 = f32[128,128]{1,0:T(8,128)S(1)} custom-call(f32[128,128]{1,0:T(8,128)S(1)} %cholesky.606), custom_call_target="Cholesky" | custom-call | tf_op jit(solution)/shard_map/jit(cholesky)/cholesky | solution.py:68
  345.9 9.8 %custom-call.70 = f32[1,128,128]{1,2,0:T(8,128)S(1)} custom-call(f32[1,128,128]{2,1,0:T(8,128)S(1)} %get-tuple-element.36), custom_call_target="InvertDiagBlocksLowerTriangular" | custom-call | tf_op jit(solution)/shard_map/jit(cholesky)/cholesky | solution.py:68
  356.7 2.1 convolution_subtract_fusion.6
  358.8 11.7 %cholesky.562 = f32[128,128]{1,0:T(8,128)S(1)} custom-call(f32[128,128]{1,0:T(8,128)S(1)} %convolution_subtract_fusion.6), custom_call_target="Cholesky" | custom-call | tf_op jit(solution)/shard_map/jit(cholesky)/cholesky | solution.py:68
  380.7 4.9 select_select_fusion
  385.5 24.0 %while.1 = (s32[]{:T(128)}, f32[1024,1024]{0,1:T(8,128)}, s32[8,2]{0,1:T(2,128)S(1)}, f32[8,128,128]{2,1,0:T(8,128)S(1)}, s32[]{:T(128)}) while((s32[]{:T(128)}, f32[1024,1024]{0,1:T(8,128)}, s32[8,2]{0,1:T(2,128)S(1)}, f32[8,128,128]{2,1,0:T(8,128)S(1)}, s32[]{:T(128)}) %tuple.57), condition=%wide.while_cond, body=%wide.while_body.sunk | while | flops 2 | bytes 393329 | solution.py:71
  386.2 2.3 dynamic-slice.7
  389.2 2.3 dynamic-slice.7
  392.2 2.3 dynamic-slice.7
  395.2 2.3 dynamic-slice.7
  398.2 2.3 dynamic-slice.7
  401.2 2.3 dynamic-slice.7
  404.2 2.3 dynamic-slice.7
  407.2 2.2 dynamic-slice.7
  409.5 78.8 %custom-call.71 = f32[8,128,128]{1,2,0:T(8,128)S(1)} custom-call(f32[8,128,128]{2,1,0:T(8,128)S(1)} %get-tuple-element.10), custom_call_target="InvertDiagBlocksLowerTriangular" | custom-call | tf_op jit(solution)/shard_map/triangular_solve | solution.py:71
  489.7 1.1 convolution_subtract_fusion.17
  490.9 1.2 convolution_subtract_fusion.16
  492.3 1.2 convolution_subtract_fusion.15
  493.7 1.3 convolution_subtract_fusion.14
  495.1 1.3 convolution_subtract_fusion.20
  496.6 1.4 convolution_subtract_fusion.8
  498.4 1.1 convolution_subtract_fusion.13
  499.7 1.1 convolution_subtract_fusion.12
  501.0 1.2 convolution_subtract_fusion.11
  502.5 1.3 convolution_subtract_fusion.10
  504.1 1.4 convolution_subtract_fusion.9
  505.7 1.4 convolution_subtract_fusion.19
  507.4 1.5 convolution_subtract_fusion.7
  509.3 20.1 %all-gather = f32[16,4,1024]{2,1,0:T(4,128)S(1)} all-gather(f32[1,4,1024]{2,1,0:T(4,128)S(1)} %bitcast.154), channel_id=1, replica_groups=mesh['groups'=2,'store'=16] {'store'}, dimensions={0}, use_global_device_ids=true | all-gather | bytes 278528 | tf_op jit(solution)/shard_map/all_gather | solution.py:74
  529.4 11.1 %fusion.101 = f32[64,4096]{1,0:T(8,128)} fusion(f32[64,1024]{1,0:T(8,128)S(1)} %reshape.148, bf16[4096,1024]{1,0:T(8,128)(2,1)} %copy-done.3), kind=kOutput, calls=%fused_computation.233 | convolution fusion | flops 3221225472 | bytes 9699328 | tf_op jit(solution)/shard_map/dot_general | solution.py:14
  (145 shorter events, 27.6 us)
Async XLA Ops:
  7.2 7.4 %copy-start = (bf16[256,4096]{1,0:T(8,128)(2,1)S(1)}, bf16[256,4096]{1,0:T(8,128)(2,1)}, u32[]{:S(2)}) copy-start(bf16[256,4096]{1,0:T(8,128)(2,1)} %param.8) | copy-start | bytes 6291460
  7.2 7.4 %copy-start.6 = (bf16[32,4096]{1,0:T(8,128)(2,1)S(1)}, bf16[32,4096]{1,0:T(8,128)(2,1)}, u32[]{:S(2)}) copy-start(bf16[32,4096]{1,0:T(8,128)(2,1)} %param.10) | copy-start | bytes 786436
  7.2 150.5 %all-reduce.3.cloned.1.call-start = ((), (), s32[]{:S(2)}) async-start(), calls=%async_computation | async-start | bytes 8388608 | tf_op jit(solution)/shard_map/psum | solution.py:60
  14.4 5.4 copy-start.7
  16.4 524.1 %copy-start.5 = (f32[8,1024]{1,0:T(8,128)}, f32[8,1024]{1,0:T(8,128)S(1)}, u32[]{:S(2)}) copy-start(f32[8,1024]{1,0:T(8,128)S(1)} %reshape.123) | copy-start | bytes 98308
  29.4 3.2 copy-start.3
  43.2 38.2 %copy-start.8 = (bf16[4,1024]{1,0:T(4,128)(2,1)S(1)}, bf16[4,1024]{1,0:T(4,128)(2,1)}, u32[]{:S(2)}) copy-start(bf16[4,1024]{1,0:T(4,128)(2,1)} %param.15) | copy-start | bytes 24580
  172.6 2.0 copy-start.4
  222.5 2.0 copy-start.2
  529.3 12.1 %copy-start.1 = (bf16[256,4096]{1,0:T(8,128)(2,1)S(1)}, bf16[256,4096]{1,0:T(8,128)(2,1)}, u32[]{:S(2)}) copy-start(bf16[256,4096]{1,0:T(8,128)(2,1)} %param.8) | copy-start | bytes 6291460
Sparse Core Ops, SparseCore 0:
  43.3 114.2 all-reduce.2
where the time goes:
time: 559 us; the launch traced here: 548 us
  other arithmetic  272 us (49%)
  matrix products  79.7 us (14%)
  waiting for transfers between devices  76.2 us (14%)
  blocking collectives  56.4 us (10%)
  local copies, waits for them, and re-layouts  42.7 us (8%)
  between operations  21.5 us (4%)
    another operation x30, other arithmetic, shards(): factor = jnp.linalg.cholesky(system)  168 us
    another operation x3, other arithmetic, shards(): lax.linalg.triangular_solve(factor, middle, left_side=True, lower=True, t...  83.7 us
    psum x1, waiting for transfers between devices, shards(): fisher = lax.psum(partial_value, 'store')  76.2 us
    psum x1, blocking collectives, shards(): trace_total = lax.psum(local_trace, 'store')  36.3 us
    another operation x14, matrix products, shards(): factor = jnp.linalg.cholesky(system)  25.9 us
    another operation x40, local copies, waits for them, and re-layouts  23.7 us
    all_gather x1, blocking collectives, shards(): shard_rows = lax.all_gather(solved.T, 'store', axis=0, tiled=True)  20.1 us
    dot_general x2, matrix products, precise_rows(): lax.dot_general(left_side, right_rows, (((1,), (1,)), ((), ())), precisio...  12 us
  transfers between devices with their start and end apart: 1, of which 1 were waited for; matrix products, arithmetic and copies ran while one was open for 0% of the time, Pallas kernels for 0%

commit v1 on v0

v1 whole, which is shorter than its diff:
```python
import functools

import jax
import jax.numpy as jnp
import numpy as np
from jax import lax
from jax.experimental import pallas as pl
from jax.experimental.pallas import tpu as pltpu
from jax.sharding import PartitionSpec as P

LANES = 128
PACK = 16
CODE_MAX = 32767.0
F32 = jnp.float32
BF16 = jnp.bfloat16
VMEM = pl.BlockSpec(memory_space=pltpu.VMEM)
SMEM = pl.BlockSpec(memory_space=pltpu.SMEM)
ANY = pl.BlockSpec(memory_space=pl.ANY)
NN = (((1,), (0,)), ((), ()))
NT = (((1,), (1,)), ((), ()))
TN = (((0,), (0,)), ((), ()))


def mm(left, right, dims=NN):
    return lax.dot_general(left, right, dims, preferred_element_type=F32)


def split2(value):
    high = value.astype(BF16)
    return high, (value - high.astype(F32)).astype(BF16)


def split3(value):
    high, _ = split2(value)
    rest = value - high.astype(F32)
    mid, low = split2(rest)
    return high, mid, low


def mm3(left, right, dims=NN):
    left_high, left_low = left
    right_high, right_low = right
    return mm(left_high, right_high, dims) + (
        mm(left_high, right_low, dims) + mm(left_low, right_high, dims)
    )


def triangle(width):
    tiles = width // LANES
    return [(i, j) for i in range(tiles) for j in range(i + 1)]


def column_of(row):
    return jnp.broadcast_to(row, (LANES, LANES)).T


def eye(size):
    return lax.broadcasted_iota(jnp.int32, (size, size), 0) == lax.broadcasted_iota(
        jnp.int32, (size, size), 1
    )


def gram_kernel(
    steps,
    weight_store,
    weight_new,
    me_ref,
    lengths_ref,
    codes_ref,
    scale_ref,
    act_ref,
    grad_ref,
    basis_in_ref,
    basis_out_ref,
    stored_ref,
    new_rows_ref,
    keep_ref,
    send_ref,
    diag_ref,
    total,
    proj_in,
    proj_out,
):
    step = pl.program_id(0)
    chunk, width = codes_ref.shape
    rank = basis_in_ref.shape[0]
    tokens = act_ref.shape[0]
    examples = new_rows_ref.shape[0]

    @pl.when(step == 0)
    def _():
        total[...] = jnp.zeros_like(total)
        proj_in[...] = jnp.zeros_like(proj_in)
        proj_out[...] = jnp.zeros_like(proj_out)

    groups = chunk // LANES
    for g in range(groups):
        index = scale_ref[pl.ds(step * groups + g, 1), :]
        scale = column_of(jnp.exp2(index.astype(F32) / 16.0) / 128.0)
        rows = slice(g * LANES, (g + 1) * LANES)
        for c in range(width // LANES):
            cols = slice(c * LANES, (c + 1) * LANES)
            stored_ref[rows, cols] = (codes_ref[rows, cols].astype(F32) * scale).astype(BF16)
    stored = stored_ref[...]
    side = 256
    for i in range(width // side):
        rows = slice(i * side, (i + 1) * side)
        total[rows, : (i + 1) * side] += mm(stored[:, rows], stored[:, : (i + 1) * side], TN)
    proj_in[...] += mm(act_ref[...], basis_in_ref[...], NT)
    proj_out[...] += mm(grad_ref[...], basis_out_ref[...], NT)

    @pl.when(step == steps - 1)
    def _():
        wide = (3 * rank, width)
        k = lax.broadcasted_iota(jnp.int32, wide, 0) % rank
        c = lax.broadcasted_iota(jnp.int32, wide, 1)
        pick_in = (k == c // rank).astype(F32).astype(BF16)
        pick_out = (k == c % rank).astype(F32).astype(BF16)
        left = mm(jnp.concatenate(split3(proj_in[...]), axis=1), pick_in)
        right = mm(jnp.concatenate(split3(proj_out[...]), axis=1), pick_out)
        products = split3(left * right)
        place = lax.broadcasted_iota(jnp.int32, (examples, tokens), 1)
        owner = lax.broadcasted_iota(jnp.int32, (examples, tokens), 0)
        member = jnp.zeros((examples, tokens), F32)
        start = jnp.int32(0)
        for e in range(examples):
            finish = start + lengths_ref[0, e]
            inside = (owner == e) & (place >= start) & (place < finish)
            member = jnp.where(inside, 1.0, member)
            start = finish
        member = member.astype(BF16)
        new_rows = mm(member, products[0]) + (mm(member, products[1]) + mm(member, products[2]))
        new_rows_ref[...] = new_rows
        high, mid, low = [part.astype(F32) for part in split3(new_rows)]
        first = jnp.concatenate([high, high, mid, high, low, mid], axis=0).astype(BF16)
        second = jnp.concatenate([high, mid, high, low, high, mid], axis=0).astype(BF16)
        for i in range(width // side):
            rows = slice(i * side, (i + 1) * side)
            total[rows, : (i + 1) * side] = weight_store * total[
                rows, : (i + 1) * side
            ] + weight_new * mm(first[:, rows], second[:, : (i + 1) * side], TN)
        tiles = triangle(width)
        half = len(tiles) // 2
        diagonal = eye(LANES)
        for i in range(width // LANES):
            at = slice(i * LANES, (i + 1) * LANES)
            diag_ref[i : i + 1, :] = jnp.sum(
                jnp.where(diagonal, total[at, at], 0.0), axis=0, keepdims=True
            )
        send_ref[half * LANES :, :] = diag_ref[...]
        for b, (i, j) in enumerate(tiles):
            rows = slice(b % half * LANES, (b % half + 1) * LANES)
            tile = total[i * LANES : (i + 1) * LANES, j * LANES : (j + 1) * LANES]

            @pl.when(me_ref[0] == b // half)
            def _():
                keep_ref[rows, :] = tile

            @pl.when(me_ref[0] != b // half)
            def _():
                send_ref[rows, :] = tile


def gram(me, lengths, codes, scale_index, activations, out_grads, basis_in, basis_out, count):
    rows, width = codes.shape
    tokens, inputs = activations.shape
    outputs = out_grads.shape[1]
    rank = basis_in.shape[0]
    examples = lengths.shape[1]
    steps = 8
    half = len(triangle(width)) // 2 * LANES
    chunk = rows // steps
    whole = lambda *shape: pl.BlockSpec(shape, lambda s: (0,) * len(shape))
    return pl.pallas_call(
        functools.partial(
            gram_kernel, steps, 0.75 / (count * rows), 0.25 / (count * examples)
        ),
        grid=(steps,),
        in_specs=[
            SMEM,
            SMEM,
            pl.BlockSpec((chunk, width), lambda s: (s, 0)),
            whole(rows // LANES, LANES),
            pl.BlockSpec((tokens, inputs // steps), lambda s: (0, s)),
            pl.BlockSpec((tokens, outputs // steps), lambda s: (0, s)),
            pl.BlockSpec((rank, inputs // steps), lambda s: (0, s)),
            pl.BlockSpec((rank, outputs // steps), lambda s: (0, s)),
        ],
        out_specs=[
            pl.BlockSpec((chunk, width), lambda s: (s, 0)),
            whole(examples, width),
            whole(half, LANES),
            whole(half + width // LANES, LANES),
            whole(width // LANES, LANES),
        ],
        out_shape=[
            jax.ShapeDtypeStruct((rows, width), BF16),
            jax.ShapeDtypeStruct((examples, width), F32),
            jax.ShapeDtypeStruct((half, LANES), F32),
            jax.ShapeDtypeStruct((half + width // LANES, LANES), F32),
            jax.ShapeDtypeStruct((width // LANES, LANES), F32),
        ],
        scratch_shapes=[
            pltpu.VMEM((width, width), F32),
            pltpu.VMEM((tokens, rank), F32),
            pltpu.VMEM((tokens, rank), F32),
        ],
        compiler_params=pltpu.CompilerParams(vmem_limit_bytes=48 << 20),
        cost_estimate=pl.CostEstimate(
            flops=6 * 10**9, bytes_accessed=40 * 10**6, transcendentals=0
        ),
        name="fisher_share",
    )(me, lengths, codes, scale_index, activations, out_grads, basis_in, basis_out)


def exponents(diag):
    return jnp.clip(jnp.ceil(32.0 * jnp.log2(jnp.maximum(diag, 1e-30))), -4000.0, 4000.0)


def fill_scales(exps, factor, columns, rows_ref):
    scale = jnp.exp2(exps / 64.0)
    rows_ref[...] = scale * factor
    for t in range(exps.shape[0]):
        columns[t * LANES : (t + 1) * LANES, :] = column_of(scale[t : t + 1, :])


def read_exps(ref, start, tiles):
    return ref[start : start + PACK, :].astype(jnp.int32).astype(F32)[:tiles, :]


def write_exps(ref, start, exps):
    tiles = exps.shape[0]
    padded = jnp.concatenate([exps, jnp.zeros((PACK - tiles, LANES), F32)], axis=0)
    ref[start : start + PACK, :] = padded.astype(jnp.int32).astype(jnp.int16)


def encode(value, inverse):
    scaled = jnp.clip(jnp.round(value * inverse), -CODE_MAX, CODE_MAX)
    return scaled.astype(jnp.int32).astype(jnp.int16)


def strip_scale(table_ref, columns, rows_ref, flat, strip):
    tile = flat // LANES
    i = table_ref[0, tile]
    j = table_ref[1, tile]
    at = pl.multiple_of(i * LANES + flat % LANES, strip)
    return columns[pl.ds(at, strip), :] * rows_ref[pl.ds(j, 1), :]


def combine_kernel(members, coded, tiles, strip, *refs):
    where_ref, table_ref, own_ref, state_ref = refs[:4]
    arrived = refs[4 : 4 + coded]
    refs = refs[4 + coded :]
    out_own, out_state = refs[:2]
    out_messages = refs[2 : 1 + members] if members > 1 else ()
    refs = refs[max(1, members) + 1 :]
    columns, rows_ref, inverse_columns, inverse_rows = refs
    rows = own_ref.shape[0]
    if coded == 1 and arrived[0].dtype == F32:
        exps = exponents(state_ref[...] + arrived[0][rows:, :])
    else:
        mine = read_exps(state_ref, 0, tiles)
        theirs = [read_exps(ref, rows, tiles) for ref in arrived]
        level = [jnp.exp2(e / 32.0) for e in [mine] + theirs]
        while len(level) > 1:
            level = [a + b for a, b in zip(level[::2], level[1::2])]
        exps = exponents(level[0])
        for m, e in enumerate(theirs):
            fill_scales(e, 1.0 / CODE_MAX, columns.at[m], rows_ref.at[m])
    fill_scales(-exps, CODE_MAX, inverse_columns, inverse_rows)
    base = where_ref[0]
    mine_at = where_ref[1]
    part = rows // max(members, 1)
    for m in range(max(members, 1)):
        first = jnp.bitwise_xor(mine_at, m) * part

        def body(s, _):
            inside = pl.multiple_of(s * strip, strip)
            at = pl.multiple_of(first + inside, strip)
            flat = base + at
            value = own_ref[pl.ds(at, strip), :]
            for a, ref in enumerate(arrived):
                got = ref[pl.ds(at, strip), :]
                if got.dtype == F32:
                    value = value + got
                else:
                    got = got.astype(jnp.int32).astype(F32)
                    value = value + got * strip_scale(
                        table_ref, columns.at[a], rows_ref.at[a], flat, strip
                    )
            if members > 1 and m == 0:
                out_own[pl.ds(inside, strip), :] = value
            else:
                inverse = strip_scale(table_ref, inverse_columns, inverse_rows, flat, strip)
                target = out_messages[m - 1] if members > 1 else out_own
                target[pl.ds(inside, strip), :] = encode(value, inverse)
            return 0

        lax.fori_loop(0, part // strip, body, 0, unroll=2)
    write_exps(out_state, 0, exps)
    for ref in out_messages:
        write_exps(ref, part, exps)


def combine(where, table, own, state, arrived, members, strip):
    rows = own.shape[0]
    tiles = table.shape[1]
    width_tiles = int(round(((8 * tiles + 1) ** 0.5 - 1) / 2))
    width = width_tiles * LANES
    part = rows // max(members, 1)
    outs = [
        jax.ShapeDtypeStruct((part, LANES), F32 if members > 1 else jnp.int16),
        jax.ShapeDtypeStruct((PACK, LANES), jnp.int16),
    ]
    outs += [jax.ShapeDtypeStruct((part + PACK, LANES), jnp.int16)] * max(members - 1, 0)
    return pl.pallas_call(
        functools.partial(combine_kernel, members, len(arrived), width_tiles, strip),
        in_specs=[SMEM, SMEM] + [VMEM] * (2 + len(arrived)),
        out_specs=[VMEM] * len(outs),
        out_shape=outs,
        scratch_shapes=[
            pltpu.VMEM((len(arrived), width, LANES), F32),
            pltpu.VMEM((len(arrived), width_tiles, LANES), F32),
            pltpu.VMEM((width, LANES), F32),
            pltpu.VMEM((width_tiles, LANES), F32),
        ],
        compiler_params=pltpu.CompilerParams(vmem_limit_bytes=32 << 20),
        cost_estimate=pl.CostEstimate(
            flops=10 * rows * LANES, bytes_accessed=8 * rows * LANES, transcendentals=0
        ),
        name="sum_shares",
    )(where, table, own, state, *arrived)


def solve_kernel(
    side,
    places_ref,
    first_ref,
    second_ref,
    state_ref,
    queries_ref,
    new_rows_ref,
    stored_hbm,
    scores_ref,
    new_scores_ref,
    flat,
    system,
    pair,
    stored,
    solved,
    columns,
    rows_ref,
    sem,
):
    copy = pltpu.make_async_copy(stored_hbm, stored, sem)
    copy.start()
    queries, width = queries_ref.shape
    tiles = width // LANES
    pieces = places_ref.shape[0]
    piece = flat.shape[0] // pieces
    for p in range(pieces):
        source = first_ref if p < pieces // 2 else second_ref
        at = p % (pieces // 2) * piece
        flat[pl.ds(pl.multiple_of(places_ref[p], PACK), piece), :] = source[at : at + piece, :]
    fill_scales(read_exps(state_ref, 0, tiles), 1.0 / CODE_MAX, columns, rows_ref)
    diagonal = eye(LANES)
    trace = jnp.zeros((1, LANES), F32)
    for b, (i, j) in enumerate(triangle(width)):
        value = flat[b * LANES : (b + 1) * LANES, :].astype(jnp.int32).astype(F32)
        value = value * columns[i * LANES : (i + 1) * LANES, :] * rows_ref[j : j + 1, :]
        system[i * LANES : (i + 1) * LANES, j * LANES : (j + 1) * LANES] = value
        if i == j:
            trace = trace + jnp.sum(jnp.where(diagonal, value, 0.0), axis=0, keepdims=True)
        elif i * LANES // side == j * LANES // side:
            system[j * LANES : (j + 1) * LANES, i * LANES : (i + 1) * LANES] = value.T
    damp = (0.1 / width) * jnp.sum(trace)
    for i in range(tiles):
        at = slice(i * LANES, (i + 1) * LANES)
        system[at, at] += jnp.where(diagonal, damp, 0.0)
    system[width:, :] = queries_ref[...].astype(F32)
    blocks = width // side
    spans = [slice(b * side, (b + 1) * side) for b in range(blocks)]
    bounds = [
        jnp.max(jnp.sum(jnp.abs(system[span, span]), axis=0, keepdims=True)) for span in spans
    ]
    unit = eye(side)
    for b, span in enumerate(spans):
        below = (b + 1) * side
        bound = bounds[b]
        low = damp / bound
        pair[:side, :] = jnp.where(unit, 1.0 / bound, 0.0)
        pair[side:, :] = system[span, span] * (1.0 / bound)

        def more(low):
            return low < 0.9995

        def newton(low):
            gain = 4.0 / ((1.0 + low) * (1.0 + low))
            both = pair[...]
            step = jnp.where(unit, gain * (1.0 + low), 0.0) - gain * both[side:, :]
            pair[...] = mm3(split2(both), split2(step))
            return gain * low

        lax.while_loop(more, newton, low)
        inverse = split2(pair[:side, :])
        panel = system[below:, span]
        weights = split2(mm3(split2(panel), inverse))
        later = split2(panel[: width - below, :])
        system[below:, span] = weights[0].astype(F32) + weights[1].astype(F32)
        for c in range(b + 1, blocks):
            from_row = c * side - below
            update = mm3(
                (weights[0][from_row:, :], weights[1][from_row:, :]),
                (
                    later[0][from_row : from_row + side, :],
                    later[1][from_row : from_row + side, :],
                ),
                NT,
            )
            system[c * side :, spans[c]] -= update
    for b in reversed(range(blocks)):
        below = (b + 1) * side
        value = system[width:, spans[b]]
        if below < width:
            value = value - mm3(
                split2(solved[:, below:]), split2(system[below:width, spans[b]])
            )
        solved[:, spans[b]] = value
    high, low = split2(solved[...])
    new_scores_ref[...] = mm3((high, low), split2(new_rows_ref[...]), NT)
    both = jnp.concatenate([high, low], axis=0)
    copy.wait()
    span = 512
    for r in range(0, stored.shape[0], span):
        value = mm(both, stored[r : r + span, :], NT)
        scores_ref[:, r : r + span] = value[:queries, :] + value[queries:, :]


def solve(places, first, second, state, queries, new_rows, stored):
    count, width = queries.shape
    rows = stored.shape[0]
    examples = new_rows.shape[0]
    side = 256
    flat_rows = len(triangle(width)) * LANES
    return pl.pallas_call(
        functools.partial(solve_kernel, side),
        in_specs=[SMEM] + [VMEM] * 5 + [ANY],
        out_specs=[VMEM, VMEM],
        out_shape=[
            jax.ShapeDtypeStruct((count, rows), F32),
            jax.ShapeDtypeStruct((count, examples), F32),
        ],
        scratch_shapes=[
            pltpu.VMEM((flat_rows, LANES), jnp.int16),
            pltpu.VMEM((width + count, width), F32),
            pltpu.VMEM((2 * side, side), F32),
            pltpu.VMEM((rows, width), BF16),
            pltpu.VMEM((count, width), F32),
            pltpu.VMEM((width, LANES), F32),
            pltpu.VMEM((width // LANES, LANES), F32),
            pltpu.SemaphoreType.DMA,
        ],
        compiler_params=pltpu.CompilerParams(vmem_limit_bytes=48 << 20),
        cost_estimate=pl.CostEstimate(
            flops=10 * 10**9, bytes_accessed=20 * 10**6, transcendentals=0
        ),
        name="solve_and_score",
    )(places, first, second, state, queries, new_rows, stored)


def swap(value, mask, count):
    return lax.ppermute(value, "store", [(i, i ^ mask) for i in range(count)])


def shards(activations, out_grads, basis_in, basis_out, lengths, codes, scale_index, queries):
    count = lax.axis_size("store")
    me = lax.axis_index("store")
    width = codes.shape[1]
    tiles = triangle(width)
    table = np.array(tiles, np.int32).T
    all_queries = lax.all_gather(queries, "store", axis=0, tiled=True)
    core = me & 1
    stored, new_rows, own, send, state = gram(
        core.astype(jnp.int32)[None],
        lengths,
        codes,
        scale_index.reshape(-1, LANES),
        activations,
        out_grads,
        basis_in,
        basis_out,
        count,
    )
    groups = []
    bit = 1
    while 1 << bit < count:
        members = 4 if 1 << (bit + 1) < count else 2
        groups.append((bit, members))
        bit += 2
    piece = len(tiles) * LANES // count
    strip = int(np.gcd(np.gcd(piece, LANES), 64))
    arrived = [swap(send, 1, count)]
    base = core * own.shape[0]
    for bit, members in groups:
        at = (me >> bit) & (members - 1)
        where = jnp.stack([base, at]).astype(jnp.int32)
        own, state, *messages = combine(where, table, own, state, arrived, members, strip)
        arrived = [swap(message, (m + 1) << bit, count) for m, message in enumerate(messages)]
        base = base + at * own.shape[0]
    where = jnp.stack([base, jnp.zeros_like(base)]).astype(jnp.int32)
    final, state = combine(where, table, own, state, arrived, 0, strip)
    for bit, members in reversed(groups):
        final = jnp.concatenate(
            [final] + [swap(final, m << bit, count) for m in range(1, members)], axis=0
        )
    other = swap(final, 1, count)
    places = []
    for slot in range(count):
        size = len(tiles) * LANES // 2
        place = (core ^ (slot // (count // 2))) * size
        left = slot % (count // 2)
        weight = count // 2
        for bit, members in groups:
            weight //= members
            size //= members
            place = place + (((me >> bit) & (members - 1)) ^ (left // weight)) * size
            left %= weight
        places.append(place)
    scores, new_scores = solve(
        jnp.stack(places).astype(jnp.int32), final, other, state, all_queries, new_rows, stored
    )
    return new_rows, scores, new_scores


def solution(mesh):
    return jax.shard_map(
        shards,
        mesh=mesh,
        in_specs=(
            P(("groups", "store"), None),
            P(("groups", "store"), None),
            P(),
            P(),
            P(("groups", "store"), None),
            P(("groups", "store"), None),
            P(("groups", "store")),
            P(("groups", "store"), None),
        ),
        out_specs=(P(("groups", "store"), None), P("groups", "store"), P("groups", "store")),
        check_vma=False,
    )
```

time: 559 us -> 110 us (0.20); the launches traced: 548 us -> 109 us
  other arithmetic: 272 us -> 0.22 us
  matrix products: 79.7 us -> 0 us
  waiting for transfers between devices: 76.2 us -> 20.6 us
  Pallas kernels: 0 us -> 46 us
  local copies, waits for them, and re-layouts: 42.7 us -> 5.99 us
  blocking collectives: 56.4 us -> 21.4 us
  between operations: 21.5 us -> 0.78 us
  starting transfers between devices: 0.04 us -> 14.4 us
    another operation x35 -> x3, other arithmetic: 252 us -> 0.22 us  [the longest x2 0.15 us: shards(): where = jnp.stack([base, at]).astype(jnp.int32)]
    psum x1 -> x0, waiting for transfers between devices: 76.2 us -> none  [shards(): fisher = lax.psum(partial_value, 'store')]
    another operation x44 -> x0, matrix products: 46.4 us -> none  [the longest x14 25.9 us: shards(): factor = jnp.linalg.cholesky(system)]
    pallas_call x0 -> x5, Pallas kernels: none -> 46 us  [the longest x1 22.1 us: solve(): pl.pallas_call(functools.partial(solve_kernel, side), in_specs=[SMEM] + [...]
    psum x1 -> x0, blocking collectives: 36.3 us -> none  [shards(): trace_total = lax.psum(local_trace, 'store')]
    dot_general x7 -> x0, matrix products: 33.3 us -> none  [the longest x2 12 us: precise_rows(): lax.dot_general(left_side, right_rows, (((1,), (1,)), ((), ())), precisio...]
    another operation x70 -> x1, local copies, waits for them, and re-layouts: 29.3 us -> 0.1 us  [shards(): jnp.stack(places).astype(jnp.int32)]
    ppermute x0 -> x10, waiting for transfers between devices: none -> 20.6 us  [swap(): return lax.ppermute(value, 'store', [(i, i ^ mask) for i in range(count)])]
  transfers between devices with their start and end apart: 1 -> 10, of which waited for: 1 -> 9; matrix products, arithmetic and copies ran while one was open for 0% -> 0% of each run, Pallas kernels for 0% -> 0%
where the time goes in v1:
time: 110 us; the launch traced here: 109 us
  Pallas kernels  46 us (42%)
  blocking collectives  21.4 us (19%)
  waiting for transfers between devices  20.6 us (19%)
  starting transfers between devices  14.4 us (13%)
  local copies, waits for them, and re-layouts  5.99 us (5%)
    pallas_call x1, Pallas kernels, solve(): pl.pallas_call(functools.partial(solve_kernel, side), in_specs=[SMEM] + [...  22.1 us
    all_gather x1, blocking collectives, shards(): all_queries = lax.all_gather(queries, 'store', axis=0, tiled=True)  21.4 us
    ppermute x10, waiting for transfers between devices, swap(): return lax.ppermute(value, 'store', [(i, i ^ mask) for i in range(count)])  20.6 us
    pallas_call x1, Pallas kernels, gram(): pl.pallas_call(functools.partial(gram_kernel, steps, 0.75 / (count * rows...  19.8 us
    ppermute x10, starting transfers between devices, swap(): return lax.ppermute(value, 'store', [(i, i ^ mask) for i in range(count)])  14.4 us
    unnamed x21, local copies, waits for them, and re-layouts  5.84 us
    pallas_call x3, Pallas kernels, combine(): pl.pallas_call(functools.partial(combine_kernel, members, len(arrived), w...  4.1 us
  transfers between devices with their start and end apart: 10, of which 9 were waited for; matrix products, arithmetic and copies ran while one was open for 0% of the time, Pallas kernels for 0%

profile of v1, /device:TPU:0, one launch (start us, length us, event | category | flops | bytes accessed | tf_op | source)
XLA Modules:
  0.0 109.4 jit_solution(6950252081146589884)
XLA Ops:
  0.6 0.0 copy-start
  0.6 1.6 %copy-done = bf16[256,4096]{1,0:T(8,128)(2,1)S(1)} copy-done((bf16[256,4096]{1,0:T(8,128)(2,1)S(1)}, bf16[256,4096]{1,0:T(8,128)(2,1)}, u32[]{:S(2)}) %copy-start) | copy-done | bytes 2097176
  2.2 0.0 copy-start.1
  2.2 1.2 %copy-done.1 = bf16[32,14336]{1,0:T(8,128)(2,1)S(1)} copy-done((bf16[32,14336]{1,0:T(8,128)(2,1)S(1)}, bf16[32,14336]{1,0:T(8,128)(2,1)}, u32[]{:S(2)}) %copy-start.1) | copy-done | bytes 917528
  3.4 0.0 copy-start.2
  3.4 0.9 copy-done.2
  4.4 0.0 copy-start.3
  4.4 0.7 copy-done.3
  5.1 0.0 copy-start.5
  5.1 0.7 copy-done.5
  5.7 0.0 copy-start.4
  5.7 19.8 %fisher_share.1 = (bf16[4096,1024]{1,0:T(8,128)(2,1)}, f32[8,1024]{1,0:T(8,128)}, f32[2304,128]{1,0:T(8,128)S(1)}, f32[2312,128]{1,0:T(8,128)}, f32[8,128]{1,0:T(8,128)S(1)}) custom-call(s32[1]{0:T(128)} %bitcast.me_ref, s32[1,8]{1,0:T(1,128)S(1)} %copy-done.5, s32[4096,1024]{1,0:T(8,128)} %codes_ref.1, s32[32,128]{1,0:T(8,128)S(1)} %bitcast.23, ...), custom_call_target="tpu_custom_call" | custom-call | flops 6000000000 | bytes 40000000 | tf_op jit(solution)/shard_map/fisher_share/pallas_call | solution.py:174
  25.5 0.5 collective-permute-start
  26.0 0.1 pad_add_fusion.2.refs_0_
  26.0 2.6 %collective-permute-done.refs_4_ = f32[2312,128]{1,0:T(8,128)S(1)} collective-permute-done((f32[2312,128]{1,0:T(8,128)}, f32[2312,128]{1,0:T(8,128)S(1)}, u32[]{:S(2)}, u32[]{:S(2)}) %collective-permute-start) | collective-permute-done | bytes 1183776 | tf_op jit(solution)/shard_map/ppermute | solution.py:472
  28.6 0.0 copy-done.4
  28.7 0.0 copy-start.7
  28.7 0.0 copy-start.6
  28.7 1.6 %sum_shares.3 = (f32[576,128]{1,0:T(8,128)S(1)}, s16[16,128]{1,0:T(8,128)(2,1)S(1)}, s16[592,128]{1,0:T(8,128)(2,1)S(1)}, s16[592,128]{1,0:T(8,128)(2,1)S(1)}, s16[592,128]{1,0:T(8,128)(2,1)S(1)}) custom-call(s32[2]{0:T(128)S(1)} %pad_add_fusion.2.refs_0_, s32[2,36]{1,0:T(2,128)S(1)} %copy-done.4, f32[2304,128]{1,0:T(8,128)S(1)} %get-tuple-element.21.refs_2_, ...), custom_call_target="tpu_custom_call" | custom-call | flops 2949120 | bytes 2359296 | tf_op jit(solution)/shard_map/sum_shares/pallas_call | solution.py:316
  30.3 3.0 %collective-permute-start.1 = (s16[592,128]{1,0:T(8,128)(2,1)S(1)}, s16[592,128]{1,0:T(8,128)(2,1)S(1)}, u32[]{:S(2)}, u32[]{:S(2)}) collective-permute-start(s16[592,128]{1,0:T(8,128)(2,1)S(1)} %get-tuple-element.26), channel_id=1, source_target_pairs={{0,2},{1,3},{2,0},{3,1},{4,6},{5,7},{6,4},{7,5},{8,10},{9,11},{10,... | collective-permute-start | bytes 454664 | tf_op jit(solution)/shard_map/ppermute | solution.py:472
  33.2 1.6 %collective-permute-start.2 = (s16[592,128]{1,0:T(8,128)(2,1)S(1)}, s16[592,128]{1,0:T(8,128)(2,1)S(1)}, u32[]{:S(2)}, u32[]{:S(2)}) collective-permute-start(s16[592,128]{1,0:T(8,128)(2,1)S(1)} %get-tuple-element.27), channel_id=1, source_target_pairs={{0,4},{1,5},{2,6},{3,7},{4,0},{5,1},{6,2},{7,3},{8,12},{9,13},{10,... | collective-permute-start | bytes 454664 | tf_op jit(solution)/shard_map/ppermute | solution.py:472
  34.8 0.0 collective-permute-start.3
  34.8 0.1 pad_add_fusion.1.refs_0_
  34.9 2.6 %collective-permute-done.1.refs_4_ = s16[592,128]{1,0:T(8,128)(2,1)S(1)} collective-permute-done((s16[592,128]{1,0:T(8,128)(2,1)S(1)}, s16[592,128]{1,0:T(8,128)(2,1)S(1)}, u32[]{:S(2)}, u32[]{:S(2)}) %collective-permute-start.1) | collective-permute-done | bytes 151584 | tf_op jit(solution)/shard_map/ppermute | solution.py:472
  37.4 2.6 %collective-permute-done.2.refs_5_ = s16[592,128]{1,0:T(8,128)(2,1)S(1)} collective-permute-done((s16[592,128]{1,0:T(8,128)(2,1)S(1)}, s16[592,128]{1,0:T(8,128)(2,1)S(1)}, u32[]{:S(2)}, u32[]{:S(2)}) %collective-permute-start.2) | collective-permute-done | bytes 151584 | tf_op jit(solution)/shard_map/ppermute | solution.py:472
  40.0 1.9 %collective-permute-done.3.refs_6_ = s16[592,128]{1,0:T(8,128)(2,1)S(1)} collective-permute-done((s16[592,128]{1,0:T(8,128)(2,1)S(1)}, s16[592,128]{1,0:T(8,128)(2,1)S(1)}, u32[]{:S(2)}, u32[]{:S(2)}) %collective-permute-start.3) | collective-permute-done | bytes 151584 | tf_op jit(solution)/shard_map/ppermute | solution.py:472
  41.9 1.5 %sum_shares.4 = (f32[288,128]{1,0:T(8,128)S(1)}, s16[16,128]{1,0:T(8,128)(2,1)S(1)}, s16[304,128]{1,0:T(8,128)(2,1)S(1)}) custom-call(s32[2]{0:T(128)S(1)} %pad_add_fusion.1.refs_0_, s32[2,36]{1,0:T(2,128)S(1)} %copy-done.4, f32[576,128]{1,0:T(8,128)S(1)} %get-tuple-element.24.refs_2_, s16[16,128]{1,0:T(8,128)(2,1)S(1)} %get-tuple-element.25.refs_3_, ...), custom_call_target="tpu_custom_call" | custom-call | flops 737280 | bytes 589824 | tf_op jit(solution)/shard_map/sum_shares/pallas_call | solution.py:316
  43.4 2.8 %collective-permute-start.4 = (s16[304,128]{1,0:T(8,128)(2,1)S(1)}, s16[304,128]{1,0:T(8,128)(2,1)S(1)}, u32[]{:S(2)}, u32[]{:S(2)}) collective-permute-start(s16[304,128]{1,0:T(8,128)(2,1)S(1)} %get-tuple-element.31), channel_id=1, source_target_pairs={{0,8},{1,9},{2,10},{3,11},{4,12},{5,13},{6,14},{7,15},{8,0},{9,1},... | collective-permute-start | bytes 233480 | tf_op jit(solution)/shard_map/ppermute | solution.py:472
  46.2 0.1 pad_add_fusion.refs_0_
  46.3 2.5 %collective-permute-done.4.refs_4_ = s16[304,128]{1,0:T(8,128)(2,1)S(1)} collective-permute-done((s16[304,128]{1,0:T(8,128)(2,1)S(1)}, s16[304,128]{1,0:T(8,128)(2,1)S(1)}, u32[]{:S(2)}, u32[]{:S(2)}) %collective-permute-start.4) | collective-permute-done | bytes 77856 | tf_op jit(solution)/shard_map/ppermute | solution.py:472
  48.8 1.0 sum_shares.5
  49.8 2.9 %collective-permute-start.5 = (s16[288,128]{1,0:T(8,128)(2,1)S(1)}, s16[288,128]{1,0:T(8,128)(2,1)S(1)}, u32[]{:S(2)}, u32[]{:S(2)}) collective-permute-start(s16[288,128]{1,0:T(8,128)(2,1)S(1)} %get-tuple-element.32), channel_id=1, source_target_pairs={{0,8},{1,9},{2,10},{3,11},{4,12},{5,13},{6,14},{7,15},{8,0},{9,1},... | collective-permute-start | bytes 221192 | tf_op jit(solution)/shard_map/ppermute | solution.py:472
  52.7 2.4 %collective-permute-done.5 = s16[288,128]{1,0:T(8,128)(2,1)S(1)} collective-permute-done((s16[288,128]{1,0:T(8,128)(2,1)S(1)}, s16[288,128]{1,0:T(8,128)(2,1)S(1)}, u32[]{:S(2)}, u32[]{:S(2)}) %collective-permute-start.5) | collective-permute-done | bytes 73760 | tf_op jit(solution)/shard_map/ppermute | solution.py:472
  55.2 1.7 %collective-permute-start.6 = (s16[576,128]{1,0:T(8,128)(2,1)S(1)}, s16[576,128]{1,0:T(8,128)(2,1)S(1)}, u32[]{:S(2)}, u32[]{:S(2)}) collective-permute-start(s16[576,128]{1,0:T(8,128)(2,1)S(1)} %get-tuple-element.43), channel_id=1, source_target_pairs={{0,2},{1,3},{2,0},{3,1},{4,6},{5,7},{6,4},{7,5},{8,10},{9,11},{10,... | collective-permute-start | bytes 442376 | tf_op jit(solution)/shard_map/ppermute | solution.py:472
  56.9 2.0 %collective-permute-start.7 = (s16[576,128]{1,0:T(8,128)(2,1)S(1)}, s16[576,128]{1,0:T(8,128)(2,1)S(1)}, u32[]{:S(2)}, u32[]{:S(2)}) collective-permute-start(s16[576,128]{1,0:T(8,128)(2,1)S(1)} %get-tuple-element.43), channel_id=1, source_target_pairs={{0,4},{1,5},{2,6},{3,7},{4,0},{5,1},{6,2},{7,3},{8,12},{9,13},{10,... | collective-permute-start | bytes 442376 | tf_op jit(solution)/shard_map/ppermute | solution.py:472
  58.9 0.0 collective-permute-start.8
  58.9 3.1 %collective-permute-done.6 = s16[576,128]{1,0:T(8,128)(2,1)S(1)} collective-permute-done((s16[576,128]{1,0:T(8,128)(2,1)S(1)}, s16[576,128]{1,0:T(8,128)(2,1)S(1)}, u32[]{:S(2)}, u32[]{:S(2)}) %collective-permute-start.6) | collective-permute-done | bytes 147488 | tf_op jit(solution)/shard_map/ppermute | solution.py:472
  62.0 0.1 collective-permute-done.7
  62.1 2.8 %collective-permute-done.8 = s16[576,128]{1,0:T(8,128)(2,1)S(1)} collective-permute-done((s16[576,128]{1,0:T(8,128)(2,1)S(1)}, s16[576,128]{1,0:T(8,128)(2,1)S(1)}, u32[]{:S(2)}, u32[]{:S(2)}) %collective-permute-start.8) | collective-permute-done | bytes 147488 | tf_op jit(solution)/shard_map/ppermute | solution.py:472
  64.9 0.1 collective-permute-start.9
  65.0 0.0 copy-done.7
  65.1 21.4 %all-gather = bf16[16,4,1024]{2,1,0:T(4,128)(2,1)S(1)} all-gather(bf16[1,4,1024]{2,1,0:T(4,128)(2,1)S(1)} %bitcast.24), channel_id=1, replica_groups=mesh['groups'=2,'store'=16] {'store'}, dimensions={0}, use_global_device_ids=true | all-gather | bytes 139264 | tf_op jit(solution)/shard_map/all_gather | solution.py:481
  86.5 0.1 stack.89.places_ref
  86.6 0.0 collective-permute-done.9.second_ref
  86.6 0.0 copy-done.6
  86.6 22.1 %solve_and_score.1 = (f32[64,4096]{1,0:T(8,128)}, f32[64,8]{1,0:T(8,128)S(1)}) custom-call(s32[16]{0:T(128)S(1)} %stack.89.places_ref, s16[2304,128]{1,0:T(8,128)(2,1)S(1)} %constant_dynamic-update-slice_fusion.2.first_ref, s16[2304,128]{1,0:T(8,128)(2,1)S(1)} %collective-permute-done.9.second_ref, s16[16,128]{1,0:T(8,128)(2,1)S(1)} %get-tuple-element.33.state_ref, ...), custom_call_target="tpu_custom_call" | custom-call | flops 10000000000 | bytes 20000000 | tf_op jit(solution)/shard_map/solve_and_score/pallas_call | solution.py:445
  108.8 0.7 copy.13
  (6 shorter events, 0.1 us)
Async XLA Ops:
  0.6 1.6 %copy-start = (bf16[256,4096]{1,0:T(8,128)(2,1)S(1)}, bf16[256,4096]{1,0:T(8,128)(2,1)}, u32[]{:S(2)}) copy-start(bf16[256,4096]{1,0:T(8,128)(2,1)} %act_ref.1) | copy-start | bytes 6291460
  2.2 1.2 %copy-start.1 = (bf16[32,14336]{1,0:T(8,128)(2,1)S(1)}, bf16[32,14336]{1,0:T(8,128)(2,1)}, u32[]{:S(2)}) copy-start(bf16[32,14336]{1,0:T(8,128)(2,1)} %basis_out_ref.1) | copy-start | bytes 2752516
  3.4 0.9 copy-start.2
  4.4 0.7 copy-start.3
  5.1 0.7 copy-start.5
  5.7 22.9 %copy-start.4 = (s32[2,36]{1,0:T(2,128)S(1)}, s32[2,36]{1,0:T(2,128)}, u32[]{:S(2)}) copy-start(s32[2,36]{1,0:T(2,128)} %constant.20.clone.refs_1_) | copy-start | bytes 868
  25.5 3.1 %collective-permute-start = (f32[2312,128]{1,0:T(8,128)}, f32[2312,128]{1,0:T(8,128)S(1)}, u32[]{:S(2)}, u32[]{:S(2)}) collective-permute-start(f32[2312,128]{1,0:T(8,128)} %get-tuple-element.23), channel_id=1, source_target_pairs={{0,1},{1,0},{2,3},{3,2},{4,5},{5,4},{6,7},{7,6},{8,9},{9,8},{10,11... | collective-permute-start | bytes 3551240 | tf_op jit(solution)/shard_map/ppermute | solution.py:472
  28.7 36.4 %copy-start.7 = (bf16[4,1024]{1,0:T(4,128)(2,1)S(1)}, bf16[4,1024]{1,0:T(4,128)(2,1)}, u32[]{:S(2)}) copy-start(bf16[4,1024]{1,0:T(4,128)(2,1)} %param.16) | copy-start | bytes 24580
  28.7 58.0 %copy-start.6 = (f32[8,1024]{1,0:T(8,128)S(1)}, f32[8,1024]{1,0:T(8,128)}, u32[]{:S(2)}) copy-start(f32[8,1024]{1,0:T(8,128)} %get-tuple-element.40.new_rows_ref) | copy-start | bytes 98308
  30.3 7.2 %collective-permute-start.1 = (s16[592,128]{1,0:T(8,128)(2,1)S(1)}, s16[592,128]{1,0:T(8,128)(2,1)S(1)}, u32[]{:S(2)}, u32[]{:S(2)}) collective-permute-start(s16[592,128]{1,0:T(8,128)(2,1)S(1)} %get-tuple-element.26), channel_id=1, source_target_pairs={{0,2},{1,3},{2,0},{3,1},{4,6},{5,7},{6,4},{7,5},{8,10},{9,11},{10,... | collective-permute-start | bytes 454664 | tf_op jit(solution)/shard_map/ppermute | solution.py:472
  33.2 6.8 %collective-permute-start.2 = (s16[592,128]{1,0:T(8,128)(2,1)S(1)}, s16[592,128]{1,0:T(8,128)(2,1)S(1)}, u32[]{:S(2)}, u32[]{:S(2)}) collective-permute-start(s16[592,128]{1,0:T(8,128)(2,1)S(1)} %get-tuple-element.27), channel_id=1, source_target_pairs={{0,4},{1,5},{2,6},{3,7},{4,0},{5,1},{6,2},{7,3},{8,12},{9,13},{10,... | collective-permute-start | bytes 454664 | tf_op jit(solution)/shard_map/ppermute | solution.py:472
  34.8 7.2 %collective-permute-start.3 = (s16[592,128]{1,0:T(8,128)(2,1)S(1)}, s16[592,128]{1,0:T(8,128)(2,1)S(1)}, u32[]{:S(2)}, u32[]{:S(2)}) collective-permute-start(s16[592,128]{1,0:T(8,128)(2,1)S(1)} %get-tuple-element.28), channel_id=1, source_target_pairs={{0,6},{1,7},{2,4},{3,5},{4,2},{5,3},{6,0},{7,1},{8,14},{9,15},{10,... | collective-permute-start | bytes 454664 | tf_op jit(solution)/shard_map/ppermute | solution.py:472
  43.4 5.4 %collective-permute-start.4 = (s16[304,128]{1,0:T(8,128)(2,1)S(1)}, s16[304,128]{1,0:T(8,128)(2,1)S(1)}, u32[]{:S(2)}, u32[]{:S(2)}) collective-permute-start(s16[304,128]{1,0:T(8,128)(2,1)S(1)} %get-tuple-element.31), channel_id=1, source_target_pairs={{0,8},{1,9},{2,10},{3,11},{4,12},{5,13},{6,14},{7,15},{8,0},{9,1},... | collective-permute-start | bytes 233480 | tf_op jit(solution)/shard_map/ppermute | solution.py:472
  49.8 5.3 %collective-permute-start.5 = (s16[288,128]{1,0:T(8,128)(2,1)S(1)}, s16[288,128]{1,0:T(8,128)(2,1)S(1)}, u32[]{:S(2)}, u32[]{:S(2)}) collective-permute-start(s16[288,128]{1,0:T(8,128)(2,1)S(1)} %get-tuple-element.32), channel_id=1, source_target_pairs={{0,8},{1,9},{2,10},{3,11},{4,12},{5,13},{6,14},{7,15},{8,0},{9,1},... | collective-permute-start | bytes 221192 | tf_op jit(solution)/shard_map/ppermute | solution.py:472
  55.2 6.7 %collective-permute-start.6 = (s16[576,128]{1,0:T(8,128)(2,1)S(1)}, s16[576,128]{1,0:T(8,128)(2,1)S(1)}, u32[]{:S(2)}, u32[]{:S(2)}) collective-permute-start(s16[576,128]{1,0:T(8,128)(2,1)S(1)} %get-tuple-element.43), channel_id=1, source_target_pairs={{0,2},{1,3},{2,0},{3,1},{4,6},{5,7},{6,4},{7,5},{8,10},{9,11},{10,... | collective-permute-start | bytes 442376 | tf_op jit(solution)/shard_map/ppermute | solution.py:472
  56.9 5.1 %collective-permute-start.7 = (s16[576,128]{1,0:T(8,128)(2,1)S(1)}, s16[576,128]{1,0:T(8,128)(2,1)S(1)}, u32[]{:S(2)}, u32[]{:S(2)}) collective-permute-start(s16[576,128]{1,0:T(8,128)(2,1)S(1)} %get-tuple-element.43), channel_id=1, source_target_pairs={{0,4},{1,5},{2,6},{3,7},{4,0},{5,1},{6,2},{7,3},{8,12},{9,13},{10,... | collective-permute-start | bytes 442376 | tf_op jit(solution)/shard_map/ppermute | solution.py:472
  58.9 6.0 %collective-permute-start.8 = (s16[576,128]{1,0:T(8,128)(2,1)S(1)}, s16[576,128]{1,0:T(8,128)(2,1)S(1)}, u32[]{:S(2)}, u32[]{:S(2)}) collective-permute-start(s16[576,128]{1,0:T(8,128)(2,1)S(1)} %get-tuple-element.43), channel_id=1, source_target_pairs={{0,6},{1,7},{2,4},{3,5},{4,2},{5,3},{6,0},{7,1},{8,14},{9,15},{10,... | collective-permute-start | bytes 442376 | tf_op jit(solution)/shard_map/ppermute | solution.py:472
  64.9 21.7 %collective-permute-start.9 = (s16[2304,128]{1,0:T(8,128)(2,1)S(1)}, s16[2304,128]{1,0:T(8,128)(2,1)S(1)}, u32[]{:S(2)}, u32[]{:S(2)}) collective-permute-start(s16[2304,128]{1,0:T(8,128)(2,1)S(1)} %constant_dynamic-update-slice_fusion.2.first_ref), channel_id=1, source_target_pairs={{0,1},{1,0},{2,3},{3,2},{4,5},{5,4},{6,7},{7,6},{8,9},{9,8},{10,11... | collective-permute-start | bytes 1769480 | tf_op jit(solution)/shard_map/ppermute | solution.py:472

commit v2 on v1

--- a/solution.py
+++ b/solution.py
@@ -60,157 +60,234 @@
     )
 
 
+def code_floats(value):
+    size = jnp.abs(value.astype(F32))
+    power = jnp.floor(jnp.log2(jnp.maximum(size, 2.0**-126)))
+    mantissa = size * jnp.exp2(-power)
+    power = power + jnp.where(mantissa >= 2.0, 1.0, 0.0) - jnp.where(mantissa < 1.0, 1.0, 0.0)
+    mantissa = jnp.where(
+        mantissa >= 2.0, mantissa * 0.5, jnp.where(mantissa < 1.0, mantissa * 2.0, mantissa)
+    )
+    code = (power + 127.0) * 128.0 + jnp.round((mantissa - 1.0) * 128.0)
+    code = jnp.where(size < 2.0**-126, 0.0, code)
+    return jnp.where(value.astype(F32) < 0.0, -code, code)
+
+
+def float_of(code):
+    size = jnp.abs(code)
+    power = lax.shift_right_logical(size, 7).astype(F32) - 127.0
+    value = (1.0 + (size & 127).astype(F32) / 128.0) * jnp.exp2(power)
+    value = jnp.where(size == 0, 0.0, value)
+    return jnp.where(code < 0, -value, value)
+
+
+def decode(codes_ref, scale_ref, start, target_ref):
+    rows, width = target_ref.shape
+    for g in range(rows // LANES):
+        index = scale_ref[pl.ds(start // LANES + g, 1), :]
+        scale = column_of(jnp.exp2(index.astype(F32) / 16.0) / 128.0)
+        at = pl.multiple_of(start + g * LANES, LANES)
+        for c in range(width // LANES):
+            cols = slice(c * LANES, (c + 1) * LANES)
+            value = codes_ref[pl.ds(at, LANES), cols].astype(F32) * scale
+            target_ref[g * LANES : (g + 1) * LANES, cols] = value.astype(BF16)
+
+
 def gram_kernel(
-    steps,
     weight_store,
     weight_new,
     me_ref,
     lengths_ref,
-    codes_ref,
     scale_ref,
-    act_ref,
-    grad_ref,
-    basis_in_ref,
-    basis_out_ref,
-    stored_ref,
+    queries_ref,
+    act_hbm,
+    grad_hbm,
+    basis_in_hbm,
+    basis_out_hbm,
+    codes_hbm,
     new_rows_ref,
     keep_ref,
     send_ref,
     diag_ref,
+    asked_ref,
+    act,
+    grad,
+    basis_in,
+    basis_out,
+    codes,
+    stored,
+    stored_next,
     total,
-    proj_in,
-    proj_out,
+    sems,
+    code_sems,
 ):
-    step = pl.program_id(0)
-    chunk, width = codes_ref.shape
-    rank = basis_in_ref.shape[0]
-    tokens = act_ref.shape[0]
+    rows, width = codes.shape
+    rank = basis_in.shape[0]
+    tokens = act.shape[0]
     examples = new_rows_ref.shape[0]
-
-    @pl.when(step == 0)
-    def _():
-        total[...] = jnp.zeros_like(total)
-        proj_in[...] = jnp.zeros_like(proj_in)
-        proj_out[...] = jnp.zeros_like(proj_out)
-
-    groups = chunk // LANES
-    for g in range(groups):
-        index = scale_ref[pl.ds(step * groups + g, 1), :]
-        scale = column_of(jnp.exp2(index.astype(F32) / 16.0) / 128.0)
-        rows = slice(g * LANES, (g + 1) * LANES)
-        for c in range(width // LANES):
-            cols = slice(c * LANES, (c + 1) * LANES)
-            stored_ref[rows, cols] = (codes_ref[rows, cols].astype(F32) * scale).astype(BF16)
-    stored = stored_ref[...]
+    chunk = stored.shape[0]
+    cuts = 4
+    span = grad.shape[1] // cuts
+    parts = [(basis_out_hbm, basis_out)]
+    for c in range(cuts):
+        at = (slice(None), slice(c * span, (c + 1) * span))
+        parts.append((grad_hbm.at[at], grad.at[at]))
+    parts += [(basis_in_hbm, basis_in), (act_hbm, act)]
+    copies = [
+        pltpu.make_async_copy(source, target, sems.at[i])
+        for i, (source, target) in enumerate(parts)
+    ]
+
+    def code_copy(c):
+        at = pl.ds(pl.multiple_of(c * chunk, chunk), chunk)
+        return pltpu.make_async_copy(codes_hbm.at[at, :], codes.at[at, :], code_sems.at[c])
+
+    chunks = rows // chunk
+    for c in range(chunks // 2):
+        code_copy(c).start()
+    for copy in copies:
+        copy.start()
+    for c in range(chunks // 2, chunks):
+        code_copy(c).start()
+    asked = code_floats(queries_ref[...])
+    asked = [asked[:, i * LANES : (i + 1) * LANES] for i in range(width // LANES)]
+    asked_ref[...] = jnp.concatenate(asked, axis=0).astype(jnp.int32).astype(jnp.int16)
     side = 256
-    for i in range(width // side):
-        rows = slice(i * side, (i + 1) * side)
-        total[rows, : (i + 1) * side] += mm(stored[:, rows], stored[:, : (i + 1) * side], TN)
-    proj_in[...] += mm(act_ref[...], basis_in_ref[...], NT)
-    proj_out[...] += mm(grad_ref[...], basis_out_ref[...], NT)
-
-    @pl.when(step == steps - 1)
-    def _():
-        wide = (3 * rank, width)
-        k = lax.broadcasted_iota(jnp.int32, wide, 0) % rank
-        c = lax.broadcasted_iota(jnp.int32, wide, 1)
-        pick_in = (k == c // rank).astype(F32).astype(BF16)
-        pick_out = (k == c % rank).astype(F32).astype(BF16)
-        left = mm(jnp.concatenate(split3(proj_in[...]), axis=1), pick_in)
-        right = mm(jnp.concatenate(split3(proj_out[...]), axis=1), pick_out)
-        products = split3(left * right)
-        place = lax.broadcasted_iota(jnp.int32, (examples, tokens), 1)
-        owner = lax.broadcasted_iota(jnp.int32, (examples, tokens), 0)
-        member = jnp.zeros((examples, tokens), F32)
-        start = jnp.int32(0)
-        for e in range(examples):
-            finish = start + lengths_ref[0, e]
-            inside = (owner == e) & (place >= start) & (place < finish)
-            member = jnp.where(inside, 1.0, member)
-            start = finish
-        member = member.astype(BF16)
-        new_rows = mm(member, products[0]) + (mm(member, products[1]) + mm(member, products[2]))
-        new_rows_ref[...] = new_rows
-        high, mid, low = [part.astype(F32) for part in split3(new_rows)]
-        first = jnp.concatenate([high, high, mid, high, low, mid], axis=0).astype(BF16)
-        second = jnp.concatenate([high, mid, high, low, high, mid], axis=0).astype(BF16)
+
+    def ready(c, target):
+        code_copy(c).wait()
+        decode(codes, scale_ref, c * chunk, target)
+
+    def add(source, first):
         for i in range(width // side):
-            rows = slice(i * side, (i + 1) * side)
-            total[rows, : (i + 1) * side] = weight_store * total[
-                rows, : (i + 1) * side
-            ] + weight_new * mm(first[:, rows], second[:, : (i + 1) * side], TN)
-        tiles = triangle(width)
-        half = len(tiles) // 2
-        diagonal = eye(LANES)
-        for i in range(width // LANES):
-            at = slice(i * LANES, (i + 1) * LANES)
-            diag_ref[i : i + 1, :] = jnp.sum(
-                jnp.where(diagonal, total[at, at], 0.0), axis=0, keepdims=True
-            )
-        send_ref[half * LANES :, :] = diag_ref[...]
-        for b, (i, j) in enumerate(tiles):
-            rows = slice(b % half * LANES, (b % half + 1) * LANES)
-            tile = total[i * LANES : (i + 1) * LANES, j * LANES : (j + 1) * LANES]
-
-            @pl.when(me_ref[0] == b // half)
-            def _():
-                keep_ref[rows, :] = tile
-
-            @pl.when(me_ref[0] != b // half)
-            def _():
-                send_ref[rows, :] = tile
-
-
-def gram(me, lengths, codes, scale_index, activations, out_grads, basis_in, basis_out, count):
+            at = slice(i * side, (i + 1) * side)
+            to = slice(0, (i + 1) * side)
+            value = mm(source[:, at], source[:, to], TN)
+            total[at, to] = value if first else total[at, to] + value
+
+    ready(0, stored)
+    ready(1, stored_next)
+    add(stored, True)
+
+    def body(pair, _):
+        ready(2 * pair + 2, stored)
+        add(stored_next, False)
+        ready(2 * pair + 3, stored_next)
+        add(stored, False)
+        return 0
+
+    lax.fori_loop(0, chunks // 4 - 1, body, 0)
+    copies[0].wait()
+    proj_out = jnp.zeros((tokens, rank), F32)
+    for c in range(cuts):
+        copies[1 + c].wait()
+        at = (slice(None), slice(c * span, (c + 1) * span))
+        proj_out = proj_out + mm(grad[at], basis_out[at], NT)
+    copies[-2].wait()
+    copies[-1].wait()
+    proj_in = mm(act[...], basis_in[...], NT)
+    wide = (3 * rank, width)
+    k = lax.broadcasted_iota(jnp.int32, wide, 0) & (rank - 1)
+    c = lax.broadcasted_iota(jnp.int32, wide, 1)
+    pick_in = (k == lax.shift_right_logical(c, rank.bit_length() - 1)).astype(F32).astype(BF16)
+    pick_out = (k == (c & (rank - 1))).astype(F32).astype(BF16)
+    left = mm(jnp.concatenate(split3(proj_in), axis=1), pick_in)
+    right = mm(jnp.concatenate(split3(proj_out), axis=1), pick_out)
+    products = split3(left * right)
+    place = lax.broadcasted_iota(jnp.int32, (examples, tokens), 1)
+    owner = lax.broadcasted_iota(jnp.int32, (examples, tokens), 0)
+    member = jnp.zeros((examples, tokens), F32)
+    start = jnp.int32(0)
+    for e in range(examples):
+        finish = start + lengths_ref[0, e]
+        inside = (owner == e) & (place >= start) & (place < finish)
+        member = jnp.where(inside, 1.0, member)
+        start = finish
+    member = member.astype(BF16)
+    new_rows = mm(member, products[0]) + (mm(member, products[1]) + mm(member, products[2]))
+    new_rows_ref[...] = new_rows
+    high, mid, low = [part.astype(F32) for part in split3(new_rows)]
+    first = jnp.concatenate([high, high, mid, high, low, mid], axis=0).astype(BF16)
+    second = jnp.concatenate([high, mid, high, low, high, mid], axis=0).astype(BF16)
+    lax.fori_loop(chunks // 4 - 1, chunks // 2 - 1, body, 0)
+    add(stored_next, False)
+    tiles = triangle(width)
+    half = len(tiles) // 2
+    diagonal = eye(LANES)
+
+    def finish(mine):
+        for i in range(width // side):
+            for j in range(i + 1):
+                down = slice(i * side, (i + 1) * side)
+                across = slice(j * side, (j + 1) * side)
+                value = weight_store * total[down, across] + weight_new * mm(
+                    first[:, down], second[:, across], TN
+                )
+                for b, (p, q) in enumerate(tiles):
+                    if p // 2 != i or q // 2 != j:
+                        continue
+                    tile = value[
+                        p % 2 * LANES : (p % 2 + 1) * LANES, q % 2 * LANES : (q % 2 + 1) * LANES
+                    ]
+                    target = keep_ref if b // half == mine else send_ref
+                    target[b % half * LANES : (b % half + 1) * LANES, :] = tile
+                    if p == q:
+                        diag_ref[p : p + 1, :] = jnp.sum(
+                            jnp.where(diagonal, tile, 0.0), axis=0, keepdims=True
+                        )
+
+    for mine in range(2):
+        pl.when(me_ref[0] == mine)(functools.partial(finish, mine))
+    send_ref[half * LANES :, :] = diag_ref[...]
+
+
+def gram(
+    me, lengths, codes, scale_index, queries, activations, out_grads, basis_in, basis_out, count
+):
     rows, width = codes.shape
-    tokens, inputs = activations.shape
-    outputs = out_grads.shape[1]
-    rank = basis_in.shape[0]
     examples = lengths.shape[1]
-    steps = 8
     half = len(triangle(width)) // 2 * LANES
-    chunk = rows // steps
-    whole = lambda *shape: pl.BlockSpec(shape, lambda s: (0,) * len(shape))
+    chunk = 256
+    extra = width // LANES
     return pl.pallas_call(
-        functools.partial(
-            gram_kernel, steps, 0.75 / (count * rows), 0.25 / (count * examples)
-        ),
-        grid=(steps,),
-        in_specs=[
-            SMEM,
-            SMEM,
-            pl.BlockSpec((chunk, width), lambda s: (s, 0)),
-            whole(rows // LANES, LANES),
-            pl.BlockSpec((tokens, inputs // steps), lambda s: (0, s)),
-            pl.BlockSpec((tokens, outputs // steps), lambda s: (0, s)),
-            pl.BlockSpec((rank, inputs // steps), lambda s: (0, s)),
-            pl.BlockSpec((rank, outputs // steps), lambda s: (0, s)),
-        ],
-        out_specs=[
-            pl.BlockSpec((chunk, width), lambda s: (s, 0)),
-            whole(examples, width),
-            whole(half, LANES),
-            whole(half + width // LANES, LANES),
-            whole(width // LANES, LANES),
-        ],
+        functools.partial(gram_kernel, 0.75 / (count * rows), 0.25 / (count * examples)),
+        in_specs=[SMEM, SMEM, VMEM, VMEM] + [ANY] * 5,
+        out_specs=[VMEM] * 5,
         out_shape=[
-            jax.ShapeDtypeStruct((rows, width), BF16),
             jax.ShapeDtypeStruct((examples, width), F32),
             jax.ShapeDtypeStruct((half, LANES), F32),
-            jax.ShapeDtypeStruct((half + width // LANES, LANES), F32),
-            jax.ShapeDtypeStruct((width // LANES, LANES), F32),
+            jax.ShapeDtypeStruct((half + extra, LANES), F32),
+            jax.ShapeDtypeStruct((extra, LANES), F32),
+            jax.ShapeDtypeStruct((queries.shape[0] * extra, LANES), jnp.int16),
         ],
         scratch_shapes=[
+            pltpu.VMEM(activations.shape, BF16),
+            pltpu.VMEM(out_grads.shape, BF16),
+            pltpu.VMEM(basis_in.shape, BF16),
+            pltpu.VMEM(basis_out.shape, BF16),
+            pltpu.VMEM((rows, width), jnp.int32),
+            pltpu.VMEM((chunk, width), BF16),
+            pltpu.VMEM((chunk, width), BF16),
             pltpu.VMEM((width, width), F32),
-            pltpu.VMEM((tokens, rank), F32),
-            pltpu.VMEM((tokens, rank), F32),
+            pltpu.SemaphoreType.DMA((8,)),
+            pltpu.SemaphoreType.DMA((rows // chunk,)),
         ],
-        compiler_params=pltpu.CompilerParams(vmem_limit_bytes=48 << 20),
+        compiler_params=pltpu.CompilerParams(vmem_limit_bytes=60 << 20),
         cost_estimate=pl.CostEstimate(
-            flops=6 * 10**9, bytes_accessed=40 * 10**6, transcendentals=0
+            flops=6 * 10**9, bytes_accessed=30 * 10**6, transcendentals=0
         ),
         name="fisher_share",
-    )(me, lengths, codes, scale_index, activations, out_grads, basis_in, basis_out)
+    )(
+        me,
+        lengths,
+        scale_index,
+        queries,
+        activations,
+        out_grads,
+        basis_in,
+        basis_out,
+        codes,
+    )
 
 
 def exponents(diag):
@@ -251,6 +328,8 @@
     where_ref, table_ref, own_ref, state_ref = refs[:4]
     arrived = refs[4 : 4 + coded]
     refs = refs[4 + coded :]
+    if not members:
+        asked_ref, refs = refs[0], refs[1:]
     out_own, out_state = refs[:2]
     out_messages = refs[2 : 1 + members] if members > 1 else ()
     refs = refs[max(1, members) + 1 :]
@@ -298,24 +377,28 @@
 
         lax.fori_loop(0, part // strip, body, 0, unroll=2)
     write_exps(out_state, 0, exps)
+    if not members:
+        out_own[rows:, :] = asked_ref[...]
     for ref in out_messages:
         write_exps(ref, part, exps)
 
 
-def combine(where, table, own, state, arrived, members, strip):
+def combine(where, table, own, state, arrived, members, strip, asked=()):
     rows = own.shape[0]
     tiles = table.shape[1]
     width_tiles = int(round(((8 * tiles + 1) ** 0.5 - 1) / 2))
     width = width_tiles * LANES
     part = rows // max(members, 1)
     outs = [
-        jax.ShapeDtypeStruct((part, LANES), F32 if members > 1 else jnp.int16),
+        jax.ShapeDtypeStruct(
+            (part + sum(a.shape[0] for a in asked), LANES), F32 if members > 1 else jnp.int16
+        ),
         jax.ShapeDtypeStruct((PACK, LANES), jnp.int16),
     ]
     outs += [jax.ShapeDtypeStruct((part + PACK, LANES), jnp.int16)] * max(members - 1, 0)
     return pl.pallas_call(
         functools.partial(combine_kernel, members, len(arrived), width_tiles, strip),
-        in_specs=[SMEM, SMEM] + [VMEM] * (2 + len(arrived)),
+        in_specs=[SMEM, SMEM] + [VMEM] * (2 + len(arrived) + len(asked)),
         out_specs=[VMEM] * len(outs),
         out_shape=outs,
         scratch_shapes=[
@@ -329,18 +412,19 @@
             flops=10 * rows * LANES, bytes_accessed=8 * rows * LANES, transcendentals=0
         ),
         name="sum_shares",
-    )(where, table, own, state, *arrived)
+    )(where, table, own, state, *arrived, *asked)
 
 
 def solve_kernel(
     side,
+    slot_bits,
     places_ref,
     first_ref,
     second_ref,
     state_ref,
-    queries_ref,
     new_rows_ref,
-    stored_hbm,
+    scale_ref,
+    codes_hbm,
     scores_ref,
     new_scores_ref,
     flat,
@@ -350,18 +434,41 @@
     solved,
     columns,
     rows_ref,
+    codes,
     sem,
 ):
-    copy = pltpu.make_async_copy(stored_hbm, stored, sem)
+    copy = pltpu.make_async_copy(codes_hbm, codes, sem)
     copy.start()
-    queries, width = queries_ref.shape
+    queries, width = solved.shape
     tiles = width // LANES
-    pieces = places_ref.shape[0]
+    pieces = places_ref.shape[0] - 1
     piece = flat.shape[0] // pieces
+    pitch = 2 * first_ref.shape[0] // pieces
+    asked = []
     for p in range(pieces):
         source = first_ref if p < pieces // 2 else second_ref
-        at = p % (pieces // 2) * piece
+        at = p % (pieces // 2) * pitch
         flat[pl.ds(pl.multiple_of(places_ref[p], PACK), piece), :] = source[at : at + piece, :]
+        asked.append(source[at + piece : at + pitch, :].astype(jnp.int32))
+    asked = float_of(jnp.concatenate(asked, axis=0)).astype(BF16)
+    each = queries // pieces
+    order = (tiles * queries, asked.shape[0])
+    to = lax.broadcasted_iota(jnp.int32, order, 0)
+    source = lax.broadcasted_iota(jnp.int32, order, 1)
+    slot = lax.shift_right_logical(source, (pitch - piece).bit_length() - 1)
+    owner = jnp.zeros(order, jnp.int32)
+    for bit, position in enumerate(slot_bits):
+        owner = owner | ((lax.shift_right_logical(slot, position) & 1) << bit)
+    owner = owner ^ places_ref[pieces]
+    inside = source & (pitch - piece - 1)
+    target = (
+        lax.shift_right_logical(inside, each.bit_length() - 1) * queries
+        + owner * each
+        + (inside & (each - 1))
+    )
+    asked = mm((target == to).astype(F32).astype(BF16), asked)
+    for i in range(tiles):
+        system[width:, i * LANES : (i + 1) * LANES] = asked[i * queries : (i + 1) * queries, :]
     fill_scales(read_exps(state_ref, 0, tiles), 1.0 / CODE_MAX, columns, rows_ref)
     diagonal = eye(LANES)
     trace = jnp.zeros((1, LANES), F32)
@@ -377,7 +484,6 @@
     for i in range(tiles):
         at = slice(i * LANES, (i + 1) * LANES)
         system[at, at] += jnp.where(diagonal, damp, 0.0)
-    system[width:, :] = queries_ref[...].astype(F32)
     blocks = width // side
     spans = [slice(b * side, (b + 1) * side) for b in range(blocks)]
     bounds = [
@@ -430,20 +536,26 @@
     new_scores_ref[...] = mm3((high, low), split2(new_rows_ref[...]), NT)
     both = jnp.concatenate([high, low], axis=0)
     copy.wait()
-    span = 512
-    for r in range(0, stored.shape[0], span):
-        value = mm(both, stored[r : r + span, :], NT)
-        scores_ref[:, r : r + span] = value[:queries, :] + value[queries:, :]
-
-
-def solve(places, first, second, state, queries, new_rows, stored):
-    count, width = queries.shape
-    rows = stored.shape[0]
+    span = stored.shape[0]
+
+    def score(c, _):
+        at = pl.multiple_of(c * span, span)
+        decode(codes, scale_ref, at, stored)
+        value = mm(both, stored[...], NT)
+        scores_ref[:, pl.ds(at, span)] = value[:queries, :] + value[queries:, :]
+        return 0
+
+    lax.fori_loop(0, codes.shape[0] // span, score, 0, unroll=2)
+
+
+def solve(places, slot_bits, first, second, state, new_rows, scale_index, codes, count):
+    rows, width = codes.shape
     examples = new_rows.shape[0]
     side = 256
+    span = 512
     flat_rows = len(triangle(width)) * LANES
     return pl.pallas_call(
-        functools.partial(solve_kernel, side),
+        functools.partial(solve_kernel, side, slot_bits),
         in_specs=[SMEM] + [VMEM] * 5 + [ANY],
         out_specs=[VMEM, VMEM],
         out_shape=[
@@ -454,18 +566,19 @@
             pltpu.VMEM((flat_rows, LANES), jnp.int16),
             pltpu.VMEM((width + count, width), F32),
             pltpu.VMEM((2 * side, side), F32),
-            pltpu.VMEM((rows, width), BF16),
+            pltpu.VMEM((span, width), BF16),
             pltpu.VMEM((count, width), F32),
             pltpu.VMEM((width, LANES), F32),
             pltpu.VMEM((width // LANES, LANES), F32),
+            pltpu.VMEM((rows, width), jnp.int32),
             pltpu.SemaphoreType.DMA,
         ],
-        compiler_params=pltpu.CompilerParams(vmem_limit_bytes=48 << 20),
+        compiler_params=pltpu.CompilerParams(vmem_limit_bytes=60 << 20),
         cost_estimate=pl.CostEstimate(
             flops=10 * 10**9, bytes_accessed=20 * 10**6, transcendentals=0
         ),
         name="solve_and_score",
-    )(places, first, second, state, queries, new_rows, stored)
+    )(places, first, second, state, new_rows, scale_index, codes)
 
 
 def swap(value, mask, count):
@@ -478,13 +591,14 @@
     width = codes.shape[1]
     tiles = triangle(width)
     table = np.array(tiles, np.int32).T
-    all_queries = lax.all_gather(queries, "store", axis=0, tiled=True)
     core = me & 1
-    stored, new_rows, own, send, state = gram(
+    scale_index = scale_index.reshape(-1, LANES)
+    new_rows, own, send, state, asked = gram(
         core.astype(jnp.int32)[None],
         lengths,
         codes,
-        scale_index.reshape(-1, LANES),
+        scale_index,
+        queries,
         activations,
         out_grads,
         basis_in,
@@ -508,26 +622,36 @@
         arrived = [swap(message, (m + 1) << bit, count) for m, message in enumerate(messages)]
         base = base + at * own.shape[0]
     where = jnp.stack([base, jnp.zeros_like(base)]).astype(jnp.int32)
-    final, state = combine(where, table, own, state, arrived, 0, strip)
+    final, state = combine(where, table, own, state, arrived, 0, strip, [asked])
     for bit, members in reversed(groups):
         final = jnp.concatenate(
             [final] + [swap(final, m << bit, count) for m in range(1, members)], axis=0
         )
     other = swap(final, 1, count)
+    slot_bits = [count.bit_length() - 2]
+    for bit, members in groups:
+        for low in range(members // 2):
+            slot_bits.append(slot_bits[0] - (bit + members // 2 - 1) + low)
     places = []
     for slot in range(count):
+        mask = sum((slot >> position & 1) << b for b, position in enumerate(slot_bits))
+        owner = me ^ mask
+        place = (owner & 1) * (len(tiles) * LANES // 2)
         size = len(tiles) * LANES // 2
-        place = (core ^ (slot // (count // 2))) * size
-        left = slot % (count // 2)
-        weight = count // 2
         for bit, members in groups:
-            weight //= members
             size //= members
-            place = place + (((me >> bit) & (members - 1)) ^ (left // weight)) * size
-            left %= weight
+            place = place + ((owner >> bit) & (members - 1)) * size
         places.append(place)
     scores, new_scores = solve(
-        jnp.stack(places).astype(jnp.int32), final, other, state, all_queries, new_rows, stored
+        jnp.stack(places + [me]).astype(jnp.int32),
+        slot_bits,
+        final,
+        other,
+        state,
+        new_rows,
+        scale_index,
+        codes,
+        count * queries.shape[0],
     )
     return new_rows, scores, new_scores
 

time: 110 us -> 91 us (0.83)
  blocking collectives: 21.4 us -> 0 us
  Pallas kernels: 46 us -> 47.9 us
  waiting for transfers between devices: 20.6 us -> 22.1 us
    all_gather x1 -> x0, blocking collectives: 21.4 us -> none  [shards(): all_queries = lax.all_gather(queries, 'store', axis=0, tiled=True)]
    pallas_call x2, Pallas kernels: 41.9 us -> 43.8 us  [the longest x1 25.1 us: solve(): pl.pallas_call(functools.partial(solve_kernel, side, slot_bits), in_specs...]
    unnamed x21 -> x18, local copies, waits for them, and re-layouts: 5.84 us -> 4.31 us
    ppermute x10, waiting for transfers between devices: 20.6 us -> 22.1 us  [swap(): return lax.ppermute(value, 'store', [(i, i ^ mask) for i in range(count)])]
  transfers between devices with their start and end apart: 10 -> 10, of which waited for: 9 -> 9; matrix products, arithmetic and copies ran while one was open for 0% -> 1% of each run, Pallas kernels for 0% -> 0%
where the time goes in v2:
time: 91 us; the launch traced here: 90.7 us
  Pallas kernels  47.9 us (53%)
  waiting for transfers between devices  22.1 us (24%)
  starting transfers between devices  14.5 us (16%)
  local copies, waits for them, and re-layouts  5.04 us (6%)
  between operations  0.94 us (1%)
    pallas_call x1, Pallas kernels, solve(): pl.pallas_call(functools.partial(solve_kernel, side, slot_bits), in_specs...  25.1 us
    ppermute x10, waiting for transfers between devices, swap(): return lax.ppermute(value, 'store', [(i, i ^ mask) for i in range(count)])  22.1 us
    pallas_call x1, Pallas kernels, gram(): pl.pallas_call(functools.partial(gram_kernel, 0.75 / (count * rows), 0.25...  18.7 us
    ppermute x10, starting transfers between devices, swap(): return lax.ppermute(value, 'store', [(i, i ^ mask) for i in range(count)])  14.5 us
    unnamed x18, local copies, waits for them, and re-layouts  4.31 us
    pallas_call x3, Pallas kernels, combine(): pl.pallas_call(functools.partial(combine_kernel, members, len(arrived), w...  4.1 us
  transfers between devices with their start and end apart: 10, of which 9 were waited for; matrix products, arithmetic and copies ran while one was open for 1% of the time, Pallas kernels for 0%

profile of v2, /device:TPU:0, one launch (start us, length us, event | category | flops | bytes accessed | tf_op | source)
XLA Modules:
  0.0 90.7 jit_solution(14479762336541882677)
XLA Ops:
  0.6 0.0 copy-start.1
  0.6 18.7 %fisher_share.1 = (f32[8,1024]{1,0:T(8,128)}, f32[2304,128]{1,0:T(8,128)}, f32[2312,128]{1,0:T(8,128)}, f32[8,128]{1,0:T(8,128)}, s16[32,128]{1,0:T(8,128)(2,1)}) custom-call(s32[1]{0:T(128)} %bitcast.me_ref, s32[1,8]{1,0:T(1,128)} %lengths_ref.1, s32[32,128]{1,0:T(8,128)} %bitcast.23, bf16[4,1024]{1,0:T(4,128)(2,1)} %queries_ref.1, ...), custom_call_target="tpu_custom_call" | custom-call | flops 6000000000 | bytes 30000000 | tf_op jit(solution)/shard_map/fisher_share/pallas_call | solution.py:252
  19.3 0.0 copy-start.2
  19.4 0.5 collective-permute-start
  19.9 0.1 pad_add_fusion.2.refs_0_
  19.9 2.6 %collective-permute-done.refs_4_ = f32[2312,128]{1,0:T(8,128)S(1)} collective-permute-done((f32[2312,128]{1,0:T(8,128)}, f32[2312,128]{1,0:T(8,128)S(1)}, u32[]{:S(2)}, u32[]{:S(2)}) %collective-permute-start) | collective-permute-done | bytes 1183776 | tf_op jit(solution)/shard_map/ppermute | solution.py:585
  22.6 0.0 copy-done.1
  22.6 0.0 copy-start
  22.6 1.3 %copy-done = f32[2304,128]{1,0:T(8,128)S(1)} copy-done((f32[2304,128]{1,0:T(8,128)S(1)}, f32[2304,128]{1,0:T(8,128)}, u32[]{:S(2)}) %copy-start) | copy-done | bytes 1179672
  23.8 0.0 copy-start.3
  23.8 0.7 copy-done.3
  24.5 1.6 %sum_shares.3 = (f32[576,128]{1,0:T(8,128)S(1)}, s16[16,128]{1,0:T(8,128)(2,1)S(1)}, s16[592,128]{1,0:T(8,128)(2,1)S(1)}, s16[592,128]{1,0:T(8,128)(2,1)S(1)}, s16[592,128]{1,0:T(8,128)(2,1)S(1)}) custom-call(s32[2]{0:T(128)S(1)} %pad_add_fusion.2.refs_0_, s32[2,36]{1,0:T(2,128)S(1)} %copy-done.1, f32[2304,128]{1,0:T(8,128)S(1)} %copy-done, ...), custom_call_target="tpu_custom_call" | custom-call | flops 2949120 | bytes 2359296 | tf_op jit(solution)/shard_map/sum_shares/pallas_call | solution.py:399
  26.1 3.0 %collective-permute-start.1 = (s16[592,128]{1,0:T(8,128)(2,1)S(1)}, s16[592,128]{1,0:T(8,128)(2,1)S(1)}, u32[]{:S(2)}, u32[]{:S(2)}) collective-permute-start(s16[592,128]{1,0:T(8,128)(2,1)S(1)} %get-tuple-element.26), channel_id=1, source_target_pairs={{0,2},{1,3},{2,0},{3,1},{4,6},{5,7},{6,4},{7,5},{8,10},{9,11},{10,... | collective-permute-start | bytes 454664 | tf_op jit(solution)/shard_map/ppermute | solution.py:585
  29.1 1.6 %collective-permute-start.2 = (s16[592,128]{1,0:T(8,128)(2,1)S(1)}, s16[592,128]{1,0:T(8,128)(2,1)S(1)}, u32[]{:S(2)}, u32[]{:S(2)}) collective-permute-start(s16[592,128]{1,0:T(8,128)(2,1)S(1)} %get-tuple-element.27), channel_id=1, source_target_pairs={{0,4},{1,5},{2,6},{3,7},{4,0},{5,1},{6,2},{7,3},{8,12},{9,13},{10,... | collective-permute-start | bytes 454664 | tf_op jit(solution)/shard_map/ppermute | solution.py:585
  30.7 0.0 collective-permute-start.3
  30.7 0.1 pad_add_fusion.1.refs_0_
  30.7 2.6 %collective-permute-done.1.refs_4_ = s16[592,128]{1,0:T(8,128)(2,1)S(1)} collective-permute-done((s16[592,128]{1,0:T(8,128)(2,1)S(1)}, s16[592,128]{1,0:T(8,128)(2,1)S(1)}, u32[]{:S(2)}, u32[]{:S(2)}) %collective-permute-start.1) | collective-permute-done | bytes 151584 | tf_op jit(solution)/shard_map/ppermute | solution.py:585
  33.3 2.6 %collective-permute-done.2.refs_5_ = s16[592,128]{1,0:T(8,128)(2,1)S(1)} collective-permute-done((s16[592,128]{1,0:T(8,128)(2,1)S(1)}, s16[592,128]{1,0:T(8,128)(2,1)S(1)}, u32[]{:S(2)}, u32[]{:S(2)}) %collective-permute-start.2) | collective-permute-done | bytes 151584 | tf_op jit(solution)/shard_map/ppermute | solution.py:585
  35.9 1.9 %collective-permute-done.3.refs_6_ = s16[592,128]{1,0:T(8,128)(2,1)S(1)} collective-permute-done((s16[592,128]{1,0:T(8,128)(2,1)S(1)}, s16[592,128]{1,0:T(8,128)(2,1)S(1)}, u32[]{:S(2)}, u32[]{:S(2)}) %collective-permute-start.3) | collective-permute-done | bytes 151584 | tf_op jit(solution)/shard_map/ppermute | solution.py:585
  37.8 1.5 %sum_shares.4 = (f32[288,128]{1,0:T(8,128)S(1)}, s16[16,128]{1,0:T(8,128)(2,1)S(1)}, s16[304,128]{1,0:T(8,128)(2,1)S(1)}) custom-call(s32[2]{0:T(128)S(1)} %pad_add_fusion.1.refs_0_, s32[2,36]{1,0:T(2,128)S(1)} %copy-done.1, f32[576,128]{1,0:T(8,128)S(1)} %get-tuple-element.24.refs_2_, s16[16,128]{1,0:T(8,128)(2,1)S(1)} %get-tuple-element.25.refs_3_, ...), custom_call_target="tpu_custom_call" | custom-call | flops 737280 | bytes 589824 | tf_op jit(solution)/shard_map/sum_shares/pallas_call | solution.py:399
  39.3 2.8 %collective-permute-start.4 = (s16[304,128]{1,0:T(8,128)(2,1)S(1)}, s16[304,128]{1,0:T(8,128)(2,1)S(1)}, u32[]{:S(2)}, u32[]{:S(2)}) collective-permute-start(s16[304,128]{1,0:T(8,128)(2,1)S(1)} %get-tuple-element.31), channel_id=1, source_target_pairs={{0,8},{1,9},{2,10},{3,11},{4,12},{5,13},{6,14},{7,15},{8,0},{9,1},... | collective-permute-start | bytes 233480 | tf_op jit(solution)/shard_map/ppermute | solution.py:585
  42.1 0.1 pad_add_fusion.refs_0_
  42.2 2.5 %collective-permute-done.4.refs_4_ = s16[304,128]{1,0:T(8,128)(2,1)S(1)} collective-permute-done((s16[304,128]{1,0:T(8,128)(2,1)S(1)}, s16[304,128]{1,0:T(8,128)(2,1)S(1)}, u32[]{:S(2)}, u32[]{:S(2)}) %collective-permute-start.4) | collective-permute-done | bytes 77856 | tf_op jit(solution)/shard_map/ppermute | solution.py:585
  44.7 0.0 copy-done.2
  44.7 1.0 %sum_shares.5 = (s16[320,128]{1,0:T(8,128)(2,1)S(1)}, s16[16,128]{1,0:T(8,128)(2,1)S(1)}) custom-call(s32[2]{0:T(128)S(1)} %pad_add_fusion.refs_0_, s32[2,36]{1,0:T(2,128)S(1)} %copy-done.1, f32[288,128]{1,0:T(8,128)S(1)} %get-tuple-element.29.refs_2_, s16[16,128]{1,0:T(8,128)(2,1)S(1)} %get-tuple-element.30.refs_3_, ...), custom_call_target="tpu_custom_call" | custom-call | flops 368640 | bytes 294912 | tf_op jit(solution)/shard_map/sum_shares/pallas_call | solution.py:399
  45.7 0.0 copy-start.4
  45.7 2.9 %collective-permute-start.5 = (s16[320,128]{1,0:T(8,128)(2,1)S(1)}, s16[320,128]{1,0:T(8,128)(2,1)S(1)}, u32[]{:S(2)}, u32[]{:S(2)}) collective-permute-start(s16[320,128]{1,0:T(8,128)(2,1)S(1)} %get-tuple-element.33), channel_id=1, source_target_pairs={{0,8},{1,9},{2,10},{3,11},{4,12},{5,13},{6,14},{7,15},{8,0},{9,1},... | collective-permute-start | bytes 245768 | tf_op jit(solution)/shard_map/ppermute | solution.py:585
  48.6 2.5 %collective-permute-done.5 = s16[320,128]{1,0:T(8,128)(2,1)S(1)} collective-permute-done((s16[320,128]{1,0:T(8,128)(2,1)S(1)}, s16[320,128]{1,0:T(8,128)(2,1)S(1)}, u32[]{:S(2)}, u32[]{:S(2)}) %collective-permute-start.5) | collective-permute-done | bytes 81952 | tf_op jit(solution)/shard_map/ppermute | solution.py:585
  51.1 0.0 copy-done.4
  51.2 1.7 %collective-permute-start.6 = (s16[640,128]{1,0:T(8,128)(2,1)S(1)}, s16[640,128]{1,0:T(8,128)(2,1)S(1)}, u32[]{:S(2)}, u32[]{:S(2)}) collective-permute-start(s16[640,128]{1,0:T(8,128)(2,1)S(1)} %get-tuple-element.40), channel_id=1, source_target_pairs={{0,2},{1,3},{2,0},{3,1},{4,6},{5,7},{6,4},{7,5},{8,10},{9,11},{10,... | collective-permute-start | bytes 491528 | tf_op jit(solution)/shard_map/ppermute | solution.py:585
  52.9 2.0 %collective-permute-start.7 = (s16[640,128]{1,0:T(8,128)(2,1)S(1)}, s16[640,128]{1,0:T(8,128)(2,1)S(1)}, u32[]{:S(2)}, u32[]{:S(2)}) collective-permute-start(s16[640,128]{1,0:T(8,128)(2,1)S(1)} %get-tuple-element.40), channel_id=1, source_target_pairs={{0,4},{1,5},{2,6},{3,7},{4,0},{5,1},{6,2},{7,3},{8,12},{9,13},{10,... | collective-permute-start | bytes 491528 | tf_op jit(solution)/shard_map/ppermute | solution.py:585
  54.9 0.0 collective-permute-start.8
  54.9 3.4 %collective-permute-done.6 = s16[640,128]{1,0:T(8,128)(2,1)S(1)} collective-permute-done((s16[640,128]{1,0:T(8,128)(2,1)S(1)}, s16[640,128]{1,0:T(8,128)(2,1)S(1)}, u32[]{:S(2)}, u32[]{:S(2)}) %collective-permute-start.6) | collective-permute-done | bytes 163872 | tf_op jit(solution)/shard_map/ppermute | solution.py:585
  58.3 0.0 collective-permute-done.7
  58.3 2.7 %collective-permute-done.8 = s16[640,128]{1,0:T(8,128)(2,1)S(1)} collective-permute-done((s16[640,128]{1,0:T(8,128)(2,1)S(1)}, s16[640,128]{1,0:T(8,128)(2,1)S(1)}, u32[]{:S(2)}, u32[]{:S(2)}) %collective-permute-start.8) | collective-permute-done | bytes 163872 | tf_op jit(solution)/shard_map/ppermute | solution.py:585
  61.1 0.0 copy-start.5
  61.1 0.1 collective-permute-start.9
  61.4 0.7 stack.93.places_ref
  62.1 1.2 %collective-permute-done.9.second_ref = s16[2560,128]{1,0:T(8,128)(2,1)S(1)} collective-permute-done((s16[2560,128]{1,0:T(8,128)(2,1)S(1)}, s16[2560,128]{1,0:T(8,128)(2,1)S(1)}, u32[]{:S(2)}, u32[]{:S(2)}) %collective-permute-start.9) | collective-permute-done | bytes 655392 | tf_op jit(solution)/shard_map/ppermute | solution.py:585
  63.3 0.0 copy-start.6
  63.3 0.0 copy-done.5
  63.3 0.8 copy-done.6
  64.1 25.1 %solve_and_score.1 = (f32[64,4096]{1,0:T(8,128)}, f32[64,8]{1,0:T(8,128)}) custom-call(s32[17]{0:T(128)} %stack.93.places_ref, s16[2560,128]{1,0:T(8,128)(2,1)} %copy-done.5, s16[2560,128]{1,0:T(8,128)(2,1)} %copy-done.6, s16[16,128]{1,0:T(8,128)(2,1)} %copy-done.4, f32[8,1024]{1,0:T(8,128)} %get-tuple-element.37.new_rows_ref, s32[32,128]{1,0:T(8,128)} %bitcast.24, ...), custom_call_target="tpu_custom_call" | custom-call | flops 10000000000 | bytes 20000000 | tf_op jit(solution)/shard_map/solve_and_score/pallas_call | solution.py:557
  89.2 1.4 %copy.12 = f32[64,8]{0,1:T(8,128)} copy(f32[64,8]{1,0:T(8,128)} %get-tuple-element.39) | data formatting | bytes 4096
  (5 shorter events, 0.1 us)
Async XLA Ops:
  0.6 21.9 %copy-start.1 = (s32[2,36]{1,0:T(2,128)S(1)}, s32[2,36]{1,0:T(2,128)}, u32[]{:S(2)}) copy-start(s32[2,36]{1,0:T(2,128)} %constant.44.clone.refs_1_) | copy-start | bytes 868
  19.3 25.3 %copy-start.2 = (s16[32,128]{1,0:T(8,128)(2,1)S(1)}, s16[32,128]{1,0:T(8,128)(2,1)}, u32[]{:S(2)}) copy-start(s16[32,128]{1,0:T(8,128)(2,1)} %get-tuple-element.32.refs_5_) | copy-start | bytes 24580
  19.4 3.2 %collective-permute-start = (f32[2312,128]{1,0:T(8,128)}, f32[2312,128]{1,0:T(8,128)S(1)}, u32[]{:S(2)}, u32[]{:S(2)}) collective-permute-start(f32[2312,128]{1,0:T(8,128)} %get-tuple-element.23), channel_id=1, source_target_pairs={{0,1},{1,0},{2,3},{3,2},{4,5},{5,4},{6,7},{7,6},{8,9},{9,8},{10,11... | collective-permute-start | bytes 3551240 | tf_op jit(solution)/shard_map/ppermute | solution.py:585
  22.6 1.3 %copy-start = (f32[2304,128]{1,0:T(8,128)S(1)}, f32[2304,128]{1,0:T(8,128)}, u32[]{:S(2)}) copy-start(f32[2304,128]{1,0:T(8,128)} %get-tuple-element.21.refs_2_) | copy-start | bytes 3538948
  23.8 0.7 copy-start.3
  26.1 7.2 %collective-permute-start.1 = (s16[592,128]{1,0:T(8,128)(2,1)S(1)}, s16[592,128]{1,0:T(8,128)(2,1)S(1)}, u32[]{:S(2)}, u32[]{:S(2)}) collective-permute-start(s16[592,128]{1,0:T(8,128)(2,1)S(1)} %get-tuple-element.26), channel_id=1, source_target_pairs={{0,2},{1,3},{2,0},{3,1},{4,6},{5,7},{6,4},{7,5},{8,10},{9,11},{10,... | collective-permute-start | bytes 454664 | tf_op jit(solution)/shard_map/ppermute | solution.py:585
  29.1 6.8 %collective-permute-start.2 = (s16[592,128]{1,0:T(8,128)(2,1)S(1)}, s16[592,128]{1,0:T(8,128)(2,1)S(1)}, u32[]{:S(2)}, u32[]{:S(2)}) collective-permute-start(s16[592,128]{1,0:T(8,128)(2,1)S(1)} %get-tuple-element.27), channel_id=1, source_target_pairs={{0,4},{1,5},{2,6},{3,7},{4,0},{5,1},{6,2},{7,3},{8,12},{9,13},{10,... | collective-permute-start | bytes 454664 | tf_op jit(solution)/shard_map/ppermute | solution.py:585
  30.7 7.2 %collective-permute-start.3 = (s16[592,128]{1,0:T(8,128)(2,1)S(1)}, s16[592,128]{1,0:T(8,128)(2,1)S(1)}, u32[]{:S(2)}, u32[]{:S(2)}) collective-permute-start(s16[592,128]{1,0:T(8,128)(2,1)S(1)} %get-tuple-element.28), channel_id=1, source_target_pairs={{0,6},{1,7},{2,4},{3,5},{4,2},{5,3},{6,0},{7,1},{8,14},{9,15},{10,... | collective-permute-start | bytes 454664 | tf_op jit(solution)/shard_map/ppermute | solution.py:585
  39.3 5.4 %collective-permute-start.4 = (s16[304,128]{1,0:T(8,128)(2,1)S(1)}, s16[304,128]{1,0:T(8,128)(2,1)S(1)}, u32[]{:S(2)}, u32[]{:S(2)}) collective-permute-start(s16[304,128]{1,0:T(8,128)(2,1)S(1)} %get-tuple-element.31), channel_id=1, source_target_pairs={{0,8},{1,9},{2,10},{3,11},{4,12},{5,13},{6,14},{7,15},{8,0},{9,1},... | collective-permute-start | bytes 233480 | tf_op jit(solution)/shard_map/ppermute | solution.py:585
  45.7 5.4 %copy-start.4 = (s16[16,128]{1,0:T(8,128)(2,1)}, s16[16,128]{1,0:T(8,128)(2,1)S(1)}, u32[]{:S(2)}) copy-start(s16[16,128]{1,0:T(8,128)(2,1)S(1)} %get-tuple-element.34.state_ref) | copy-start | bytes 12292
  45.7 5.4 %collective-permute-start.5 = (s16[320,128]{1,0:T(8,128)(2,1)S(1)}, s16[320,128]{1,0:T(8,128)(2,1)S(1)}, u32[]{:S(2)}, u32[]{:S(2)}) collective-permute-start(s16[320,128]{1,0:T(8,128)(2,1)S(1)} %get-tuple-element.33), channel_id=1, source_target_pairs={{0,8},{1,9},{2,10},{3,11},{4,12},{5,13},{6,14},{7,15},{8,0},{9,1},... | collective-permute-start | bytes 245768 | tf_op jit(solution)/shard_map/ppermute | solution.py:585
  51.2 7.1 %collective-permute-start.6 = (s16[640,128]{1,0:T(8,128)(2,1)S(1)}, s16[640,128]{1,0:T(8,128)(2,1)S(1)}, u32[]{:S(2)}, u32[]{:S(2)}) collective-permute-start(s16[640,128]{1,0:T(8,128)(2,1)S(1)} %get-tuple-element.40), channel_id=1, source_target_pairs={{0,2},{1,3},{2,0},{3,1},{4,6},{5,7},{6,4},{7,5},{8,10},{9,11},{10,... | collective-permute-start | bytes 491528 | tf_op jit(solution)/shard_map/ppermute | solution.py:585
  52.9 5.4 %collective-permute-start.7 = (s16[640,128]{1,0:T(8,128)(2,1)S(1)}, s16[640,128]{1,0:T(8,128)(2,1)S(1)}, u32[]{:S(2)}, u32[]{:S(2)}) collective-permute-start(s16[640,128]{1,0:T(8,128)(2,1)S(1)} %get-tuple-element.40), channel_id=1, source_target_pairs={{0,4},{1,5},{2,6},{3,7},{4,0},{5,1},{6,2},{7,3},{8,12},{9,13},{10,... | collective-permute-start | bytes 491528 | tf_op jit(solution)/shard_map/ppermute | solution.py:585
  54.9 6.2 %collective-permute-start.8 = (s16[640,128]{1,0:T(8,128)(2,1)S(1)}, s16[640,128]{1,0:T(8,128)(2,1)S(1)}, u32[]{:S(2)}, u32[]{:S(2)}) collective-permute-start(s16[640,128]{1,0:T(8,128)(2,1)S(1)} %get-tuple-element.40), channel_id=1, source_target_pairs={{0,6},{1,7},{2,4},{3,5},{4,2},{5,3},{6,0},{7,1},{8,14},{9,15},{10,... | collective-permute-start | bytes 491528 | tf_op jit(solution)/shard_map/ppermute | solution.py:585
  61.1 2.2 %copy-start.5 = (s16[2560,128]{1,0:T(8,128)(2,1)}, s16[2560,128]{1,0:T(8,128)(2,1)S(1)}, u32[]{:S(2)}) copy-start(s16[2560,128]{1,0:T(8,128)(2,1)S(1)} %constant_dynamic-update-slice_fusion.2.first_ref) | copy-start | bytes 1966084
  61.1 2.2 %collective-permute-start.9 = (s16[2560,128]{1,0:T(8,128)(2,1)S(1)}, s16[2560,128]{1,0:T(8,128)(2,1)S(1)}, u32[]{:S(2)}, u32[]{:S(2)}) collective-permute-start(s16[2560,128]{1,0:T(8,128)(2,1)S(1)} %constant_dynamic-update-slice_fusion.2.first_ref), channel_id=1, source_target_pairs={{0,1},{1,0},{2,3},{3,2},{4,5},{5,4},{6,7},{7,6},{8,9},{9,8},{10,11... | collective-permute-start | bytes 1966088 | tf_op jit(solution)/shard_map/ppermute | solution.py:585
  63.3 0.9 copy-start.6

commit v3 on v2

--- a/solution.py
+++ b/solution.py
@@ -52,6 +52,10 @@
 
 def column_of(row):
     return jnp.broadcast_to(row, (LANES, LANES)).T
+
+
+def offset_of(me, levels):
+    return sum(((me >> bit) & (members - 1)) * size for bit, members, size in levels)
 
 
 def eye(size):
@@ -237,7 +241,7 @@
                         )
 
     for mine in range(2):
-        pl.when(me_ref[0] == mine)(functools.partial(finish, mine))
+        pl.when((me_ref[0] & 1) == mine)(functools.partial(finish, mine))
     send_ref[half * LANES :, :] = diag_ref[...]
 
 
@@ -272,7 +276,7 @@
             pltpu.SemaphoreType.DMA((8,)),
             pltpu.SemaphoreType.DMA((rows // chunk,)),
         ],
-        compiler_params=pltpu.CompilerParams(vmem_limit_bytes=60 << 20),
+        compiler_params=pltpu.CompilerParams(vmem_limit_bytes=57 << 20),
         cost_estimate=pl.CostEstimate(
             flops=6 * 10**9, bytes_accessed=30 * 10**6, transcendentals=0
         ),
@@ -324,40 +328,50 @@
     return columns[pl.ds(at, strip), :] * rows_ref[pl.ds(j, 1), :]
 
 
-def combine_kernel(members, coded, tiles, strip, *refs):
-    where_ref, table_ref, own_ref, state_ref = refs[:4]
-    arrived = refs[4 : 4 + coded]
-    refs = refs[4 + coded :]
-    if not members:
+def combine_kernel(levels, bit, members, has_own, coded, tiles, strip, *refs):
+    me_ref, table_ref = refs[:2]
+    refs = refs[2:]
+    if has_own:
+        (own_ref, state_ref), refs = refs[:2], refs[2:]
+    arrived, refs = refs[:coded], refs[coded:]
+    if members < 2:
         asked_ref, refs = refs[0], refs[1:]
-    out_own, out_state = refs[:2]
-    out_messages = refs[2 : 1 + members] if members > 1 else ()
-    refs = refs[max(1, members) + 1 :]
+    if members > 1:
+        (out_own, out_state), refs = refs[:2], refs[2:]
+        targets, refs = refs[: members - 1], refs[members - 1 :]
+    else:
+        (out_own, out_state), refs = refs[:2], refs[2:]
+        targets = [out_own]
     columns, rows_ref, inverse_columns, inverse_rows = refs
-    rows = own_ref.shape[0]
-    if coded == 1 and arrived[0].dtype == F32:
+    extra = asked_ref.shape[0] if members < 2 else 0
+    rows = (out_own.shape[0] - (PACK if members else 0) - extra) if members < 2 else (
+        own_ref.shape[0]
+    )
+    if not members and not has_own:
+        rows = out_own.shape[0] - 2 * extra
+    if arrived[0].dtype == F32:
         exps = exponents(state_ref[...] + arrived[0][rows:, :])
     else:
-        mine = read_exps(state_ref, 0, tiles)
         theirs = [read_exps(ref, rows, tiles) for ref in arrived]
-        level = [jnp.exp2(e / 32.0) for e in [mine] + theirs]
+        known = [read_exps(state_ref, 0, tiles)] if has_own else []
+        level = [jnp.exp2(e / 32.0) for e in known + theirs]
         while len(level) > 1:
             level = [a + b for a, b in zip(level[::2], level[1::2])]
         exps = exponents(level[0])
         for m, e in enumerate(theirs):
             fill_scales(e, 1.0 / CODE_MAX, columns.at[m], rows_ref.at[m])
     fill_scales(-exps, CODE_MAX, inverse_columns, inverse_rows)
-    base = where_ref[0]
-    mine_at = where_ref[1]
+    base = offset_of(me_ref[0], levels)
+    mine_at = (me_ref[0] >> bit) & (members - 1) if members > 1 else 0
     part = rows // max(members, 1)
     for m in range(max(members, 1)):
-        first = jnp.bitwise_xor(mine_at, m) * part
+        first = (mine_at ^ m) * part
 
         def body(s, _):
             inside = pl.multiple_of(s * strip, strip)
             at = pl.multiple_of(first + inside, strip)
             flat = base + at
-            value = own_ref[pl.ds(at, strip), :]
+            value = own_ref[pl.ds(at, strip), :] if has_own else 0.0
             for a, ref in enumerate(arrived):
                 got = ref[pl.ds(at, strip), :]
                 if got.dtype == F32:
@@ -371,34 +385,53 @@
                 out_own[pl.ds(inside, strip), :] = value
             else:
                 inverse = strip_scale(table_ref, inverse_columns, inverse_rows, flat, strip)
-                target = out_messages[m - 1] if members > 1 else out_own
+                target = targets[max(m - 1, 0)]
                 target[pl.ds(inside, strip), :] = encode(value, inverse)
             return 0
 
         lax.fori_loop(0, part // strip, body, 0, unroll=2)
     write_exps(out_state, 0, exps)
-    if not members:
+    if members:
+        for ref in targets:
+            write_exps(ref, part, exps)
+    if members == 1:
+        out_own[rows + PACK :, :] = asked_ref[...]
+    elif not members and has_own:
         out_own[rows:, :] = asked_ref[...]
-    for ref in out_messages:
-        write_exps(ref, part, exps)
-
-
-def combine(where, table, own, state, arrived, members, strip, asked=()):
-    rows = own.shape[0]
+    elif not members:
+        out_own[rows : rows + extra, :] = asked_ref[...]
+        out_own[rows + extra :, :] = arrived[1][rows + PACK :, :]
+
+
+def combine(me, table, levels, rows, own, arrived, bit, members, strip, asked):
     tiles = table.shape[1]
     width_tiles = int(round(((8 * tiles + 1) ** 0.5 - 1) / 2))
     width = width_tiles * LANES
     part = rows // max(members, 1)
-    outs = [
-        jax.ShapeDtypeStruct(
-            (part + sum(a.shape[0] for a in asked), LANES), F32 if members > 1 else jnp.int16
+    short = jnp.int16
+    state = jax.ShapeDtypeStruct((PACK, LANES), short)
+    if members > 1:
+        message = jax.ShapeDtypeStruct((part + PACK, LANES), short)
+        outs = [jax.ShapeDtypeStruct((part, LANES), F32), state] + [message] * (members - 1)
+        more = []
+    else:
+        extra = asked.shape[0]
+        size = rows + (PACK + extra if members else extra if own else 2 * extra)
+        outs = [jax.ShapeDtypeStruct((size, LANES), short), state]
+        more = [asked]
+    operands = [*own, *arrived, *more]
+    return pl.pallas_call(
+        functools.partial(
+            combine_kernel,
+            levels,
+            bit,
+            members,
+            bool(own),
+            len(arrived),
+            width_tiles,
+            strip,
         ),
-        jax.ShapeDtypeStruct((PACK, LANES), jnp.int16),
-    ]
-    outs += [jax.ShapeDtypeStruct((part + PACK, LANES), jnp.int16)] * max(members - 1, 0)
-    return pl.pallas_call(
-        functools.partial(combine_kernel, members, len(arrived), width_tiles, strip),
-        in_specs=[SMEM, SMEM] + [VMEM] * (2 + len(arrived) + len(asked)),
+        in_specs=[SMEM, SMEM] + [VMEM] * len(operands),
         out_specs=[VMEM] * len(outs),
         out_shape=outs,
         scratch_shapes=[
@@ -412,20 +445,23 @@
             flops=10 * rows * LANES, bytes_accessed=8 * rows * LANES, transcendentals=0
         ),
         name="sum_shares",
-    )(where, table, own, state, *arrived, *asked)
+    )(me, table, *operands)
 
 
 def solve_kernel(
     side,
+    levels,
+    masks,
+    count,
     slot_bits,
-    places_ref,
+    me_ref,
     first_ref,
     second_ref,
     state_ref,
     new_rows_ref,
     scale_ref,
     codes_hbm,
-    scores_ref,
+    scores_hbm,
     new_scores_ref,
     flat,
     system,
@@ -435,32 +471,43 @@
     columns,
     rows_ref,
     codes,
-    sem,
+    scores,
+    sems,
+    out_sems,
 ):
-    copy = pltpu.make_async_copy(codes_hbm, codes, sem)
-    copy.start()
+    lots = sems.shape[0]
+    lot = codes.shape[0] // lots
+
+    def fetch(c):
+        at = pl.ds(pl.multiple_of(c * lot, lot), lot)
+        return pltpu.make_async_copy(codes_hbm.at[at, :], codes.at[at, :], sems.at[c])
+
+    for c in range(lots):
+        fetch(c).start()
     queries, width = solved.shape
     tiles = width // LANES
-    pieces = places_ref.shape[0] - 1
+    pieces = len(masks)
     piece = flat.shape[0] // pieces
     pitch = 2 * first_ref.shape[0] // pieces
     asked = []
     for p in range(pieces):
         source = first_ref if p < pieces // 2 else second_ref
         at = p % (pieces // 2) * pitch
-        flat[pl.ds(pl.multiple_of(places_ref[p], PACK), piece), :] = source[at : at + piece, :]
+        place = pl.multiple_of(offset_of(me_ref[0] ^ masks[p], levels), PACK)
+        flat[pl.ds(place, piece), :] = source[at : at + piece, :]
         asked.append(source[at + piece : at + pitch, :].astype(jnp.int32))
     asked = float_of(jnp.concatenate(asked, axis=0)).astype(BF16)
-    each = queries // pieces
+    each = queries // count
+    packet = each * tiles
     order = (tiles * queries, asked.shape[0])
     to = lax.broadcasted_iota(jnp.int32, order, 0)
     source = lax.broadcasted_iota(jnp.int32, order, 1)
-    slot = lax.shift_right_logical(source, (pitch - piece).bit_length() - 1)
+    slot = lax.shift_right_logical(source, packet.bit_length() - 1)
     owner = jnp.zeros(order, jnp.int32)
     for bit, position in enumerate(slot_bits):
         owner = owner | ((lax.shift_right_logical(slot, position) & 1) << bit)
-    owner = owner ^ places_ref[pieces]
-    inside = source & (pitch - piece - 1)
+    owner = owner ^ me_ref[0]
+    inside = source & (packet - 1)
     target = (
         lax.shift_right_logical(inside, each.bit_length() - 1) * queries
         + owner * each
@@ -486,29 +533,49 @@
         system[at, at] += jnp.where(diagonal, damp, 0.0)
     blocks = width // side
     spans = [slice(b * side, (b + 1) * side) for b in range(blocks)]
-    bounds = [
-        jnp.max(jnp.sum(jnp.abs(system[span, span]), axis=0, keepdims=True)) for span in spans
-    ]
     unit = eye(side)
+    def await_lot(c):
+        @pl.when(c < lots)
+        def _():
+            fetch(c).wait()
+
+    def decode_lot(c):
+        start = pl.multiple_of(jnp.minimum(c, lots - 1) * lot, lot)
+        decode(codes, scale_ref, start, stored.at[pl.ds(start, lot), :])
+
+    taken = jnp.int32(0)
     for b, span in enumerate(spans):
         below = (b + 1) * side
-        bound = bounds[b]
+        block = system[span, span]
+        bound = jnp.max(jnp.sum(jnp.abs(block), axis=0, keepdims=True))
         low = damp / bound
-        pair[:side, :] = jnp.where(unit, 1.0 / bound, 0.0)
-        pair[side:, :] = system[span, span] * (1.0 / bound)
-
-        def more(low):
-            return low < 0.9995
-
-        def newton(low):
+
+        def step_from(value, low):
             gain = 4.0 / ((1.0 + low) * (1.0 + low))
+            return gain, jnp.where(unit, gain * (1.0 + low), 0.0) - gain * value
+
+        block = block * (1.0 / bound)
+        gain, step = step_from(block, low)
+        pair[:side, :] = step * (1.0 / bound)
+        pair[side:, :] = mm3(split2(block), split2(step))
+
+        def more(carry):
+            return carry[0] < 0.95
+
+        def newton(carry):
+            low, taken = carry
+            await_lot(taken)
             both = pair[...]
-            step = jnp.where(unit, gain * (1.0 + low), 0.0) - gain * both[side:, :]
+            gain, step = step_from(both[side:, :], low)
+            decode_lot(taken)
             pair[...] = mm3(split2(both), split2(step))
-            return gain * low
-
-        lax.while_loop(more, newton, low)
-        inverse = split2(pair[:side, :])
+            return gain * low, taken + 1
+
+        low, taken = lax.while_loop(more, newton, (gain * low, taken))
+        both = pair[...]
+        gain, step = step_from(both[side:, :], low)
+        low = gain * low
+        inverse = split2(mm3(split2(both[:side, :]), split2(step)) * (2.0 / (1.0 + low)))
         panel = system[below:, span]
         weights = split2(mm3(split2(panel), inverse))
         later = split2(panel[: width - below, :])
@@ -533,52 +600,62 @@
             )
         solved[:, spans[b]] = value
     high, low = split2(solved[...])
-    new_scores_ref[...] = mm3((high, low), split2(new_rows_ref[...]), NT)
+    new_scores_ref[...] = mm3(split2(new_rows_ref[...]), (high, low), NT)
     both = jnp.concatenate([high, low], axis=0)
-    copy.wait()
-    span = stored.shape[0]
-
-    def score(c, _):
-        at = pl.multiple_of(c * span, span)
-        decode(codes, scale_ref, at, stored)
-        value = mm(both, stored[...], NT)
-        scores_ref[:, pl.ds(at, span)] = value[:queries, :] + value[queries:, :]
+
+    def rest(c, _):
+        fetch(c).wait()
+        decode_lot(c)
         return 0
 
-    lax.fori_loop(0, codes.shape[0] // span, score, 0, unroll=2)
-
-
-def solve(places, slot_bits, first, second, state, new_rows, scale_index, codes, count):
+    lax.fori_loop(taken, lots, rest, 0)
+    span = scores.shape[1] // out_sems.shape[0]
+    copies = []
+    for c in range(out_sems.shape[0]):
+        at = slice(c * span, (c + 1) * span)
+        value = mm(both, stored[at, :], NT)
+        scores[:, at] = value[:queries, :] + value[queries:, :]
+        out = pltpu.make_async_copy(scores.at[:, at], scores_hbm.at[:, at], out_sems.at[c])
+        out.start()
+        copies.append(out)
+    for out in copies:
+        out.wait()
+
+
+def solve(
+    me, levels, masks, count, slot_bits, first, second, state, new_rows, scale_index, codes, asked
+):
     rows, width = codes.shape
     examples = new_rows.shape[0]
     side = 256
-    span = 512
     flat_rows = len(triangle(width)) * LANES
     return pl.pallas_call(
-        functools.partial(solve_kernel, side, slot_bits),
+        functools.partial(solve_kernel, side, levels, masks, count, slot_bits),
         in_specs=[SMEM] + [VMEM] * 5 + [ANY],
-        out_specs=[VMEM, VMEM],
+        out_specs=[ANY, VMEM],
         out_shape=[
-            jax.ShapeDtypeStruct((count, rows), F32),
-            jax.ShapeDtypeStruct((count, examples), F32),
+            jax.ShapeDtypeStruct((asked, rows), F32),
+            jax.ShapeDtypeStruct((examples, asked), F32),
         ],
         scratch_shapes=[
             pltpu.VMEM((flat_rows, LANES), jnp.int16),
-            pltpu.VMEM((width + count, width), F32),
+            pltpu.VMEM((width + asked, width), F32),
             pltpu.VMEM((2 * side, side), F32),
-            pltpu.VMEM((span, width), BF16),
-            pltpu.VMEM((count, width), F32),
+            pltpu.VMEM((rows, width), BF16),
+            pltpu.VMEM((asked, width), F32),
             pltpu.VMEM((width, LANES), F32),
             pltpu.VMEM((width // LANES, LANES), F32),
             pltpu.VMEM((rows, width), jnp.int32),
-            pltpu.SemaphoreType.DMA,
+            pltpu.VMEM((asked, rows), F32),
+            pltpu.SemaphoreType.DMA((rows // (2 * LANES),)),
+            pltpu.SemaphoreType.DMA((8,)),
         ],
-        compiler_params=pltpu.CompilerParams(vmem_limit_bytes=60 << 20),
+        compiler_params=pltpu.CompilerParams(vmem_limit_bytes=46 << 20),
         cost_estimate=pl.CostEstimate(
             flops=10 * 10**9, bytes_accessed=20 * 10**6, transcendentals=0
         ),
         name="solve_and_score",
-    )(places, first, second, state, new_rows, scale_index, codes)
+    )(me, first, second, state, new_rows, scale_index, codes)
 
 
 def swap(value, mask, count):
@@ -587,14 +664,13 @@
 
 def shards(activations, out_grads, basis_in, basis_out, lengths, codes, scale_index, queries):
     count = lax.axis_size("store")
-    me = lax.axis_index("store")
+    me = lax.axis_index("store").astype(jnp.int32)[None]
     width = codes.shape[1]
     tiles = triangle(width)
     table = np.array(tiles, np.int32).T
-    core = me & 1
     scale_index = scale_index.reshape(-1, LANES)
     new_rows, own, send, state, asked = gram(
-        core.astype(jnp.int32)[None],
+        me,
         lengths,
         codes,
         scale_index,
@@ -614,36 +690,40 @@
     piece = len(tiles) * LANES // count
     strip = int(np.gcd(np.gcd(piece, LANES), 64))
     arrived = [swap(send, 1, count)]
-    base = core * own.shape[0]
+    rows = own.shape[0]
+    levels = [(0, 2, rows)]
+    own = [own, state]
     for bit, members in groups:
-        at = (me >> bit) & (members - 1)
-        where = jnp.stack([base, at]).astype(jnp.int32)
-        own, state, *messages = combine(where, table, own, state, arrived, members, strip)
+        if members == 2:
+            coded, _ = combine(me, table, levels, rows, own, arrived, bit, 1, strip, asked)
+            own, arrived = [], [coded, swap(coded, 1 << bit, count)]
+            break
+        own = combine(me, table, levels, rows, own, arrived, bit, members, strip, asked)
+        own, messages = own[:2], own[2:]
         arrived = [swap(message, (m + 1) << bit, count) for m, message in enumerate(messages)]
-        base = base + at * own.shape[0]
-    where = jnp.stack([base, jnp.zeros_like(base)]).astype(jnp.int32)
-    final, state = combine(where, table, own, state, arrived, 0, strip, [asked])
+        rows //= members
+        levels = levels + [(bit, members, rows)]
+    final, state = combine(me, table, levels, rows, own, arrived, 0, 0, strip, asked)
     for bit, members in reversed(groups):
-        final = jnp.concatenate(
-            [final] + [swap(final, m << bit, count) for m in range(1, members)], axis=0
-        )
+        if members > 2:
+            final = jnp.concatenate(
+                [final] + [swap(final, m << bit, count) for m in range(1, members)], axis=0
+            )
     other = swap(final, 1, count)
     slot_bits = [count.bit_length() - 2]
     for bit, members in groups:
         for low in range(members // 2):
             slot_bits.append(slot_bits[0] - (bit + members // 2 - 1) + low)
-    places = []
-    for slot in range(count):
-        mask = sum((slot >> position & 1) << b for b, position in enumerate(slot_bits))
-        owner = me ^ mask
-        place = (owner & 1) * (len(tiles) * LANES // 2)
-        size = len(tiles) * LANES // 2
-        for bit, members in groups:
-            size //= members
-            place = place + ((owner >> bit) & (members - 1)) * size
-        places.append(place)
+    packets = len(tiles) * LANES // rows
+    masks = []
+    for slot in range(packets):
+        first = slot * (count // packets)
+        masks.append(sum((first >> position & 1) << b for b, position in enumerate(slot_bits)))
     scores, new_scores = solve(
-        jnp.stack(places + [me]).astype(jnp.int32),
+        me,
+        levels,
+        masks,
+        count,
         slot_bits,
         final,
         other,
@@ -653,7 +733,7 @@
         codes,
         count * queries.shape[0],
     )
-    return new_rows, scores, new_scores
+    return new_rows, scores, new_scores.T
 
 
 def solution(mesh):

time: 91 us -> 84.5 us (0.929)
  Pallas kernels: 47.9 us -> 44.6 us
  waiting for transfers between devices: 22.1 us -> 25.3 us
  starting transfers between devices: 14.5 us -> 11.4 us
  local copies, waits for them, and re-layouts: 5.04 us -> 2.05 us
    pallas_call x4, Pallas kernels: 29.2 us -> 25.9 us  [the longest x1 20.9 us: solve(): pl.pallas_call(functools.partial(solve_kernel, side, levels, masks, count...]
    ppermute x10 -> x9, waiting for transfers between devices: 22.1 us -> 25.3 us  [swap(): return lax.ppermute(value, 'store', [(i, i ^ mask) for i in range(count)])]
    ppermute x10 -> x9, starting transfers between devices: 14.5 us -> 11.4 us  [swap(): return lax.ppermute(value, 'store', [(i, i ^ mask) for i in range(count)])]
    unnamed x18 -> x15, local copies, waits for them, and re-layouts: 4.31 us -> 2.03 us
  transfers between devices with their start and end apart: 10 -> 9, of which waited for: 9 -> 8; matrix products, arithmetic and copies ran while one was open for 1% -> 0% of each run, Pallas kernels for 0% -> 0%
where the time goes in v3:
time: 84.5 us; the launch traced here: 84.3 us
  Pallas kernels  44.6 us (53%)
  waiting for transfers between devices  25.3 us (30%)
  starting transfers between devices  11.4 us (13%)
  local copies, waits for them, and re-layouts  2.05 us (2%)
  between operations  0.88 us (1%)
    ppermute x9, waiting for transfers between devices, swap(): return lax.ppermute(value, 'store', [(i, i ^ mask) for i in range(count)])  25.3 us
    pallas_call x1, Pallas kernels, solve(): pl.pallas_call(functools.partial(solve_kernel, side, levels, masks, count...  20.9 us
    pallas_call x1, Pallas kernels, gram(): pl.pallas_call(functools.partial(gram_kernel, 0.75 / (count * rows), 0.25...  18.7 us
    ppermute x9, starting transfers between devices, swap(): return lax.ppermute(value, 'store', [(i, i ^ mask) for i in range(count)])  11.4 us
    pallas_call x3, Pallas kernels, combine(): pl.pallas_call(functools.partial(combine_kernel, levels, bit, members, bo...  4.99 us
    unnamed x15, local copies, waits for them, and re-layouts  2.03 us
  transfers between devices with their start and end apart: 9, of which 8 were waited for; matrix products, arithmetic and copies ran while one was open for 0% of the time, Pallas kernels for 0%

profile of v3, /device:TPU:0, one launch (start us, length us, event | category | flops | bytes accessed | tf_op | source)
XLA Modules:
  0.0 84.3 jit_solution(13624804650839017881)
XLA Ops:
  0.6 0.0 copy-start.3
  0.6 18.7 %fisher_share.1 = (f32[8,1024]{1,0:T(8,128)}, f32[2304,128]{1,0:T(8,128)}, f32[2312,128]{1,0:T(8,128)}, f32[8,128]{1,0:T(8,128)}, s16[32,128]{1,0:T(8,128)(2,1)}) custom-call(s32[1]{0:T(128)} %bitcast.me_ref.refs_0_, s32[1,8]{1,0:T(1,128)} %lengths_ref.1, s32[32,128]{1,0:T(8,128)} %bitcast.3, bf16[4,1024]{1,0:T(4,128)(2,1)} %queries_ref.1, ...), custom_call_target="tpu_custom_call" | custom-call | flops 6000000000 | bytes 30000000 | tf_op jit(solution)/shard_map/fisher_share/pallas_call | solution.py:256
  19.4 0.5 collective-permute-start
  19.9 2.7 %collective-permute-done.refs_4_ = f32[2312,128]{1,0:T(8,128)S(1)} collective-permute-done((f32[2312,128]{1,0:T(8,128)}, f32[2312,128]{1,0:T(8,128)S(1)}, u32[]{:S(2)}, u32[]{:S(2)}) %collective-permute-start) | collective-permute-done | bytes 1183776 | tf_op jit(solution)/shard_map/ppermute | solution.py:662
  22.6 0.0 copy-done.3
  22.6 0.0 copy-start
  22.6 1.3 %copy-done = f32[2304,128]{1,0:T(8,128)S(1)} copy-done((f32[2304,128]{1,0:T(8,128)S(1)}, f32[2304,128]{1,0:T(8,128)}, u32[]{:S(2)}) %copy-start) | copy-done | bytes 1179672
  23.8 0.0 copy-start.4
  23.8 0.7 copy-done.4
  24.5 0.0 copy-start.1
  24.5 0.0 copy-start.2
  24.5 0.0 copy-start.5
  24.5 1.6 %sum_shares.3 = (f32[576,128]{1,0:T(8,128)S(1)}, s16[16,128]{1,0:T(8,128)(2,1)S(1)}, s16[592,128]{1,0:T(8,128)(2,1)S(1)}, s16[592,128]{1,0:T(8,128)(2,1)S(1)}, s16[592,128]{1,0:T(8,128)(2,1)S(1)}) custom-call(s32[1]{0:T(128)} %bitcast.me_ref.refs_0_, s32[2,36]{1,0:T(2,128)S(1)} %copy-done.3, f32[2304,128]{1,0:T(8,128)S(1)} %copy-done, ...), custom_call_target="tpu_custom_call" | custom-call | flops 2949120 | bytes 2359296 | tf_op jit(solution)/shard_map/sum_shares/pallas_call | solution.py:423
  26.1 3.0 %collective-permute-start.1 = (s16[592,128]{1,0:T(8,128)(2,1)S(1)}, s16[592,128]{1,0:T(8,128)(2,1)S(1)}, u32[]{:S(2)}, u32[]{:S(2)}) collective-permute-start(s16[592,128]{1,0:T(8,128)(2,1)S(1)} %get-tuple-element.24), channel_id=1, source_target_pairs={{0,2},{1,3},{2,0},{3,1},{4,6},{5,7},{6,4},{7,5},{8,10},{9,11},{10,... | collective-permute-start | bytes 454664 | tf_op jit(solution)/shard_map/ppermute | solution.py:662
  29.1 1.6 %collective-permute-start.2 = (s16[592,128]{1,0:T(8,128)(2,1)S(1)}, s16[592,128]{1,0:T(8,128)(2,1)S(1)}, u32[]{:S(2)}, u32[]{:S(2)}) collective-permute-start(s16[592,128]{1,0:T(8,128)(2,1)S(1)} %get-tuple-element.25), channel_id=1, source_target_pairs={{0,4},{1,5},{2,6},{3,7},{4,0},{5,1},{6,2},{7,3},{8,12},{9,13},{10,... | collective-permute-start | bytes 454664 | tf_op jit(solution)/shard_map/ppermute | solution.py:662
  30.7 0.0 collective-permute-start.3
  30.7 2.7 %collective-permute-done.1.refs_4_ = s16[592,128]{1,0:T(8,128)(2,1)S(1)} collective-permute-done((s16[592,128]{1,0:T(8,128)(2,1)S(1)}, s16[592,128]{1,0:T(8,128)(2,1)S(1)}, u32[]{:S(2)}, u32[]{:S(2)}) %collective-permute-start.1) | collective-permute-done | bytes 151584 | tf_op jit(solution)/shard_map/ppermute | solution.py:662
  33.3 2.6 %collective-permute-done.2.refs_5_ = s16[592,128]{1,0:T(8,128)(2,1)S(1)} collective-permute-done((s16[592,128]{1,0:T(8,128)(2,1)S(1)}, s16[592,128]{1,0:T(8,128)(2,1)S(1)}, u32[]{:S(2)}, u32[]{:S(2)}) %collective-permute-start.2) | collective-permute-done | bytes 151584 | tf_op jit(solution)/shard_map/ppermute | solution.py:662
  35.9 1.9 %collective-permute-done.3.refs_6_ = s16[592,128]{1,0:T(8,128)(2,1)S(1)} collective-permute-done((s16[592,128]{1,0:T(8,128)(2,1)S(1)}, s16[592,128]{1,0:T(8,128)(2,1)S(1)}, u32[]{:S(2)}, u32[]{:S(2)}) %collective-permute-start.3) | collective-permute-done | bytes 151584 | tf_op jit(solution)/shard_map/ppermute | solution.py:662
  37.8 0.0 copy-done.1
  37.8 2.1 %sum_shares.4 = (s16[624,128]{1,0:T(8,128)(2,1)S(1)}, s16[16,128]{1,0:T(8,128)(2,1)}) custom-call(s32[1]{0:T(128)} %bitcast.me_ref.refs_0_, s32[2,36]{1,0:T(2,128)S(1)} %copy-done.3, f32[576,128]{1,0:T(8,128)S(1)} %get-tuple-element.22.refs_2_, s16[16,128]{1,0:T(8,128)(2,1)S(1)} %get-tuple-element.23.refs_3_, ...), custom_call_target="tpu_custom_call" | custom-call | flops 737280 | bytes 589824 | tf_op jit(solution)/shard_map/sum_shares/pallas_call | solution.py:423
  39.9 2.7 %collective-permute-start.4 = (s16[624,128]{1,0:T(8,128)(2,1)S(1)}, s16[624,128]{1,0:T(8,128)(2,1)S(1)}, u32[]{:S(2)}, u32[]{:S(2)}) collective-permute-start(s16[624,128]{1,0:T(8,128)(2,1)S(1)} %get-tuple-element.28.refs_2_), channel_id=1, source_target_pairs={{0,8},{1,9},{2,10},{3,11},{4,12},{5,13},{6,14},{7,15},{8,0},{9,1},... | collective-permute-start | bytes 479240 | tf_op jit(solution)/shard_map/ppermute | solution.py:662
  42.6 6.9 %collective-permute-done.4.refs_3_ = s16[624,128]{1,0:T(8,128)(2,1)S(1)} collective-permute-done((s16[624,128]{1,0:T(8,128)(2,1)S(1)}, s16[624,128]{1,0:T(8,128)(2,1)S(1)}, u32[]{:S(2)}, u32[]{:S(2)}) %collective-permute-start.4) | collective-permute-done | bytes 159776 | tf_op jit(solution)/shard_map/ppermute | solution.py:662
  49.6 1.3 %sum_shares.5 = (s16[640,128]{1,0:T(8,128)(2,1)S(1)}, s16[16,128]{1,0:T(8,128)(2,1)S(1)}) custom-call(s32[1]{0:T(128)} %bitcast.me_ref.refs_0_, s32[2,36]{1,0:T(2,128)S(1)} %copy-done.3, s16[624,128]{1,0:T(8,128)(2,1)S(1)} %get-tuple-element.28.refs_2_, s16[624,128]{1,0:T(8,128)(2,1)S(1)} %collective-permute-done.4.refs_3_, s16[32,128]{1,0:T(8,128)(2,1)S(1)} %copy-done.1), custom_call_target="tpu_custom_call" | custom-call | flops 737280 | bytes 589824 | tf_op jit(solution)/shard_map/sum_shares/pallas_call | solution.py:423
  50.9 1.4 %collective-permute-start.5 = (s16[640,128]{1,0:T(8,128)(2,1)S(1)}, s16[640,128]{1,0:T(8,128)(2,1)S(1)}, u32[]{:S(2)}, u32[]{:S(2)}) collective-permute-start(s16[640,128]{1,0:T(8,128)(2,1)S(1)} %get-tuple-element.29), channel_id=1, source_target_pairs={{0,2},{1,3},{2,0},{3,1},{4,6},{5,7},{6,4},{7,5},{8,10},{9,11},{10,... | collective-permute-start | bytes 491528 | tf_op jit(solution)/shard_map/ppermute | solution.py:662
  52.3 0.7 collective-permute-start.7
  53.0 1.4 %collective-permute-start.6 = (s16[640,128]{1,0:T(8,128)(2,1)S(1)}, s16[640,128]{1,0:T(8,128)(2,1)S(1)}, u32[]{:S(2)}, u32[]{:S(2)}) collective-permute-start(s16[640,128]{1,0:T(8,128)(2,1)S(1)} %get-tuple-element.29), channel_id=1, source_target_pairs={{0,4},{1,5},{2,6},{3,7},{4,0},{5,1},{6,2},{7,3},{8,12},{9,13},{10,... | collective-permute-start | bytes 491528 | tf_op jit(solution)/shard_map/ppermute | solution.py:662
  54.5 4.6 %collective-permute-done.5 = s16[640,128]{1,0:T(8,128)(2,1)S(1)} collective-permute-done((s16[640,128]{1,0:T(8,128)(2,1)S(1)}, s16[640,128]{1,0:T(8,128)(2,1)S(1)}, u32[]{:S(2)}, u32[]{:S(2)}) %collective-permute-start.5) | collective-permute-done | bytes 163872 | tf_op jit(solution)/shard_map/ppermute | solution.py:662
  59.1 1.8 %collective-permute-done.6 = s16[640,128]{1,0:T(8,128)(2,1)S(1)} collective-permute-done((s16[640,128]{1,0:T(8,128)(2,1)S(1)}, s16[640,128]{1,0:T(8,128)(2,1)S(1)}, u32[]{:S(2)}, u32[]{:S(2)}) %collective-permute-start.6) | collective-permute-done | bytes 163872 | tf_op jit(solution)/shard_map/ppermute | solution.py:662
  60.9 0.0 collective-permute-done.7
  61.0 0.1 collective-permute-start.8
  61.1 2.1 %collective-permute-done.8.second_ref = s16[2560,128]{1,0:T(8,128)(2,1)S(1)} collective-permute-done((s16[2560,128]{1,0:T(8,128)(2,1)S(1)}, s16[2560,128]{1,0:T(8,128)(2,1)S(1)}, u32[]{:S(2)}, u32[]{:S(2)}) %collective-permute-start.8) | collective-permute-done | bytes 655392 | tf_op jit(solution)/shard_map/ppermute | solution.py:662
  63.2 0.0 copy-done.2
  63.2 0.0 copy-done.5
  63.2 20.9 %solve_and_score.1 = (f32[64,4096]{1,0:T(8,128)}, f32[8,64]{1,0:T(8,128)}) custom-call(s32[1]{0:T(128)} %bitcast.me_ref.refs_0_, s16[2560,128]{1,0:T(8,128)(2,1)S(1)} %constant_dynamic-update-slice_fusion.first_ref, s16[2560,128]{1,0:T(8,128)(2,1)S(1)} %collective-permute-done.8.second_ref, s16[16,128]{1,0:T(8,128)(2,1)S(1)} %get-tuple-element.30.state_ref, ...), custom_call_target="tpu_custom_call" | custom-call | flops 10000000000 | bytes 20000000 | tf_op jit(solution)/shard_map/solve_and_score/pallas_call | solution.py:632
  (4 shorter events, 0.1 us)
Async XLA Ops:
  0.6 21.9 %copy-start.3 = (s32[2,36]{1,0:T(2,128)S(1)}, s32[2,36]{1,0:T(2,128)}, u32[]{:S(2)}) copy-start(s32[2,36]{1,0:T(2,128)} %constant.6.clone.refs_1_) | copy-start | bytes 868
  19.4 3.2 %collective-permute-start = (f32[2312,128]{1,0:T(8,128)}, f32[2312,128]{1,0:T(8,128)S(1)}, u32[]{:S(2)}, u32[]{:S(2)}) collective-permute-start(f32[2312,128]{1,0:T(8,128)} %get-tuple-element.21), channel_id=1, source_target_pairs={{0,1},{1,0},{2,3},{3,2},{4,5},{5,4},{6,7},{7,6},{8,9},{9,8},{10,11... | collective-permute-start | bytes 3551240 | tf_op jit(solution)/shard_map/ppermute | solution.py:662
  22.6 1.3 %copy-start = (f32[2304,128]{1,0:T(8,128)S(1)}, f32[2304,128]{1,0:T(8,128)}, u32[]{:S(2)}) copy-start(f32[2304,128]{1,0:T(8,128)} %get-tuple-element.19.refs_2_) | copy-start | bytes 3538948
  23.8 0.7 copy-start.4
  24.5 13.3 %copy-start.1 = (s16[32,128]{1,0:T(8,128)(2,1)S(1)}, s16[32,128]{1,0:T(8,128)(2,1)}, u32[]{:S(2)}) copy-start(s16[32,128]{1,0:T(8,128)(2,1)} %get-tuple-element.27.refs_7_.refs_4_) | copy-start | bytes 24580
  24.5 38.6 %copy-start.2 = (s32[4096]{0:T(1024)S(1)}, s32[4096]{0:T(1024)}, u32[]{:S(2)}) copy-start(s32[4096]{0:T(1024)} %param.15) | copy-start | bytes 49156
  24.5 38.6 %copy-start.5 = (f32[8,1024]{1,0:T(8,128)S(1)}, f32[8,1024]{1,0:T(8,128)}, u32[]{:S(2)}) copy-start(f32[8,1024]{1,0:T(8,128)} %get-tuple-element.15.new_rows_ref) | copy-start | bytes 98308
  26.1 7.2 %collective-permute-start.1 = (s16[592,128]{1,0:T(8,128)(2,1)S(1)}, s16[592,128]{1,0:T(8,128)(2,1)S(1)}, u32[]{:S(2)}, u32[]{:S(2)}) collective-permute-start(s16[592,128]{1,0:T(8,128)(2,1)S(1)} %get-tuple-element.24), channel_id=1, source_target_pairs={{0,2},{1,3},{2,0},{3,1},{4,6},{5,7},{6,4},{7,5},{8,10},{9,11},{10,... | collective-permute-start | bytes 454664 | tf_op jit(solution)/shard_map/ppermute | solution.py:662
  29.1 6.8 %collective-permute-start.2 = (s16[592,128]{1,0:T(8,128)(2,1)S(1)}, s16[592,128]{1,0:T(8,128)(2,1)S(1)}, u32[]{:S(2)}, u32[]{:S(2)}) collective-permute-start(s16[592,128]{1,0:T(8,128)(2,1)S(1)} %get-tuple-element.25), channel_id=1, source_target_pairs={{0,4},{1,5},{2,6},{3,7},{4,0},{5,1},{6,2},{7,3},{8,12},{9,13},{10,... | collective-permute-start | bytes 454664 | tf_op jit(solution)/shard_map/ppermute | solution.py:662
  30.7 7.2 %collective-permute-start.3 = (s16[592,128]{1,0:T(8,128)(2,1)S(1)}, s16[592,128]{1,0:T(8,128)(2,1)S(1)}, u32[]{:S(2)}, u32[]{:S(2)}) collective-permute-start(s16[592,128]{1,0:T(8,128)(2,1)S(1)} %get-tuple-element.26), channel_id=1, source_target_pairs={{0,6},{1,7},{2,4},{3,5},{4,2},{5,3},{6,0},{7,1},{8,14},{9,15},{10,... | collective-permute-start | bytes 454664 | tf_op jit(solution)/shard_map/ppermute | solution.py:662
  39.9 9.6 %collective-permute-start.4 = (s16[624,128]{1,0:T(8,128)(2,1)S(1)}, s16[624,128]{1,0:T(8,128)(2,1)S(1)}, u32[]{:S(2)}, u32[]{:S(2)}) collective-permute-start(s16[624,128]{1,0:T(8,128)(2,1)S(1)} %get-tuple-element.28.refs_2_), channel_id=1, source_target_pairs={{0,8},{1,9},{2,10},{3,11},{4,12},{5,13},{6,14},{7,15},{8,0},{9,1},... | collective-permute-start | bytes 479240 | tf_op jit(solution)/shard_map/ppermute | solution.py:662
  50.9 8.2 %collective-permute-start.5 = (s16[640,128]{1,0:T(8,128)(2,1)S(1)}, s16[640,128]{1,0:T(8,128)(2,1)S(1)}, u32[]{:S(2)}, u32[]{:S(2)}) collective-permute-start(s16[640,128]{1,0:T(8,128)(2,1)S(1)} %get-tuple-element.29), channel_id=1, source_target_pairs={{0,2},{1,3},{2,0},{3,1},{4,6},{5,7},{6,4},{7,5},{8,10},{9,11},{10,... | collective-permute-start | bytes 491528 | tf_op jit(solution)/shard_map/ppermute | solution.py:662
  52.3 8.6 %collective-permute-start.7 = (s16[640,128]{1,0:T(8,128)(2,1)S(1)}, s16[640,128]{1,0:T(8,128)(2,1)S(1)}, u32[]{:S(2)}, u32[]{:S(2)}) collective-permute-start(s16[640,128]{1,0:T(8,128)(2,1)S(1)} %get-tuple-element.29), channel_id=1, source_target_pairs={{0,6},{1,7},{2,4},{3,5},{4,2},{5,3},{6,0},{7,1},{8,14},{9,15},{10,... | collective-permute-start | bytes 491528 | tf_op jit(solution)/shard_map/ppermute | solution.py:662
  53.0 7.9 %collective-permute-start.6 = (s16[640,128]{1,0:T(8,128)(2,1)S(1)}, s16[640,128]{1,0:T(8,128)(2,1)S(1)}, u32[]{:S(2)}, u32[]{:S(2)}) collective-permute-start(s16[640,128]{1,0:T(8,128)(2,1)S(1)} %get-tuple-element.29), channel_id=1, source_target_pairs={{0,4},{1,5},{2,6},{3,7},{4,0},{5,1},{6,2},{7,3},{8,12},{9,13},{10,... | collective-permute-start | bytes 491528 | tf_op jit(solution)/shard_map/ppermute | solution.py:662
  61.0 2.2 %collective-permute-start.8 = (s16[2560,128]{1,0:T(8,128)(2,1)S(1)}, s16[2560,128]{1,0:T(8,128)(2,1)S(1)}, u32[]{:S(2)}, u32[]{:S(2)}) collective-permute-start(s16[2560,128]{1,0:T(8,128)(2,1)S(1)} %constant_dynamic-update-slice_fusion.first_ref), channel_id=1, source_target_pairs={{0,1},{1,0},{2,3},{3,2},{4,5},{5,4},{6,7},{7,6},{8,9},{9,8},{10,11... | collective-permute-start | bytes 1966088 | tf_op jit(solution)/shard_map/ppermute | solution.py:662

commit v4 on v3

--- a/solution.py
+++ b/solution.py
@@ -43,6 +43,15 @@
     return mm(left_high, right_high, dims) + (
         mm(left_high, right_low, dims) + mm(left_low, right_high, dims)
     )
+
+
+def mm6(left, right, dims=NN):
+    left_high, left_mid, left_low = left
+    right_high, right_mid, right_low = right
+    small = mm(left_high, right_low, dims) + mm(left_low, right_high, dims)
+    small = small + mm(left_mid, right_mid, dims)
+    middle = mm(left_high, right_mid, dims) + mm(left_mid, right_high, dims)
+    return mm(left_high, right_high, dims) + (middle + small)
 
 
 def triangle(width):
@@ -328,6 +337,38 @@
     return columns[pl.ds(at, strip), :] * rows_ref[pl.ds(j, 1), :]
 
 
+def fetch_kernel(first_hbm, second_hbm, first_ref, second_ref, sems):
+    copies = [pltpu.make_async_copy(second_hbm, second_ref, sems.at[0])]
+    rows = first_ref.shape[0] // 4
+    for c in range(4):
+        at = pl.ds(c * rows, rows)
+        copies.append(
+            pltpu.make_async_copy(first_hbm.at[at, :], first_ref.at[at, :], sems.at[c + 1])
+        )
+    for copy in copies:
+        copy.start()
+    for copy in copies:
+        copy.wait()
+
+
+def fetch_rows(first, second):
+    return pl.pallas_call(
+        fetch_kernel,
+        in_specs=[ANY, ANY],
+        out_specs=[VMEM, VMEM],
+        out_shape=[
+            jax.ShapeDtypeStruct(first.shape, first.dtype),
+            jax.ShapeDtypeStruct(second.shape, second.dtype),
+        ],
+        scratch_shapes=[pltpu.SemaphoreType.DMA((5,))],
+        compiler_params=pltpu.CompilerParams(vmem_limit_bytes=32 << 20),
+        cost_estimate=pl.CostEstimate(
+            flops=0, bytes_accessed=2 * first.size * first.dtype.itemsize, transcendentals=0
+        ),
+        name="fetch_rows",
+    )(first, second)
+
+
 def combine_kernel(levels, bit, members, has_own, coded, tiles, strip, *refs):
     me_ref, table_ref = refs[:2]
     refs = refs[2:]
@@ -472,6 +513,7 @@
     rows_ref,
     codes,
     scores,
+    taken_ref,
     sems,
     out_sems,
 ):
@@ -543,62 +585,72 @@
         start = pl.multiple_of(jnp.minimum(c, lots - 1) * lot, lot)
         decode(codes, scale_ref, start, stored.at[pl.ds(start, lot), :])
 
-    taken = jnp.int32(0)
-    for b, span in enumerate(spans):
-        below = (b + 1) * side
-        block = system[span, span]
-        bound = jnp.max(jnp.sum(jnp.abs(block), axis=0, keepdims=True))
-        low = damp / bound
-
-        def step_from(value, low):
-            gain = 4.0 / ((1.0 + low) * (1.0 + low))
-            return gain, jnp.where(unit, gain * (1.0 + low), 0.0) - gain * value
-
-        block = block * (1.0 / bound)
-        gain, step = step_from(block, low)
-        pair[:side, :] = step * (1.0 / bound)
-        pair[side:, :] = mm3(split2(block), split2(step))
-
-        def more(carry):
-            return carry[0] < 0.95
-
-        def newton(carry):
-            low, taken = carry
-            await_lot(taken)
+    def eliminate(split, mul, refine):
+        for b, span in enumerate(spans):
+            below = (b + 1) * side
+            block = system[span, span]
+            bound = jnp.max(jnp.sum(jnp.abs(block), axis=0, keepdims=True))
+            low = damp / bound
+
+            def step_from(value, low):
+                gain = 4.0 / ((1.0 + low) * (1.0 + low))
+                return gain, jnp.where(unit, gain * (1.0 + low), 0.0) - gain * value
+
+            block = block * (1.0 / bound)
+            gain, step = step_from(block, low)
+            pair[:side, :] = step * (1.0 / bound)
+            pair[side:, :] = mul(split(block), split(step))
+
+            def more(low):
+                return low < 0.95
+
+            def newton(low):
+                taken = taken_ref[0]
+                taken_ref[0] = taken + 1
+                await_lot(taken)
+                both = pair[...]
+                gain, step = step_from(both[side:, :], low)
+                decode_lot(taken)
+                pair[...] = mul(split(both), split(step))
+                return gain * low
+
+            low = lax.while_loop(more, newton, gain * low)
             both = pair[...]
             gain, step = step_from(both[side:, :], low)
-            decode_lot(taken)
-            pair[...] = mm3(split2(both), split2(step))
-            return gain * low, taken + 1
-
-        low, taken = lax.while_loop(more, newton, (gain * low, taken))
-        both = pair[...]
-        gain, step = step_from(both[side:, :], low)
-        low = gain * low
-        inverse = split2(mm3(split2(both[:side, :]), split2(step)) * (2.0 / (1.0 + low)))
-        panel = system[below:, span]
-        weights = split2(mm3(split2(panel), inverse))
-        later = split2(panel[: width - below, :])
-        system[below:, span] = weights[0].astype(F32) + weights[1].astype(F32)
-        for c in range(b + 1, blocks):
-            from_row = c * side - below
-            update = mm3(
-                (weights[0][from_row:, :], weights[1][from_row:, :]),
-                (
-                    later[0][from_row : from_row + side, :],
-                    later[1][from_row : from_row + side, :],
-                ),
-                NT,
-            )
-            system[c * side :, spans[c]] -= update
-    for b in reversed(range(blocks)):
-        below = (b + 1) * side
-        value = system[width:, spans[b]]
-        if below < width:
-            value = value - mm3(
-                split2(solved[:, below:]), split2(system[below:width, spans[b]])
-            )
-        solved[:, spans[b]] = value
+            low = gain * low
+            inverse = mul(split(both[:side, :]), split(step)) * (2.0 / (1.0 + low))
+            if refine:
+                left = jnp.where(unit, 1.0, 0.0) - mul(split(system[span, span]), split(inverse))
+                inverse = inverse + mul(split(inverse), split(left))
+            inverse = split(inverse)
+            panel = system[below:, span]
+            weights = split(mul(split(panel), inverse))
+            later = split(panel[: width - below, :])
+            system[below:, span] = sum(part.astype(F32) for part in weights)
+            for c in range(b + 1, blocks):
+                from_row = c * side - below
+                update = mul(
+                    tuple(part[from_row:, :] for part in weights),
+                    tuple(part[from_row : from_row + side, :] for part in later),
+                    NT,
+                )
+                system[c * side :, spans[c]] -= update
+        for b in reversed(range(blocks)):
+            below = (b + 1) * side
+            value = system[width:, spans[b]]
+            if below < width:
+                value = value - mul(
+                    split(solved[:, below:]), split(system[below:width, spans[b]])
+                )
+            solved[:, spans[b]] = value
+
+    taken_ref[0] = 0
+    ratio = jnp.float32(0.0)
+    for span in spans:
+        sums = jnp.sum(jnp.abs(system[span, span]), axis=0, keepdims=True)
+        ratio = jnp.maximum(ratio, jnp.max(sums) / damp)
+    pl.when(ratio <= 800.0)(lambda: eliminate(split2, mm3, False))
+    pl.when(jnp.logical_not(ratio <= 800.0))(lambda: eliminate(split3, mm6, True))
     high, low = split2(solved[...])
     new_scores_ref[...] = mm3(split2(new_rows_ref[...]), (high, low), NT)
     both = jnp.concatenate([high, low], axis=0)
@@ -608,7 +660,7 @@
         decode_lot(c)
         return 0
 
-    lax.fori_loop(taken, lots, rest, 0)
+    lax.fori_loop(jnp.minimum(taken_ref[0], lots), lots, rest, 0)
     span = scores.shape[1] // out_sems.shape[0]
     copies = []
     for c in range(out_sems.shape[0]):
@@ -647,6 +699,7 @@
             pltpu.VMEM((width // LANES, LANES), F32),
             pltpu.VMEM((rows, width), jnp.int32),
             pltpu.VMEM((asked, rows), F32),
+            pltpu.SMEM((1,), jnp.int32),
             pltpu.SemaphoreType.DMA((rows // (2 * LANES),)),
             pltpu.SemaphoreType.DMA((8,)),
         ],
@@ -692,7 +745,7 @@
     arrived = [swap(send, 1, count)]
     rows = own.shape[0]
     levels = [(0, 2, rows)]
-    own = [own, state]
+    own = fetch_rows(own, state)
     for bit, members in groups:
         if members == 2:
             coded, _ = combine(me, table, levels, rows, own, arrived, bit, 1, strip, asked)

time: 84.5 us -> 83.4 us (0.987)
  waiting for transfers between devices: 25.3 us -> 23 us
  Pallas kernels: 44.6 us -> 45.7 us
    ppermute x9, waiting for transfers between devices: 25.3 us -> 23 us  [swap(): return lax.ppermute(value, 'store', [(i, i ^ mask) for i in range(count)])]
where the time goes in v4:
time: 83.4 us; the launch traced here: 83.1 us
  Pallas kernels  45.7 us (55%)
  waiting for transfers between devices  23 us (28%)
  starting transfers between devices  11.4 us (14%)
  local copies, waits for them, and re-layouts  2.05 us (2%)
  between operations  0.9 us (1%)
    ppermute x9, waiting for transfers between devices, swap(): return lax.ppermute(value, 'store', [(i, i ^ mask) for i in range(count)])  23 us
    pallas_call x1, Pallas kernels, solve(): pl.pallas_call(functools.partial(solve_kernel, side, levels, masks, count...  21.8 us
    pallas_call x1, Pallas kernels, gram(): pl.pallas_call(functools.partial(gram_kernel, 0.75 / (count * rows), 0.25...  18.7 us
    ppermute x9, starting transfers between devices, swap(): return lax.ppermute(value, 'store', [(i, i ^ mask) for i in range(count)])  11.4 us
    pallas_call x3, Pallas kernels, combine(): pl.pallas_call(functools.partial(combine_kernel, levels, bit, members, bo...  4.99 us
    unnamed x15, local copies, waits for them, and re-layouts  2.03 us
  transfers between devices with their start and end apart: 9, of which 8 were waited for; matrix products, arithmetic and copies ran while one was open for 0% of the time, Pallas kernels for 0%

profile of v4, /device:TPU:0, one launch (start us, length us, event | category | flops | bytes accessed | tf_op | source)
XLA Modules:
  0.0 83.1 jit_solution(9532181638737593766)
XLA Ops:
  0.6 18.7 %fisher_share.1 = (f32[8,1024]{1,0:T(8,128)}, f32[2304,128]{1,0:T(8,128)}, f32[2312,128]{1,0:T(8,128)}, f32[8,128]{1,0:T(8,128)}, s16[32,128]{1,0:T(8,128)(2,1)}) custom-call(s32[1]{0:T(128)} %bitcast.me_ref.refs_0_, s32[1,8]{1,0:T(1,128)} %lengths_ref.1, s32[32,128]{1,0:T(8,128)} %bitcast.3, bf16[4,1024]{1,0:T(4,128)(2,1)} %queries_ref.1, ...), custom_call_target="tpu_custom_call" | custom-call | flops 6000000000 | bytes 30000000 | tf_op jit(solution)/shard_map/fisher_share/pallas_call | solution.py:265
  19.3 0.0 copy-start.3
  19.4 0.5 collective-permute-start
  19.9 0.0 copy-start
  19.9 1.3 %copy-done = f32[2304,128]{1,0:T(8,128)S(1)} copy-done((f32[2304,128]{1,0:T(8,128)S(1)}, f32[2304,128]{1,0:T(8,128)}, u32[]{:S(2)}) %copy-start) | copy-done | bytes 1179672
  21.1 0.0 copy-start.4
  21.1 0.7 copy-done.4
  21.8 0.3 fetch_rows.1
  22.1 0.4 collective-permute-done.refs_4_
  22.6 0.0 copy-done.3
  22.6 0.0 copy-start.1
  22.6 1.6 %sum_shares.3 = (f32[576,128]{1,0:T(8,128)S(1)}, s16[16,128]{1,0:T(8,128)(2,1)S(1)}, s16[592,128]{1,0:T(8,128)(2,1)S(1)}, s16[592,128]{1,0:T(8,128)(2,1)S(1)}, s16[592,128]{1,0:T(8,128)(2,1)S(1)}) custom-call(s32[1]{0:T(128)} %bitcast.me_ref.refs_0_, s32[2,36]{1,0:T(2,128)S(1)} %copy-done.3, f32[2304,128]{1,0:T(8,128)S(1)} %get-tuple-element.23.refs_2_, ...), custom_call_target="tpu_custom_call" | custom-call | flops 2949120 | bytes 2359296 | tf_op jit(solution)/shard_map/sum_shares/pallas_call | solution.py:464
  24.2 3.0 %collective-permute-start.1 = (s16[592,128]{1,0:T(8,128)(2,1)S(1)}, s16[592,128]{1,0:T(8,128)(2,1)S(1)}, u32[]{:S(2)}, u32[]{:S(2)}) collective-permute-start(s16[592,128]{1,0:T(8,128)(2,1)S(1)} %get-tuple-element.28), channel_id=1, source_target_pairs={{0,2},{1,3},{2,0},{3,1},{4,6},{5,7},{6,4},{7,5},{8,10},{9,11},{10,... | collective-permute-start | bytes 454664 | tf_op jit(solution)/shard_map/ppermute | solution.py:715
  27.1 1.6 %collective-permute-start.2 = (s16[592,128]{1,0:T(8,128)(2,1)S(1)}, s16[592,128]{1,0:T(8,128)(2,1)S(1)}, u32[]{:S(2)}, u32[]{:S(2)}) collective-permute-start(s16[592,128]{1,0:T(8,128)(2,1)S(1)} %get-tuple-element.29), channel_id=1, source_target_pairs={{0,4},{1,5},{2,6},{3,7},{4,0},{5,1},{6,2},{7,3},{8,12},{9,13},{10,... | collective-permute-start | bytes 454664 | tf_op jit(solution)/shard_map/ppermute | solution.py:715
  28.7 0.0 collective-permute-start.3
  28.7 2.7 %collective-permute-done.1.refs_4_ = s16[592,128]{1,0:T(8,128)(2,1)S(1)} collective-permute-done((s16[592,128]{1,0:T(8,128)(2,1)S(1)}, s16[592,128]{1,0:T(8,128)(2,1)S(1)}, u32[]{:S(2)}, u32[]{:S(2)}) %collective-permute-start.1) | collective-permute-done | bytes 151584 | tf_op jit(solution)/shard_map/ppermute | solution.py:715
  31.4 2.6 %collective-permute-done.2.refs_5_ = s16[592,128]{1,0:T(8,128)(2,1)S(1)} collective-permute-done((s16[592,128]{1,0:T(8,128)(2,1)S(1)}, s16[592,128]{1,0:T(8,128)(2,1)S(1)}, u32[]{:S(2)}, u32[]{:S(2)}) %collective-permute-start.2) | collective-permute-done | bytes 151584 | tf_op jit(solution)/shard_map/ppermute | solution.py:715
  33.9 1.9 %collective-permute-done.3.refs_6_ = s16[592,128]{1,0:T(8,128)(2,1)S(1)} collective-permute-done((s16[592,128]{1,0:T(8,128)(2,1)S(1)}, s16[592,128]{1,0:T(8,128)(2,1)S(1)}, u32[]{:S(2)}, u32[]{:S(2)}) %collective-permute-start.3) | collective-permute-done | bytes 151584 | tf_op jit(solution)/shard_map/ppermute | solution.py:715
  35.9 0.0 copy-done.1
  35.9 0.0 copy-start.2
  35.9 0.0 copy-start.5
  35.9 2.1 %sum_shares.4 = (s16[624,128]{1,0:T(8,128)(2,1)S(1)}, s16[16,128]{1,0:T(8,128)(2,1)}) custom-call(s32[1]{0:T(128)} %bitcast.me_ref.refs_0_, s32[2,36]{1,0:T(2,128)S(1)} %copy-done.3, f32[576,128]{1,0:T(8,128)S(1)} %get-tuple-element.26.refs_2_, s16[16,128]{1,0:T(8,128)(2,1)S(1)} %get-tuple-element.27.refs_3_, ...), custom_call_target="tpu_custom_call" | custom-call | flops 737280 | bytes 589824 | tf_op jit(solution)/shard_map/sum_shares/pallas_call | solution.py:464
  37.9 2.7 %collective-permute-start.4 = (s16[624,128]{1,0:T(8,128)(2,1)S(1)}, s16[624,128]{1,0:T(8,128)(2,1)S(1)}, u32[]{:S(2)}, u32[]{:S(2)}) collective-permute-start(s16[624,128]{1,0:T(8,128)(2,1)S(1)} %get-tuple-element.32.refs_2_), channel_id=1, source_target_pairs={{0,8},{1,9},{2,10},{3,11},{4,12},{5,13},{6,14},{7,15},{8,0},{9,1},... | collective-permute-start | bytes 479240 | tf_op jit(solution)/shard_map/ppermute | solution.py:715
  40.7 6.9 %collective-permute-done.4.refs_3_ = s16[624,128]{1,0:T(8,128)(2,1)S(1)} collective-permute-done((s16[624,128]{1,0:T(8,128)(2,1)S(1)}, s16[624,128]{1,0:T(8,128)(2,1)S(1)}, u32[]{:S(2)}, u32[]{:S(2)}) %collective-permute-start.4) | collective-permute-done | bytes 159776 | tf_op jit(solution)/shard_map/ppermute | solution.py:715
  47.6 1.3 %sum_shares.5 = (s16[640,128]{1,0:T(8,128)(2,1)S(1)}, s16[16,128]{1,0:T(8,128)(2,1)S(1)}) custom-call(s32[1]{0:T(128)} %bitcast.me_ref.refs_0_, s32[2,36]{1,0:T(2,128)S(1)} %copy-done.3, s16[624,128]{1,0:T(8,128)(2,1)S(1)} %get-tuple-element.32.refs_2_, s16[624,128]{1,0:T(8,128)(2,1)S(1)} %collective-permute-done.4.refs_3_, s16[32,128]{1,0:T(8,128)(2,1)S(1)} %copy-done.1), custom_call_target="tpu_custom_call" | custom-call | flops 737280 | bytes 589824 | tf_op jit(solution)/shard_map/sum_shares/pallas_call | solution.py:464
  48.9 1.4 %collective-permute-start.5 = (s16[640,128]{1,0:T(8,128)(2,1)S(1)}, s16[640,128]{1,0:T(8,128)(2,1)S(1)}, u32[]{:S(2)}, u32[]{:S(2)}) collective-permute-start(s16[640,128]{1,0:T(8,128)(2,1)S(1)} %get-tuple-element.33), channel_id=1, source_target_pairs={{0,2},{1,3},{2,0},{3,1},{4,6},{5,7},{6,4},{7,5},{8,10},{9,11},{10,... | collective-permute-start | bytes 491528 | tf_op jit(solution)/shard_map/ppermute | solution.py:715
  50.3 0.7 collective-permute-start.7
  51.1 1.4 %collective-permute-start.6 = (s16[640,128]{1,0:T(8,128)(2,1)S(1)}, s16[640,128]{1,0:T(8,128)(2,1)S(1)}, u32[]{:S(2)}, u32[]{:S(2)}) collective-permute-start(s16[640,128]{1,0:T(8,128)(2,1)S(1)} %get-tuple-element.33), channel_id=1, source_target_pairs={{0,4},{1,5},{2,6},{3,7},{4,0},{5,1},{6,2},{7,3},{8,12},{9,13},{10,... | collective-permute-start | bytes 491528 | tf_op jit(solution)/shard_map/ppermute | solution.py:715
  52.5 4.6 %collective-permute-done.5 = s16[640,128]{1,0:T(8,128)(2,1)S(1)} collective-permute-done((s16[640,128]{1,0:T(8,128)(2,1)S(1)}, s16[640,128]{1,0:T(8,128)(2,1)S(1)}, u32[]{:S(2)}, u32[]{:S(2)}) %collective-permute-start.5) | collective-permute-done | bytes 163872 | tf_op jit(solution)/shard_map/ppermute | solution.py:715
  57.1 1.8 %collective-permute-done.6 = s16[640,128]{1,0:T(8,128)(2,1)S(1)} collective-permute-done((s16[640,128]{1,0:T(8,128)(2,1)S(1)}, s16[640,128]{1,0:T(8,128)(2,1)S(1)}, u32[]{:S(2)}, u32[]{:S(2)}) %collective-permute-start.6) | collective-permute-done | bytes 163872 | tf_op jit(solution)/shard_map/ppermute | solution.py:715
  59.0 0.0 collective-permute-done.7
  59.0 0.1 collective-permute-start.8
  59.1 2.1 %collective-permute-done.8.second_ref = s16[2560,128]{1,0:T(8,128)(2,1)S(1)} collective-permute-done((s16[2560,128]{1,0:T(8,128)(2,1)S(1)}, s16[2560,128]{1,0:T(8,128)(2,1)S(1)}, u32[]{:S(2)}, u32[]{:S(2)}) %collective-permute-start.8) | collective-permute-done | bytes 655392 | tf_op jit(solution)/shard_map/ppermute | solution.py:715
  61.2 0.0 copy-done.2
  61.2 0.0 copy-done.5
  61.2 21.8 %solve_and_score.1 = (f32[64,4096]{1,0:T(8,128)}, f32[8,64]{1,0:T(8,128)}) custom-call(s32[1]{0:T(128)} %bitcast.me_ref.refs_0_, s16[2560,128]{1,0:T(8,128)(2,1)S(1)} %constant_dynamic-update-slice_fusion.first_ref, s16[2560,128]{1,0:T(8,128)(2,1)S(1)} %collective-permute-done.8.second_ref, s16[16,128]{1,0:T(8,128)(2,1)S(1)} %get-tuple-element.34.state_ref, ...), custom_call_target="tpu_custom_call" | custom-call | flops 10000000000 | bytes 20000000 | tf_op jit(solution)/shard_map/solve_and_score/pallas_call | solution.py:684
  (4 shorter events, 0.1 us)
Async XLA Ops:
  19.3 3.2 %copy-start.3 = (s32[2,36]{1,0:T(2,128)S(1)}, s32[2,36]{1,0:T(2,128)}, u32[]{:S(2)}) copy-start(s32[2,36]{1,0:T(2,128)} %constant.6.clone.refs_1_) | copy-start | bytes 868
  19.4 3.2 %collective-permute-start = (f32[2312,128]{1,0:T(8,128)}, f32[2312,128]{1,0:T(8,128)S(1)}, u32[]{:S(2)}, u32[]{:S(2)}) collective-permute-start(f32[2312,128]{1,0:T(8,128)} %get-tuple-element.25), channel_id=1, source_target_pairs={{0,1},{1,0},{2,3},{3,2},{4,5},{5,4},{6,7},{7,6},{8,9},{9,8},{10,11... | collective-permute-start | bytes 3551240 | tf_op jit(solution)/shard_map/ppermute | solution.py:715
  19.9 1.3 %copy-start = (f32[2304,128]{1,0:T(8,128)S(1)}, f32[2304,128]{1,0:T(8,128)}, u32[]{:S(2)}) copy-start(f32[2304,128]{1,0:T(8,128)} %get-tuple-element.21.first_hbm) | copy-start | bytes 3538948
  21.1 0.7 copy-start.4
  22.6 13.3 %copy-start.1 = (s16[32,128]{1,0:T(8,128)(2,1)S(1)}, s16[32,128]{1,0:T(8,128)(2,1)}, u32[]{:S(2)}) copy-start(s16[32,128]{1,0:T(8,128)(2,1)} %get-tuple-element.31.refs_7_.refs_4_) | copy-start | bytes 24580
  24.2 7.2 %collective-permute-start.1 = (s16[592,128]{1,0:T(8,128)(2,1)S(1)}, s16[592,128]{1,0:T(8,128)(2,1)S(1)}, u32[]{:S(2)}, u32[]{:S(2)}) collective-permute-start(s16[592,128]{1,0:T(8,128)(2,1)S(1)} %get-tuple-element.28), channel_id=1, source_target_pairs={{0,2},{1,3},{2,0},{3,1},{4,6},{5,7},{6,4},{7,5},{8,10},{9,11},{10,... | collective-permute-start | bytes 454664 | tf_op jit(solution)/shard_map/ppermute | solution.py:715
  27.1 6.8 %collective-permute-start.2 = (s16[592,128]{1,0:T(8,128)(2,1)S(1)}, s16[592,128]{1,0:T(8,128)(2,1)S(1)}, u32[]{:S(2)}, u32[]{:S(2)}) collective-permute-start(s16[592,128]{1,0:T(8,128)(2,1)S(1)} %get-tuple-element.29), channel_id=1, source_target_pairs={{0,4},{1,5},{2,6},{3,7},{4,0},{5,1},{6,2},{7,3},{8,12},{9,13},{10,... | collective-permute-start | bytes 454664 | tf_op jit(solution)/shard_map/ppermute | solution.py:715
  28.7 7.2 %collective-permute-start.3 = (s16[592,128]{1,0:T(8,128)(2,1)S(1)}, s16[592,128]{1,0:T(8,128)(2,1)S(1)}, u32[]{:S(2)}, u32[]{:S(2)}) collective-permute-start(s16[592,128]{1,0:T(8,128)(2,1)S(1)} %get-tuple-element.30), channel_id=1, source_target_pairs={{0,6},{1,7},{2,4},{3,5},{4,2},{5,3},{6,0},{7,1},{8,14},{9,15},{10,... | collective-permute-start | bytes 454664 | tf_op jit(solution)/shard_map/ppermute | solution.py:715
  35.9 25.3 %copy-start.2 = (s32[4096]{0:T(1024)S(1)}, s32[4096]{0:T(1024)}, u32[]{:S(2)}) copy-start(s32[4096]{0:T(1024)} %param.15) | copy-start | bytes 49156
  35.9 25.3 %copy-start.5 = (f32[8,1024]{1,0:T(8,128)S(1)}, f32[8,1024]{1,0:T(8,128)}, u32[]{:S(2)}) copy-start(f32[8,1024]{1,0:T(8,128)} %get-tuple-element.17.new_rows_ref) | copy-start | bytes 98308
  37.9 9.6 %collective-permute-start.4 = (s16[624,128]{1,0:T(8,128)(2,1)S(1)}, s16[624,128]{1,0:T(8,128)(2,1)S(1)}, u32[]{:S(2)}, u32[]{:S(2)}) collective-permute-start(s16[624,128]{1,0:T(8,128)(2,1)S(1)} %get-tuple-element.32.refs_2_), channel_id=1, source_target_pairs={{0,8},{1,9},{2,10},{3,11},{4,12},{5,13},{6,14},{7,15},{8,0},{9,1},... | collective-permute-start | bytes 479240 | tf_op jit(solution)/shard_map/ppermute | solution.py:715
  48.9 8.2 %collective-permute-start.5 = (s16[640,128]{1,0:T(8,128)(2,1)S(1)}, s16[640,128]{1,0:T(8,128)(2,1)S(1)}, u32[]{:S(2)}, u32[]{:S(2)}) collective-permute-start(s16[640,128]{1,0:T(8,128)(2,1)S(1)} %get-tuple-element.33), channel_id=1, source_target_pairs={{0,2},{1,3},{2,0},{3,1},{4,6},{5,7},{6,4},{7,5},{8,10},{9,11},{10,... | collective-permute-start | bytes 491528 | tf_op jit(solution)/shard_map/ppermute | solution.py:715
  50.3 8.6 %collective-permute-start.7 = (s16[640,128]{1,0:T(8,128)(2,1)S(1)}, s16[640,128]{1,0:T(8,128)(2,1)S(1)}, u32[]{:S(2)}, u32[]{:S(2)}) collective-permute-start(s16[640,128]{1,0:T(8,128)(2,1)S(1)} %get-tuple-element.33), channel_id=1, source_target_pairs={{0,6},{1,7},{2,4},{3,5},{4,2},{5,3},{6,0},{7,1},{8,14},{9,15},{10,... | collective-permute-start | bytes 491528 | tf_op jit(solution)/shard_map/ppermute | solution.py:715
  51.1 7.9 %collective-permute-start.6 = (s16[640,128]{1,0:T(8,128)(2,1)S(1)}, s16[640,128]{1,0:T(8,128)(2,1)S(1)}, u32[]{:S(2)}, u32[]{:S(2)}) collective-permute-start(s16[640,128]{1,0:T(8,128)(2,1)S(1)} %get-tuple-element.33), channel_id=1, source_target_pairs={{0,4},{1,5},{2,6},{3,7},{4,0},{5,1},{6,2},{7,3},{8,12},{9,13},{10,... | collective-permute-start | bytes 491528 | tf_op jit(solution)/shard_map/ppermute | solution.py:715
  59.0 2.2 %collective-permute-start.8 = (s16[2560,128]{1,0:T(8,128)(2,1)S(1)}, s16[2560,128]{1,0:T(8,128)(2,1)S(1)}, u32[]{:S(2)}, u32[]{:S(2)}) collective-permute-start(s16[2560,128]{1,0:T(8,128)(2,1)S(1)} %constant_dynamic-update-slice_fusion.first_ref), channel_id=1, source_target_pairs={{0,1},{1,0},{2,3},{3,2},{4,5},{5,4},{6,7},{7,6},{8,9},{9,8},{10,11... | collective-permute-start | bytes 1966088 | tf_op jit(solution)/shard_map/ppermute | solution.py:715

commit v5 on v4

--- a/solution.py
+++ b/solution.py
@@ -430,7 +430,7 @@
                 target[pl.ds(inside, strip), :] = encode(value, inverse)
             return 0
 
-        lax.fori_loop(0, part // strip, body, 0, unroll=2)
+        lax.fori_loop(0, part // strip, body, 0, unroll=9)
     write_exps(out_state, 0, exps)
     if members:
         for ref in targets:
@@ -740,7 +740,9 @@
         members = 4 if 1 << (bit + 1) < count else 2
         groups.append((bit, members))
         bit += 2
-    piece = len(tiles) * LANES // count
+    piece = len(tiles) * LANES // 2
+    for _, members in groups:
+        piece //= members if members > 2 else 1
     strip = int(np.gcd(np.gcd(piece, LANES), 64))
     arrived = [swap(send, 1, count)]
     rows = own.shape[0]

time: 83.4 us -> 81.8 us (0.981)
  Pallas kernels: 45.7 us -> 44.3 us
    pallas_call x3, Pallas kernels: 4.99 us -> 4 us  [combine(): pl.pallas_call(functools.partial(combine_kernel, levels, bit, members, bo...]
where the time goes in v5:
time: 81.8 us; the launch traced here: 81.7 us
  Pallas kernels  44.3 us (54%)
  waiting for transfers between devices  23 us (28%)
  starting transfers between devices  11.4 us (14%)
  local copies, waits for them, and re-layouts  2.05 us (3%)
  between operations  0.9 us (1%)
    ppermute x9, waiting for transfers between devices, swap(): return lax.ppermute(value, 'store', [(i, i ^ mask) for i in range(count)])  23 us
    pallas_call x1, Pallas kernels, solve(): pl.pallas_call(functools.partial(solve_kernel, side, levels, masks, count...  21.3 us
    pallas_call x1, Pallas kernels, gram(): pl.pallas_call(functools.partial(gram_kernel, 0.75 / (count * rows), 0.25...  18.7 us
    ppermute x9, starting transfers between devices, swap(): return lax.ppermute(value, 'store', [(i, i ^ mask) for i in range(count)])  11.4 us
    pallas_call x3, Pallas kernels, combine(): pl.pallas_call(functools.partial(combine_kernel, levels, bit, members, bo...  4 us
    unnamed x15, local copies, waits for them, and re-layouts  2.03 us
  transfers between devices with their start and end apart: 9, of which 8 were waited for; matrix products, arithmetic and copies ran while one was open for 0% of the time, Pallas kernels for 0%

profile of v5, /device:TPU:0, one launch (start us, length us, event | category | flops | bytes accessed | tf_op | source)
XLA Modules:
  0.0 81.7 jit_solution(7784754384977708640)
XLA Ops:
  0.6 18.7 %fisher_share.1 = (f32[8,1024]{1,0:T(8,128)}, f32[2304,128]{1,0:T(8,128)}, f32[2312,128]{1,0:T(8,128)}, f32[8,128]{1,0:T(8,128)}, s16[32,128]{1,0:T(8,128)(2,1)}) custom-call(s32[1]{0:T(128)} %bitcast.me_ref.refs_0_, s32[1,8]{1,0:T(1,128)} %lengths_ref.1, s32[32,128]{1,0:T(8,128)} %bitcast.3, bf16[4,1024]{1,0:T(4,128)(2,1)} %queries_ref.1, ...), custom_call_target="tpu_custom_call" | custom-call | flops 6000000000 | bytes 30000000 | tf_op jit(solution)/shard_map/fisher_share/pallas_call | solution.py:265
  19.3 0.0 copy-start.3
  19.4 0.5 collective-permute-start
  19.9 0.0 copy-start
  19.9 1.3 %copy-done = f32[2304,128]{1,0:T(8,128)S(1)} copy-done((f32[2304,128]{1,0:T(8,128)S(1)}, f32[2304,128]{1,0:T(8,128)}, u32[]{:S(2)}) %copy-start) | copy-done | bytes 1179672
  21.1 0.0 copy-start.4
  21.1 0.7 copy-done.4
  21.8 0.3 fetch_rows.1
  22.1 0.4 collective-permute-done.refs_4_
  22.6 0.0 copy-done.3
  22.6 0.0 copy-start.1
  22.6 1.1 %sum_shares.3 = (f32[576,128]{1,0:T(8,128)S(1)}, s16[16,128]{1,0:T(8,128)(2,1)S(1)}, s16[592,128]{1,0:T(8,128)(2,1)S(1)}, s16[592,128]{1,0:T(8,128)(2,1)S(1)}, s16[592,128]{1,0:T(8,128)(2,1)S(1)}) custom-call(s32[1]{0:T(128)} %bitcast.me_ref.refs_0_, s32[2,36]{1,0:T(2,128)S(1)} %copy-done.3, f32[2304,128]{1,0:T(8,128)S(1)} %get-tuple-element.23.refs_2_, ...), custom_call_target="tpu_custom_call" | custom-call | flops 2949120 | bytes 2359296 | tf_op jit(solution)/shard_map/sum_shares/pallas_call | solution.py:464
  23.6 3.0 %collective-permute-start.1 = (s16[592,128]{1,0:T(8,128)(2,1)S(1)}, s16[592,128]{1,0:T(8,128)(2,1)S(1)}, u32[]{:S(2)}, u32[]{:S(2)}) collective-permute-start(s16[592,128]{1,0:T(8,128)(2,1)S(1)} %get-tuple-element.28), channel_id=1, source_target_pairs={{0,2},{1,3},{2,0},{3,1},{4,6},{5,7},{6,4},{7,5},{8,10},{9,11},{10,... | collective-permute-start | bytes 454664 | tf_op jit(solution)/shard_map/ppermute | solution.py:715
  26.6 1.6 %collective-permute-start.2 = (s16[592,128]{1,0:T(8,128)(2,1)S(1)}, s16[592,128]{1,0:T(8,128)(2,1)S(1)}, u32[]{:S(2)}, u32[]{:S(2)}) collective-permute-start(s16[592,128]{1,0:T(8,128)(2,1)S(1)} %get-tuple-element.29), channel_id=1, source_target_pairs={{0,4},{1,5},{2,6},{3,7},{4,0},{5,1},{6,2},{7,3},{8,12},{9,13},{10,... | collective-permute-start | bytes 454664 | tf_op jit(solution)/shard_map/ppermute | solution.py:715
  28.2 0.0 collective-permute-start.3
  28.2 2.7 %collective-permute-done.1.refs_4_ = s16[592,128]{1,0:T(8,128)(2,1)S(1)} collective-permute-done((s16[592,128]{1,0:T(8,128)(2,1)S(1)}, s16[592,128]{1,0:T(8,128)(2,1)S(1)}, u32[]{:S(2)}, u32[]{:S(2)}) %collective-permute-start.1) | collective-permute-done | bytes 151584 | tf_op jit(solution)/shard_map/ppermute | solution.py:715
  30.8 2.6 %collective-permute-done.2.refs_5_ = s16[592,128]{1,0:T(8,128)(2,1)S(1)} collective-permute-done((s16[592,128]{1,0:T(8,128)(2,1)S(1)}, s16[592,128]{1,0:T(8,128)(2,1)S(1)}, u32[]{:S(2)}, u32[]{:S(2)}) %collective-permute-start.2) | collective-permute-done | bytes 151584 | tf_op jit(solution)/shard_map/ppermute | solution.py:715
  33.4 1.9 %collective-permute-done.3.refs_6_ = s16[592,128]{1,0:T(8,128)(2,1)S(1)} collective-permute-done((s16[592,128]{1,0:T(8,128)(2,1)S(1)}, s16[592,128]{1,0:T(8,128)(2,1)S(1)}, u32[]{:S(2)}, u32[]{:S(2)}) %collective-permute-start.3) | collective-permute-done | bytes 151584 | tf_op jit(solution)/shard_map/ppermute | solution.py:715
  35.3 0.0 copy-done.1
  35.3 0.0 copy-start.2
  35.3 0.0 copy-start.5
  35.3 1.8 %sum_shares.4 = (s16[624,128]{1,0:T(8,128)(2,1)S(1)}, s16[16,128]{1,0:T(8,128)(2,1)}) custom-call(s32[1]{0:T(128)} %bitcast.me_ref.refs_0_, s32[2,36]{1,0:T(2,128)S(1)} %copy-done.3, f32[576,128]{1,0:T(8,128)S(1)} %get-tuple-element.26.refs_2_, s16[16,128]{1,0:T(8,128)(2,1)S(1)} %get-tuple-element.27.refs_3_, ...), custom_call_target="tpu_custom_call" | custom-call | flops 737280 | bytes 589824 | tf_op jit(solution)/shard_map/sum_shares/pallas_call | solution.py:464
  37.2 2.7 %collective-permute-start.4 = (s16[624,128]{1,0:T(8,128)(2,1)S(1)}, s16[624,128]{1,0:T(8,128)(2,1)S(1)}, u32[]{:S(2)}, u32[]{:S(2)}) collective-permute-start(s16[624,128]{1,0:T(8,128)(2,1)S(1)} %get-tuple-element.32.refs_2_), channel_id=1, source_target_pairs={{0,8},{1,9},{2,10},{3,11},{4,12},{5,13},{6,14},{7,15},{8,0},{9,1},... | collective-permute-start | bytes 479240 | tf_op jit(solution)/shard_map/ppermute | solution.py:715
  39.9 6.9 %collective-permute-done.4.refs_3_ = s16[624,128]{1,0:T(8,128)(2,1)S(1)} collective-permute-done((s16[624,128]{1,0:T(8,128)(2,1)S(1)}, s16[624,128]{1,0:T(8,128)(2,1)S(1)}, u32[]{:S(2)}, u32[]{:S(2)}) %collective-permute-start.4) | collective-permute-done | bytes 159776 | tf_op jit(solution)/shard_map/ppermute | solution.py:715
  46.8 1.1 %sum_shares.5 = (s16[640,128]{1,0:T(8,128)(2,1)S(1)}, s16[16,128]{1,0:T(8,128)(2,1)S(1)}) custom-call(s32[1]{0:T(128)} %bitcast.me_ref.refs_0_, s32[2,36]{1,0:T(2,128)S(1)} %copy-done.3, s16[624,128]{1,0:T(8,128)(2,1)S(1)} %get-tuple-element.32.refs_2_, s16[624,128]{1,0:T(8,128)(2,1)S(1)} %collective-permute-done.4.refs_3_, s16[32,128]{1,0:T(8,128)(2,1)S(1)} %copy-done.1), custom_call_target="tpu_custom_call" | custom-call | flops 737280 | bytes 589824 | tf_op jit(solution)/shard_map/sum_shares/pallas_call | solution.py:464
  47.9 1.4 %collective-permute-start.5 = (s16[640,128]{1,0:T(8,128)(2,1)S(1)}, s16[640,128]{1,0:T(8,128)(2,1)S(1)}, u32[]{:S(2)}, u32[]{:S(2)}) collective-permute-start(s16[640,128]{1,0:T(8,128)(2,1)S(1)} %get-tuple-element.33), channel_id=1, source_target_pairs={{0,2},{1,3},{2,0},{3,1},{4,6},{5,7},{6,4},{7,5},{8,10},{9,11},{10,... | collective-permute-start | bytes 491528 | tf_op jit(solution)/shard_map/ppermute | solution.py:715
  49.3 0.7 collective-permute-start.7
  50.1 1.4 %collective-permute-start.6 = (s16[640,128]{1,0:T(8,128)(2,1)S(1)}, s16[640,128]{1,0:T(8,128)(2,1)S(1)}, u32[]{:S(2)}, u32[]{:S(2)}) collective-permute-start(s16[640,128]{1,0:T(8,128)(2,1)S(1)} %get-tuple-element.33), channel_id=1, source_target_pairs={{0,4},{1,5},{2,6},{3,7},{4,0},{5,1},{6,2},{7,3},{8,12},{9,13},{10,... | collective-permute-start | bytes 491528 | tf_op jit(solution)/shard_map/ppermute | solution.py:715
  51.5 4.6 %collective-permute-done.5 = s16[640,128]{1,0:T(8,128)(2,1)S(1)} collective-permute-done((s16[640,128]{1,0:T(8,128)(2,1)S(1)}, s16[640,128]{1,0:T(8,128)(2,1)S(1)}, u32[]{:S(2)}, u32[]{:S(2)}) %collective-permute-start.5) | collective-permute-done | bytes 163872 | tf_op jit(solution)/shard_map/ppermute | solution.py:715
  56.1 1.8 %collective-permute-done.6 = s16[640,128]{1,0:T(8,128)(2,1)S(1)} collective-permute-done((s16[640,128]{1,0:T(8,128)(2,1)S(1)}, s16[640,128]{1,0:T(8,128)(2,1)S(1)}, u32[]{:S(2)}, u32[]{:S(2)}) %collective-permute-start.6) | collective-permute-done | bytes 163872 | tf_op jit(solution)/shard_map/ppermute | solution.py:715
  58.0 0.0 collective-permute-done.7
  58.0 0.1 collective-permute-start.8
  58.1 2.1 %collective-permute-done.8.second_ref = s16[2560,128]{1,0:T(8,128)(2,1)S(1)} collective-permute-done((s16[2560,128]{1,0:T(8,128)(2,1)S(1)}, s16[2560,128]{1,0:T(8,128)(2,1)S(1)}, u32[]{:S(2)}, u32[]{:S(2)}) %collective-permute-start.8) | collective-permute-done | bytes 655392 | tf_op jit(solution)/shard_map/ppermute | solution.py:715
  60.2 0.0 copy-done.2
  60.2 0.0 copy-done.5
  60.2 21.3 %solve_and_score.1 = (f32[64,4096]{1,0:T(8,128)}, f32[8,64]{1,0:T(8,128)}) custom-call(s32[1]{0:T(128)} %bitcast.me_ref.refs_0_, s16[2560,128]{1,0:T(8,128)(2,1)S(1)} %constant_dynamic-update-slice_fusion.first_ref, s16[2560,128]{1,0:T(8,128)(2,1)S(1)} %collective-permute-done.8.second_ref, s16[16,128]{1,0:T(8,128)(2,1)S(1)} %get-tuple-element.34.state_ref, ...), custom_call_target="tpu_custom_call" | custom-call | flops 10000000000 | bytes 20000000 | tf_op jit(solution)/shard_map/solve_and_score/pallas_call | solution.py:684
  (4 shorter events, 0.1 us)
Async XLA Ops:
  19.3 3.2 %copy-start.3 = (s32[2,36]{1,0:T(2,128)S(1)}, s32[2,36]{1,0:T(2,128)}, u32[]{:S(2)}) copy-start(s32[2,36]{1,0:T(2,128)} %constant.6.clone.refs_1_) | copy-start | bytes 868
  19.4 3.2 %collective-permute-start = (f32[2312,128]{1,0:T(8,128)}, f32[2312,128]{1,0:T(8,128)S(1)}, u32[]{:S(2)}, u32[]{:S(2)}) collective-permute-start(f32[2312,128]{1,0:T(8,128)} %get-tuple-element.25), channel_id=1, source_target_pairs={{0,1},{1,0},{2,3},{3,2},{4,5},{5,4},{6,7},{7,6},{8,9},{9,8},{10,11... | collective-permute-start | bytes 3551240 | tf_op jit(solution)/shard_map/ppermute | solution.py:715
  19.9 1.3 %copy-start = (f32[2304,128]{1,0:T(8,128)S(1)}, f32[2304,128]{1,0:T(8,128)}, u32[]{:S(2)}) copy-start(f32[2304,128]{1,0:T(8,128)} %get-tuple-element.21.first_hbm) | copy-start | bytes 3538948
  21.1 0.7 copy-start.4
  22.6 12.8 %copy-start.1 = (s16[32,128]{1,0:T(8,128)(2,1)S(1)}, s16[32,128]{1,0:T(8,128)(2,1)}, u32[]{:S(2)}) copy-start(s16[32,128]{1,0:T(8,128)(2,1)} %get-tuple-element.31.refs_7_.refs_4_) | copy-start | bytes 24580
  23.6 7.2 %collective-permute-start.1 = (s16[592,128]{1,0:T(8,128)(2,1)S(1)}, s16[592,128]{1,0:T(8,128)(2,1)S(1)}, u32[]{:S(2)}, u32[]{:S(2)}) collective-permute-start(s16[592,128]{1,0:T(8,128)(2,1)S(1)} %get-tuple-element.28), channel_id=1, source_target_pairs={{0,2},{1,3},{2,0},{3,1},{4,6},{5,7},{6,4},{7,5},{8,10},{9,11},{10,... | collective-permute-start | bytes 454664 | tf_op jit(solution)/shard_map/ppermute | solution.py:715
  26.6 6.8 %collective-permute-start.2 = (s16[592,128]{1,0:T(8,128)(2,1)S(1)}, s16[592,128]{1,0:T(8,128)(2,1)S(1)}, u32[]{:S(2)}, u32[]{:S(2)}) collective-permute-start(s16[592,128]{1,0:T(8,128)(2,1)S(1)} %get-tuple-element.29), channel_id=1, source_target_pairs={{0,4},{1,5},{2,6},{3,7},{4,0},{5,1},{6,2},{7,3},{8,12},{9,13},{10,... | collective-permute-start | bytes 454664 | tf_op jit(solution)/shard_map/ppermute | solution.py:715
  28.2 7.2 %collective-permute-start.3 = (s16[592,128]{1,0:T(8,128)(2,1)S(1)}, s16[592,128]{1,0:T(8,128)(2,1)S(1)}, u32[]{:S(2)}, u32[]{:S(2)}) collective-permute-start(s16[592,128]{1,0:T(8,128)(2,1)S(1)} %get-tuple-element.30), channel_id=1, source_target_pairs={{0,6},{1,7},{2,4},{3,5},{4,2},{5,3},{6,0},{7,1},{8,14},{9,15},{10,... | collective-permute-start | bytes 454664 | tf_op jit(solution)/shard_map/ppermute | solution.py:715
  35.3 24.9 %copy-start.2 = (s32[4096]{0:T(1024)S(1)}, s32[4096]{0:T(1024)}, u32[]{:S(2)}) copy-start(s32[4096]{0:T(1024)} %param.15) | copy-start | bytes 49156
  35.3 24.9 %copy-start.5 = (f32[8,1024]{1,0:T(8,128)S(1)}, f32[8,1024]{1,0:T(8,128)}, u32[]{:S(2)}) copy-start(f32[8,1024]{1,0:T(8,128)} %get-tuple-element.17.new_rows_ref) | copy-start | bytes 98308
  37.2 9.6 %collective-permute-start.4 = (s16[624,128]{1,0:T(8,128)(2,1)S(1)}, s16[624,128]{1,0:T(8,128)(2,1)S(1)}, u32[]{:S(2)}, u32[]{:S(2)}) collective-permute-start(s16[624,128]{1,0:T(8,128)(2,1)S(1)} %get-tuple-element.32.refs_2_), channel_id=1, source_target_pairs={{0,8},{1,9},{2,10},{3,11},{4,12},{5,13},{6,14},{7,15},{8,0},{9,1},... | collective-permute-start | bytes 479240 | tf_op jit(solution)/shard_map/ppermute | solution.py:715
  47.9 8.2 %collective-permute-start.5 = (s16[640,128]{1,0:T(8,128)(2,1)S(1)}, s16[640,128]{1,0:T(8,128)(2,1)S(1)}, u32[]{:S(2)}, u32[]{:S(2)}) collective-permute-start(s16[640,128]{1,0:T(8,128)(2,1)S(1)} %get-tuple-element.33), channel_id=1, source_target_pairs={{0,2},{1,3},{2,0},{3,1},{4,6},{5,7},{6,4},{7,5},{8,10},{9,11},{10,... | collective-permute-start | bytes 491528 | tf_op jit(solution)/shard_map/ppermute | solution.py:715
  49.3 8.6 %collective-permute-start.7 = (s16[640,128]{1,0:T(8,128)(2,1)S(1)}, s16[640,128]{1,0:T(8,128)(2,1)S(1)}, u32[]{:S(2)}, u32[]{:S(2)}) collective-permute-start(s16[640,128]{1,0:T(8,128)(2,1)S(1)} %get-tuple-element.33), channel_id=1, source_target_pairs={{0,6},{1,7},{2,4},{3,5},{4,2},{5,3},{6,0},{7,1},{8,14},{9,15},{10,... | collective-permute-start | bytes 491528 | tf_op jit(solution)/shard_map/ppermute | solution.py:715
  50.1 7.9 %collective-permute-start.6 = (s16[640,128]{1,0:T(8,128)(2,1)S(1)}, s16[640,128]{1,0:T(8,128)(2,1)S(1)}, u32[]{:S(2)}, u32[]{:S(2)}) collective-permute-start(s16[640,128]{1,0:T(8,128)(2,1)S(1)} %get-tuple-element.33), channel_id=1, source_target_pairs={{0,4},{1,5},{2,6},{3,7},{4,0},{5,1},{6,2},{7,3},{8,12},{9,13},{10,... | collective-permute-start | bytes 491528 | tf_op jit(solution)/shard_map/ppermute | solution.py:715
  58.0 2.2 %collective-permute-start.8 = (s16[2560,128]{1,0:T(8,128)(2,1)S(1)}, s16[2560,128]{1,0:T(8,128)(2,1)S(1)}, u32[]{:S(2)}, u32[]{:S(2)}) collective-permute-start(s16[2560,128]{1,0:T(8,128)(2,1)S(1)} %constant_dynamic-update-slice_fusion.first_ref), channel_id=1, source_target_pairs={{0,1},{1,0},{2,3},{3,2},{4,5},{5,4},{6,7},{7,6},{8,9},{9,8},{10,11... | collective-permute-start | bytes 1966088 | tf_op jit(solution)/shard_map/ppermute | solution.py:715

commit v6 on v5

--- a/solution.py
+++ b/solution.py
@@ -141,11 +141,10 @@
     chunk = stored.shape[0]
     cuts = 4
     span = grad.shape[1] // cuts
-    parts = [(basis_out_hbm, basis_out)]
+    parts = [(basis_in_hbm, basis_in), (act_hbm, act), (basis_out_hbm, basis_out)]
     for c in range(cuts):
         at = (slice(None), slice(c * span, (c + 1) * span))
         parts.append((grad_hbm.at[at], grad.at[at]))
-    parts += [(basis_in_hbm, basis_in), (act_hbm, act)]
     copies = [
         pltpu.make_async_copy(source, target, sems.at[i])
         for i, (source, target) in enumerate(parts)
@@ -156,11 +155,12 @@
         return pltpu.make_async_copy(codes_hbm.at[at, :], codes.at[at, :], code_sems.at[c])
 
     chunks = rows // chunk
-    for c in range(chunks // 2):
+    early = 2 * (5 * chunks // 16)
+    for c in range(early):
         code_copy(c).start()
     for copy in copies:
         copy.start()
-    for c in range(chunks // 2, chunks):
+    for c in range(early, chunks):
         code_copy(c).start()
     asked = code_floats(queries_ref[...])
     asked = [asked[:, i * LANES : (i + 1) * LANES] for i in range(width // LANES)]
@@ -189,16 +189,16 @@
         add(stored, False)
         return 0
 
-    lax.fori_loop(0, chunks // 4 - 1, body, 0)
+    lax.fori_loop(0, early // 2 - 1, body, 0)
     copies[0].wait()
+    copies[1].wait()
+    proj_in = mm(act[...], basis_in[...], NT)
+    copies[2].wait()
     proj_out = jnp.zeros((tokens, rank), F32)
     for c in range(cuts):
-        copies[1 + c].wait()
+        copies[3 + c].wait()
         at = (slice(None), slice(c * span, (c + 1) * span))
         proj_out = proj_out + mm(grad[at], basis_out[at], NT)
-    copies[-2].wait()
-    copies[-1].wait()
-    proj_in = mm(act[...], basis_in[...], NT)
     wide = (3 * rank, width)
     k = lax.broadcasted_iota(jnp.int32, wide, 0) & (rank - 1)
     c = lax.broadcasted_iota(jnp.int32, wide, 1)
@@ -222,7 +222,7 @@
     high, mid, low = [part.astype(F32) for part in split3(new_rows)]
     first = jnp.concatenate([high, high, mid, high, low, mid], axis=0).astype(BF16)
     second = jnp.concatenate([high, mid, high, low, high, mid], axis=0).astype(BF16)
-    lax.fori_loop(chunks // 4 - 1, chunks // 2 - 1, body, 0)
+    lax.fori_loop(early // 2 - 1, chunks // 2 - 1, body, 0)
     add(stored_next, False)
     tiles = triangle(width)
     half = len(tiles) // 2
@@ -645,12 +645,11 @@
             solved[:, spans[b]] = value
 
     taken_ref[0] = 0
-    ratio = jnp.float32(0.0)
-    for span in spans:
-        sums = jnp.sum(jnp.abs(system[span, span]), axis=0, keepdims=True)
-        ratio = jnp.maximum(ratio, jnp.max(sums) / damp)
-    pl.when(ratio <= 800.0)(lambda: eliminate(split2, mm3, False))
-    pl.when(jnp.logical_not(ratio <= 800.0))(lambda: eliminate(split3, mm6, True))
+    sums = [jnp.sum(jnp.abs(system[span, span]), axis=0, keepdims=True) for span in spans]
+    worst = jnp.max(functools.reduce(jnp.maximum, sums))
+    mild = worst <= 800.0 * damp
+    pl.when(mild)(lambda: eliminate(split2, mm3, False))
+    pl.when(jnp.logical_not(mild))(lambda: eliminate(split3, mm6, True))
     high, low = split2(solved[...])
     new_scores_ref[...] = mm3(split2(new_rows_ref[...]), (high, low), NT)
     both = jnp.concatenate([high, low], axis=0)

time: 81.8 us -> 81.6 us (level)
  no operation moved by 1% of the time
where the time goes in v6:
time: 81.6 us
  Pallas kernels  44.2 us (54%)
  waiting for transfers between devices  23 us (28%)
  starting transfers between devices  11.4 us (14%)
  local copies, waits for them, and re-layouts  2.05 us (3%)
  between operations  0.9 us (1%)
    ppermute x9, waiting for transfers between devices, swap(): return lax.ppermute(value, 'store', [(i, i ^ mask) for i in range(count)])  23 us
    pallas_call x1, Pallas kernels, solve(): pl.pallas_call(functools.partial(solve_kernel, side, levels, masks, count...  21.8 us
    pallas_call x1, Pallas kernels, gram(): pl.pallas_call(functools.partial(gram_kernel, 0.75 / (count * rows), 0.25...  18.2 us
    ppermute x9, starting transfers between devices, swap(): return lax.ppermute(value, 'store', [(i, i ^ mask) for i in range(count)])  11.4 us
    pallas_call x3, Pallas kernels, combine(): pl.pallas_call(functools.partial(combine_kernel, levels, bit, members, bo...  4 us
    unnamed x15, local copies, waits for them, and re-layouts  2.03 us
  transfers between devices with their start and end apart: 9, of which 8 were waited for; matrix products, arithmetic and copies ran while one was open for 0% of the time, Pallas kernels for 0%

profile of v6, /device:TPU:0, one launch (start us, length us, event | category | flops | bytes accessed | tf_op | source)
XLA Modules:
  0.0 81.6 jit_solution(9439124452830050535)
XLA Ops:
  0.6 18.2 %fisher_share.1 = (f32[8,1024]{1,0:T(8,128)}, f32[2304,128]{1,0:T(8,128)}, f32[2312,128]{1,0:T(8,128)}, f32[8,128]{1,0:T(8,128)}, s16[32,128]{1,0:T(8,128)(2,1)}) custom-call(s32[1]{0:T(128)} %bitcast.me_ref.refs_0_, s32[1,8]{1,0:T(1,128)} %lengths_ref.1, s32[32,128]{1,0:T(8,128)} %bitcast.3, bf16[4,1024]{1,0:T(4,128)(2,1)} %queries_ref.1, ...), custom_call_target="tpu_custom_call" | custom-call | flops 6000000000 | bytes 30000000 | tf_op jit(solution)/shard_map/fisher_share/pallas_call | solution.py:265
  18.8 0.0 copy-start.3
  18.8 0.5 collective-permute-start
  19.3 0.0 copy-start
  19.3 1.3 %copy-done = f32[2304,128]{1,0:T(8,128)S(1)} copy-done((f32[2304,128]{1,0:T(8,128)S(1)}, f32[2304,128]{1,0:T(8,128)}, u32[]{:S(2)}) %copy-start) | copy-done | bytes 1179672
  20.6 0.0 copy-start.4
  20.6 0.7 copy-done.4
  21.3 0.3 fetch_rows.1
  21.6 0.4 collective-permute-done.refs_4_
  22.0 0.0 copy-done.3
  22.0 0.0 copy-start.1
  22.0 1.1 %sum_shares.3 = (f32[576,128]{1,0:T(8,128)S(1)}, s16[16,128]{1,0:T(8,128)(2,1)S(1)}, s16[592,128]{1,0:T(8,128)(2,1)S(1)}, s16[592,128]{1,0:T(8,128)(2,1)S(1)}, s16[592,128]{1,0:T(8,128)(2,1)S(1)}) custom-call(s32[1]{0:T(128)} %bitcast.me_ref.refs_0_, s32[2,36]{1,0:T(2,128)S(1)} %copy-done.3, f32[2304,128]{1,0:T(8,128)S(1)} %get-tuple-element.23.refs_2_, ...), custom_call_target="tpu_custom_call" | custom-call | flops 2949120 | bytes 2359296 | tf_op jit(solution)/shard_map/sum_shares/pallas_call | solution.py:464
  23.1 3.0 %collective-permute-start.1 = (s16[592,128]{1,0:T(8,128)(2,1)S(1)}, s16[592,128]{1,0:T(8,128)(2,1)S(1)}, u32[]{:S(2)}, u32[]{:S(2)}) collective-permute-start(s16[592,128]{1,0:T(8,128)(2,1)S(1)} %get-tuple-element.28), channel_id=1, source_target_pairs={{0,2},{1,3},{2,0},{3,1},{4,6},{5,7},{6,4},{7,5},{8,10},{9,11},{10,... | collective-permute-start | bytes 454664 | tf_op jit(solution)/shard_map/ppermute | solution.py:714
  26.0 1.6 %collective-permute-start.2 = (s16[592,128]{1,0:T(8,128)(2,1)S(1)}, s16[592,128]{1,0:T(8,128)(2,1)S(1)}, u32[]{:S(2)}, u32[]{:S(2)}) collective-permute-start(s16[592,128]{1,0:T(8,128)(2,1)S(1)} %get-tuple-element.29), channel_id=1, source_target_pairs={{0,4},{1,5},{2,6},{3,7},{4,0},{5,1},{6,2},{7,3},{8,12},{9,13},{10,... | collective-permute-start | bytes 454664 | tf_op jit(solution)/shard_map/ppermute | solution.py:714
  27.6 0.0 collective-permute-start.3
  27.6 2.7 %collective-permute-done.1.refs_4_ = s16[592,128]{1,0:T(8,128)(2,1)S(1)} collective-permute-done((s16[592,128]{1,0:T(8,128)(2,1)S(1)}, s16[592,128]{1,0:T(8,128)(2,1)S(1)}, u32[]{:S(2)}, u32[]{:S(2)}) %collective-permute-start.1) | collective-permute-done | bytes 151584 | tf_op jit(solution)/shard_map/ppermute | solution.py:714
  30.3 2.6 %collective-permute-done.2.refs_5_ = s16[592,128]{1,0:T(8,128)(2,1)S(1)} collective-permute-done((s16[592,128]{1,0:T(8,128)(2,1)S(1)}, s16[592,128]{1,0:T(8,128)(2,1)S(1)}, u32[]{:S(2)}, u32[]{:S(2)}) %collective-permute-start.2) | collective-permute-done | bytes 151584 | tf_op jit(solution)/shard_map/ppermute | solution.py:714
  32.9 1.9 %collective-permute-done.3.refs_6_ = s16[592,128]{1,0:T(8,128)(2,1)S(1)} collective-permute-done((s16[592,128]{1,0:T(8,128)(2,1)S(1)}, s16[592,128]{1,0:T(8,128)(2,1)S(1)}, u32[]{:S(2)}, u32[]{:S(2)}) %collective-permute-start.3) | collective-permute-done | bytes 151584 | tf_op jit(solution)/shard_map/ppermute | solution.py:714
  34.8 0.0 copy-done.1
  34.8 0.0 copy-start.2
  34.8 0.0 copy-start.5
  34.8 1.8 %sum_shares.4 = (s16[624,128]{1,0:T(8,128)(2,1)S(1)}, s16[16,128]{1,0:T(8,128)(2,1)}) custom-call(s32[1]{0:T(128)} %bitcast.me_ref.refs_0_, s32[2,36]{1,0:T(2,128)S(1)} %copy-done.3, f32[576,128]{1,0:T(8,128)S(1)} %get-tuple-element.26.refs_2_, s16[16,128]{1,0:T(8,128)(2,1)S(1)} %get-tuple-element.27.refs_3_, ...), custom_call_target="tpu_custom_call" | custom-call | flops 737280 | bytes 589824 | tf_op jit(solution)/shard_map/sum_shares/pallas_call | solution.py:464
  36.6 2.7 %collective-permute-start.4 = (s16[624,128]{1,0:T(8,128)(2,1)S(1)}, s16[624,128]{1,0:T(8,128)(2,1)S(1)}, u32[]{:S(2)}, u32[]{:S(2)}) collective-permute-start(s16[624,128]{1,0:T(8,128)(2,1)S(1)} %get-tuple-element.32.refs_2_), channel_id=1, source_target_pairs={{0,8},{1,9},{2,10},{3,11},{4,12},{5,13},{6,14},{7,15},{8,0},{9,1},... | collective-permute-start | bytes 479240 | tf_op jit(solution)/shard_map/ppermute | solution.py:714
  39.4 6.9 %collective-permute-done.4.refs_3_ = s16[624,128]{1,0:T(8,128)(2,1)S(1)} collective-permute-done((s16[624,128]{1,0:T(8,128)(2,1)S(1)}, s16[624,128]{1,0:T(8,128)(2,1)S(1)}, u32[]{:S(2)}, u32[]{:S(2)}) %collective-permute-start.4) | collective-permute-done | bytes 159776 | tf_op jit(solution)/shard_map/ppermute | solution.py:714
  46.3 1.1 %sum_shares.5 = (s16[640,128]{1,0:T(8,128)(2,1)S(1)}, s16[16,128]{1,0:T(8,128)(2,1)S(1)}) custom-call(s32[1]{0:T(128)} %bitcast.me_ref.refs_0_, s32[2,36]{1,0:T(2,128)S(1)} %copy-done.3, s16[624,128]{1,0:T(8,128)(2,1)S(1)} %get-tuple-element.32.refs_2_, s16[624,128]{1,0:T(8,128)(2,1)S(1)} %collective-permute-done.4.refs_3_, s16[32,128]{1,0:T(8,128)(2,1)S(1)} %copy-done.1), custom_call_target="tpu_custom_call" | custom-call | flops 737280 | bytes 589824 | tf_op jit(solution)/shard_map/sum_shares/pallas_call | solution.py:464
  47.4 1.4 %collective-permute-start.5 = (s16[640,128]{1,0:T(8,128)(2,1)S(1)}, s16[640,128]{1,0:T(8,128)(2,1)S(1)}, u32[]{:S(2)}, u32[]{:S(2)}) collective-permute-start(s16[640,128]{1,0:T(8,128)(2,1)S(1)} %get-tuple-element.33), channel_id=1, source_target_pairs={{0,2},{1,3},{2,0},{3,1},{4,6},{5,7},{6,4},{7,5},{8,10},{9,11},{10,... | collective-permute-start | bytes 491528 | tf_op jit(solution)/shard_map/ppermute | solution.py:714
  48.8 0.7 collective-permute-start.7
  49.5 1.4 %collective-permute-start.6 = (s16[640,128]{1,0:T(8,128)(2,1)S(1)}, s16[640,128]{1,0:T(8,128)(2,1)S(1)}, u32[]{:S(2)}, u32[]{:S(2)}) collective-permute-start(s16[640,128]{1,0:T(8,128)(2,1)S(1)} %get-tuple-element.33), channel_id=1, source_target_pairs={{0,4},{1,5},{2,6},{3,7},{4,0},{5,1},{6,2},{7,3},{8,12},{9,13},{10,... | collective-permute-start | bytes 491528 | tf_op jit(solution)/shard_map/ppermute | solution.py:714
  51.0 4.6 %collective-permute-done.5 = s16[640,128]{1,0:T(8,128)(2,1)S(1)} collective-permute-done((s16[640,128]{1,0:T(8,128)(2,1)S(1)}, s16[640,128]{1,0:T(8,128)(2,1)S(1)}, u32[]{:S(2)}, u32[]{:S(2)}) %collective-permute-start.5) | collective-permute-done | bytes 163872 | tf_op jit(solution)/shard_map/ppermute | solution.py:714
  55.6 1.8 %collective-permute-done.6 = s16[640,128]{1,0:T(8,128)(2,1)S(1)} collective-permute-done((s16[640,128]{1,0:T(8,128)(2,1)S(1)}, s16[640,128]{1,0:T(8,128)(2,1)S(1)}, u32[]{:S(2)}, u32[]{:S(2)}) %collective-permute-start.6) | collective-permute-done | bytes 163872 | tf_op jit(solution)/shard_map/ppermute | solution.py:714
  57.4 0.0 collective-permute-done.7
  57.5 0.1 collective-permute-start.8
  57.6 2.1 %collective-permute-done.8.second_ref = s16[2560,128]{1,0:T(8,128)(2,1)S(1)} collective-permute-done((s16[2560,128]{1,0:T(8,128)(2,1)S(1)}, s16[2560,128]{1,0:T(8,128)(2,1)S(1)}, u32[]{:S(2)}, u32[]{:S(2)}) %collective-permute-start.8) | collective-permute-done | bytes 655392 | tf_op jit(solution)/shard_map/ppermute | solution.py:714
  59.6 0.0 copy-done.2
  59.7 0.0 copy-done.5
  59.7 21.8 %solve_and_score.1 = (f32[64,4096]{1,0:T(8,128)}, f32[8,64]{1,0:T(8,128)}) custom-call(s32[1]{0:T(128)} %bitcast.me_ref.refs_0_, s16[2560,128]{1,0:T(8,128)(2,1)S(1)} %constant_dynamic-update-slice_fusion.first_ref, s16[2560,128]{1,0:T(8,128)(2,1)S(1)} %collective-permute-done.8.second_ref, s16[16,128]{1,0:T(8,128)(2,1)S(1)} %get-tuple-element.34.state_ref, ...), custom_call_target="tpu_custom_call" | custom-call | flops 10000000000 | bytes 20000000 | tf_op jit(solution)/shard_map/solve_and_score/pallas_call | solution.py:683
  (4 shorter events, 0.1 us)
Async XLA Ops:
  18.8 3.2 %copy-start.3 = (s32[2,36]{1,0:T(2,128)S(1)}, s32[2,36]{1,0:T(2,128)}, u32[]{:S(2)}) copy-start(s32[2,36]{1,0:T(2,128)} %constant.6.clone.refs_1_) | copy-start | bytes 868
  18.8 3.2 %collective-permute-start = (f32[2312,128]{1,0:T(8,128)}, f32[2312,128]{1,0:T(8,128)S(1)}, u32[]{:S(2)}, u32[]{:S(2)}) collective-permute-start(f32[2312,128]{1,0:T(8,128)} %get-tuple-element.25), channel_id=1, source_target_pairs={{0,1},{1,0},{2,3},{3,2},{4,5},{5,4},{6,7},{7,6},{8,9},{9,8},{10,11... | collective-permute-start | bytes 3551240 | tf_op jit(solution)/shard_map/ppermute | solution.py:714
  19.3 1.3 %copy-start = (f32[2304,128]{1,0:T(8,128)S(1)}, f32[2304,128]{1,0:T(8,128)}, u32[]{:S(2)}) copy-start(f32[2304,128]{1,0:T(8,128)} %get-tuple-element.21.first_hbm) | copy-start | bytes 3538948
  20.6 0.7 copy-start.4
  22.0 12.8 %copy-start.1 = (s16[32,128]{1,0:T(8,128)(2,1)S(1)}, s16[32,128]{1,0:T(8,128)(2,1)}, u32[]{:S(2)}) copy-start(s16[32,128]{1,0:T(8,128)(2,1)} %get-tuple-element.31.refs_7_.refs_4_) | copy-start | bytes 24580
  23.1 7.2 %collective-permute-start.1 = (s16[592,128]{1,0:T(8,128)(2,1)S(1)}, s16[592,128]{1,0:T(8,128)(2,1)S(1)}, u32[]{:S(2)}, u32[]{:S(2)}) collective-permute-start(s16[592,128]{1,0:T(8,128)(2,1)S(1)} %get-tuple-element.28), channel_id=1, source_target_pairs={{0,2},{1,3},{2,0},{3,1},{4,6},{5,7},{6,4},{7,5},{8,10},{9,11},{10,... | collective-permute-start | bytes 454664 | tf_op jit(solution)/shard_map/ppermute | solution.py:714
  26.0 6.8 %collective-permute-start.2 = (s16[592,128]{1,0:T(8,128)(2,1)S(1)}, s16[592,128]{1,0:T(8,128)(2,1)S(1)}, u32[]{:S(2)}, u32[]{:S(2)}) collective-permute-start(s16[592,128]{1,0:T(8,128)(2,1)S(1)} %get-tuple-element.29), channel_id=1, source_target_pairs={{0,4},{1,5},{2,6},{3,7},{4,0},{5,1},{6,2},{7,3},{8,12},{9,13},{10,... | collective-permute-start | bytes 454664 | tf_op jit(solution)/shard_map/ppermute | solution.py:714
  27.6 7.2 %collective-permute-start.3 = (s16[592,128]{1,0:T(8,128)(2,1)S(1)}, s16[592,128]{1,0:T(8,128)(2,1)S(1)}, u32[]{:S(2)}, u32[]{:S(2)}) collective-permute-start(s16[592,128]{1,0:T(8,128)(2,1)S(1)} %get-tuple-element.30), channel_id=1, source_target_pairs={{0,6},{1,7},{2,4},{3,5},{4,2},{5,3},{6,0},{7,1},{8,14},{9,15},{10,... | collective-permute-start | bytes 454664 | tf_op jit(solution)/shard_map/ppermute | solution.py:714
  34.8 24.9 %copy-start.2 = (s32[4096]{0:T(1024)S(1)}, s32[4096]{0:T(1024)}, u32[]{:S(2)}) copy-start(s32[4096]{0:T(1024)} %param.15) | copy-start | bytes 49156
  34.8 24.9 %copy-start.5 = (f32[8,1024]{1,0:T(8,128)S(1)}, f32[8,1024]{1,0:T(8,128)}, u32[]{:S(2)}) copy-start(f32[8,1024]{1,0:T(8,128)} %get-tuple-element.17.new_rows_ref) | copy-start | bytes 98308
  36.6 9.6 %collective-permute-start.4 = (s16[624,128]{1,0:T(8,128)(2,1)S(1)}, s16[624,128]{1,0:T(8,128)(2,1)S(1)}, u32[]{:S(2)}, u32[]{:S(2)}) collective-permute-start(s16[624,128]{1,0:T(8,128)(2,1)S(1)} %get-tuple-element.32.refs_2_), channel_id=1, source_target_pairs={{0,8},{1,9},{2,10},{3,11},{4,12},{5,13},{6,14},{7,15},{8,0},{9,1},... | collective-permute-start | bytes 479240 | tf_op jit(solution)/shard_map/ppermute | solution.py:714
  47.4 8.2 %collective-permute-start.5 = (s16[640,128]{1,0:T(8,128)(2,1)S(1)}, s16[640,128]{1,0:T(8,128)(2,1)S(1)}, u32[]{:S(2)}, u32[]{:S(2)}) collective-permute-start(s16[640,128]{1,0:T(8,128)(2,1)S(1)} %get-tuple-element.33), channel_id=1, source_target_pairs={{0,2},{1,3},{2,0},{3,1},{4,6},{5,7},{6,4},{7,5},{8,10},{9,11},{10,... | collective-permute-start | bytes 491528 | tf_op jit(solution)/shard_map/ppermute | solution.py:714
  48.8 8.6 %collective-permute-start.7 = (s16[640,128]{1,0:T(8,128)(2,1)S(1)}, s16[640,128]{1,0:T(8,128)(2,1)S(1)}, u32[]{:S(2)}, u32[]{:S(2)}) collective-permute-start(s16[640,128]{1,0:T(8,128)(2,1)S(1)} %get-tuple-element.33), channel_id=1, source_target_pairs={{0,6},{1,7},{2,4},{3,5},{4,2},{5,3},{6,0},{7,1},{8,14},{9,15},{10,... | collective-permute-start | bytes 491528 | tf_op jit(solution)/shard_map/ppermute | solution.py:714
  49.5 7.9 %collective-permute-start.6 = (s16[640,128]{1,0:T(8,128)(2,1)S(1)}, s16[640,128]{1,0:T(8,128)(2,1)S(1)}, u32[]{:S(2)}, u32[]{:S(2)}) collective-permute-start(s16[640,128]{1,0:T(8,128)(2,1)S(1)} %get-tuple-element.33), channel_id=1, source_target_pairs={{0,4},{1,5},{2,6},{3,7},{4,0},{5,1},{6,2},{7,3},{8,12},{9,13},{10,... | collective-permute-start | bytes 491528 | tf_op jit(solution)/shard_map/ppermute | solution.py:714
  57.5 2.2 %collective-permute-start.8 = (s16[2560,128]{1,0:T(8,128)(2,1)S(1)}, s16[2560,128]{1,0:T(8,128)(2,1)S(1)}, u32[]{:S(2)}, u32[]{:S(2)}) collective-permute-start(s16[2560,128]{1,0:T(8,128)(2,1)S(1)} %constant_dynamic-update-slice_fusion.first_ref), channel_id=1, source_target_pairs={{0,1},{1,0},{2,3},{3,2},{4,5},{5,4},{6,7},{7,6},{8,9},{9,8},{10,11... | collective-permute-start | bytes 1966088 | tf_op jit(solution)/shard_map/ppermute | solution.py:714
